TPU v7x, 256 devices: a whole 4x4x8 slice. The times are simulated.
256 devices in a mesh: grp: 8 (over z), tile: 32 (over y, x, core).
Axes of the slice: x: 4, y: 4, z: 8, core: 2. Of those that a mesh axis runs over, the one named last changes fastest.
Arguments:
- amplitudes: bfloat16 [2, 2048, 16384], P(None, ('grp', 'tile')), may hold values from -6 to 6
- integrals: bfloat16 [128, 128, 128, 128], P('tile', 'grp'), may hold values from -0.046875 to 0.046875
- tile_in: int32 [128, 128], P('tile'), may hold values from 0 to 127, each once within a row
- tile_list: int32 [2, 128, 128], P(None, 'tile'), may hold values from 0 to 127, as said below
- tile_count: int32 [2, 128], P(None, 'tile'), may hold values from 1 to 128, as said below
Outputs:
- ladder: bfloat16 [2, 2048, 16384], P(None, 'grp', 'tile')
Inputs may be any that keep to these rules, and one draw needn't show every extreme that they name: Each row of tile_in names every input pair block once, so distinct tiles of one output block couple distinct input blocks. Entries of one row of tile_list are distinct; entries at j >= tile_count are ignored. `tile_count`: in each slab some block has exactly 128 live tiles.
All inputs are finite; a program needn't handle non-finite values.
Results may differ from a plain program's by a relative error of at most 0.001.
Values may be sent and summed in bfloat16 or wider, within the bound.
No kernel may reach another device: no remote copies, remote signals or barrier semaphores. Data moves between devices by JAX's collectives and lax.ppermute only.
A program may use at most 192 MiB of HBM per device.

v0:
```python
import jax
import jax.numpy as jnp
from jax import lax
from jax.sharding import PartitionSpec as P


def on_device(amplitudes, integrals, tile_in, tile_list, tile_count):
    gathered = lax.all_gather(integrals, "grp", axis=1, tiled=True)
    local_blocks = gathered.shape[0]
    pool_size = gathered.shape[1]
    tile_width = gathered.shape[-1]
    capacity = tile_list.shape[-1]
    blocks_all = amplitudes.shape[-1] // tile_width
    flat_pool = gathered.reshape(local_blocks, pool_size, tile_width * tile_width)
    pool_ids = jnp.arange(pool_size, dtype=jnp.int32)
    block_ids = jnp.arange(blocks_all, dtype=jnp.int32)
    slot_ids = jnp.arange(capacity, dtype=jnp.int32)

    def dense_tiles(slab_number):
        listed = tile_list[slab_number][:, :, None] == pool_ids[None, None, :]
        within = slot_ids[None, :, None] < tile_count[slab_number][:, None, None]
        selected = jnp.any(listed & within, axis=1).astype(jnp.float32)
        placing = (tile_in[:, :, None] == block_ids[None, None, :]).astype(jnp.float32)
        selector = (placing * selected[:, :, None]).astype(jnp.bfloat16)
        dense = jnp.einsum("lkm,lkx->lmx", selector, flat_pool, preferred_element_type=jnp.float32)
        return dense.astype(jnp.bfloat16).reshape(local_blocks, blocks_all * tile_width, tile_width)

    dense_all = [dense_tiles(slab_number) for slab_number in range(2)]

    def ladder(slab_rows, dense):
        height = slab_rows.shape[0]
        product = jnp.einsum("hx,lxj->hlj", slab_rows, dense, preferred_element_type=jnp.float32)
        return (0.5 * product).astype(jnp.bfloat16).reshape(height, local_blocks * tile_width)

    everyone = lax.all_gather(amplitudes, "tile", axis=1, tiled=True)
    results = [ladder(everyone[slab_number], dense_all[slab_number]) for slab_number in range(2)]
    return jnp.stack(results)


def solution(mesh):
    placed = (
        P(None, ("grp", "tile"), None),
        P("tile", "grp", None, None),
        P("tile", None),
        P(None, "tile", None),
        P(None, "tile"),
    )
    return jax.shard_map(
        on_device, mesh=mesh, in_specs=placed, out_specs=P(None, "grp", "tile"), check_vma=False
    )
```

profile of v0, /device:TPU:1, one launch (start us, length us, event | category | flops | bytes accessed | tf_op | source)
XLA Modules:
  0.0 319.8 jit_solution(10856158543539031370)
XLA Ops:
  6.5 0.0 all-gather.3.cloned.1.call-start
  6.5 0.7 all-gather.3.cloned.1.call-update
  7.3 0.0 all-gather.5.cloned.1.call-start
  7.3 0.7 all-gather.5.cloned.1.call-update
  8.0 0.8 slice_bitcast_fusion.15
  8.8 0.1 iota_compare_fusion.3
  8.8 0.1 iota_compare_fusion.4
  8.9 0.7 slice_bitcast_fusion.13
  9.6 0.4 fusion.7
  10.0 0.0 copy-start
  10.0 175.7 %all-gather.3.cloned.1.call-done = bf16[4,128,128,128]{3,2,1,0:T(8,128)(2,1)} async-done(((bf16[4,16,128,128]{3,2,1,0:T(8,128)(2,1)}), bf16[4,128,128,128]{3,2,1,0:T(8,128)(2,1)}) %all-gather.3.cloned.1.call-update) | async-done | bytes 16777232 | tf_op jit(solution)/shard_map/all_gather | solution.py:8
  185.7 25.5 %reshape.74 = bf16[4,128,16384]{2,1,0:T(8,128)(2,1)} reshape(bf16[4,128,128,128]{3,2,1,0:T(8,128)(2,1)} %all-gather.3.cloned.1.call-done) | data formatting | bytes 33554432 | tf_op jit(solution)/shard_map/reshape | solution.py:14
  211.2 0.0 copy-done
  211.2 11.5 %convolution_convert_fusion.1 = bf16[4,128,16384]{2,1,0:T(8,128)(2,1)} fusion(bf16[4,128,16384]{2,1,0:T(8,128)(2,1)} %reshape.74, bf16[4,128]{1,0:T(4,128)(2,1)S(1)} %convert_element_type.40, s32[4,128]{1,0:T(4,128)S(1)} %copy-done), kind=kOutput, calls=%fused_computation.1 | convolution fusion | flops 2156003328 | bytes 33557504 | tf_op jit(solution)/shard_map/lkm,lkx->lmx/dot_general | solution.py:25
  222.7 26.0 %reshape.75 = bf16[4,16384,128]{2,1,0:T(8,128)(2,1)} reshape(bf16[4,128,16384]{2,1,0:T(8,128)(2,1)} %convolution_convert_fusion.1) | data formatting | bytes 33554432 | tf_op jit(solution)/shard_map/reshape | solution.py:26
  248.7 12.0 %convolution_convert_fusion = bf16[4,128,16384]{2,1,0:T(8,128)(2,1)} fusion(bf16[4,128,16384]{2,1,0:T(8,128)(2,1)} %reshape.74, bf16[4,128]{1,0:T(4,128)(2,1)S(1)} %convert_element_type.45, s32[4,128]{1,0:T(4,128)S(1)} %copy-done), kind=kOutput, calls=%fused_computation | convolution fusion | flops 2156003328 | bytes 33557504 | tf_op jit(solution)/shard_map/lkm,lkx->lmx/dot_general | solution.py:25
  260.7 25.6 %reshape.76 = bf16[4,16384,128]{2,1,0:T(8,128)(2,1)} reshape(bf16[4,128,16384]{2,1,0:T(8,128)(2,1)} %convolution_convert_fusion) | data formatting | bytes 33554432 | tf_op jit(solution)/shard_map/reshape | solution.py:26
  286.4 0.0 all-gather.5.cloned.1.call-done
  286.4 12.7 %fusion.5 = bf16[4,128,256]{2,1,0:T(8,128)(2,1)S(1)} fusion(bf16[4,16384,128]{2,1,0:T(8,128)(2,1)} %reshape.75, bf16[2,256,16384]{2,1,0:T(8,128)(2,1)} %all-gather.5.cloned.1.call-done), kind=kOutput, calls=%fused_computation.9 | convolution fusion | flops 4295229440 | bytes 25427968 | tf_op jit(solution)/shard_map/hx,lxj->hlj/dot_general | solution.py:32
  299.1 0.1 copy.12
  299.2 12.7 %fusion.4 = bf16[4,128,256]{2,1,0:T(8,128)(2,1)S(1)} fusion(bf16[4,16384,128]{2,1,0:T(8,128)(2,1)} %reshape.76, bf16[2,256,16384]{2,1,0:T(8,128)(2,1)} %all-gather.5.cloned.1.call-done), kind=kOutput, calls=%fused_computation.8 | convolution fusion | flops 4295229440 | bytes 25427968 | tf_op jit(solution)/shard_map/hx,lxj->hlj/dot_general | solution.py:32
  311.9 0.1 copy.13
  312.1 0.8 pad_maximum_fusion
  (2 shorter events, 0.0 us)
Async XLA Ops:
  6.5 179.2 %all-gather.3.cloned.1.call-start = ((), (), s32[]{:S(2)}) async-start(), calls=%async_computation | async-start | bytes 18874368 | tf_op jit(solution)/shard_map/all_gather | solution.py:8
  7.3 279.1 %all-gather.5.cloned.1.call-start = ((), (), s32[]{:S(2)}) async-start(), calls=%async_computation.1 | async-start | bytes 17301504 | tf_op jit(solution)/shard_map/all_gather | solution.py:35
  10.0 201.2 %copy-start = (s32[4,128]{1,0:T(4,128)S(1)}, s32[4,128]{1,0:T(4,128)}, u32[]{:S(2)}) copy-start(s32[4,128]{1,0:T(4,128)} %param.7) | copy-start | bytes 6148
Sparse Core Ops, SparseCore 0:
  9.1 176.5 all-gather.2
  188.3 76.5 all-gather.4
where the time goes:
time: 322 us; the launch traced here: 320 us
  waiting for transfers between devices  177 us (55%)
  local copies, waits for them, and re-layouts  78.9 us (25%)
  matrix products  48.9 us (15%)
  between operations  13.5 us (4%)
    all_gather x1, waiting for transfers between devices, on_device(): gathered = lax.all_gather(integrals, 'grp', axis=1, tiled=True)  176 us
    reshape x2, local copies, waits for them, and re-layouts, dense_tiles(): dense.astype(jnp.bfloat16)  51.7 us
    reshape x1, local copies, waits for them, and re-layouts, on_device(): gathered.reshape(local_blocks, pool_size, tile_width * tile_width)  25.5 us
    dot_general x2, matrix products, ladder(): jnp.einsum('hx,lxj->hlj', slab_rows, dense, preferred_element_type=jnp.fl...  25.4 us
    dot_general x2, matrix products, dense_tiles(): jnp.einsum('lkm,lkx->lmx', selector, flat_pool, preferred_element_type=jn...  23.5 us
  transfers between devices with their start and end apart: 2, of which 1 were waited for; matrix products, arithmetic and copies ran while one was open for 32% of the time, Pallas kernels for 0%

commit v1 on v0

v1 whole, which is shorter than its diff:
```python
import functools

import jax
import jax.numpy as jnp
from jax import lax
from jax.experimental import pallas as pl
from jax.experimental.pallas import tpu as pltpu
from jax.sharding import PartitionSpec as P

WIDE = 8


def body(count, final, blocks, pool, ids, tile_in, live, *refs):
    amps = refs[:WIDE]
    tiles = refs[WIDE : WIDE + 2 * count]
    acc, out, total = refs[WIDE + 2 * count :]
    block, step = pl.program_id(0), pl.program_id(1)
    per_shard = 16 // WIDE

    @pl.when(step == 0)
    def _():
        total[...] = acc[...]

    start = ids[step // per_shard] * 16 + (step % per_shard) * WIDE

    def add(tile_ref):
        for slab in range(2):
            left = jnp.concatenate([a[slab] for a in amps], axis=1)
            picked = []
            for j in range(WIDE):
                on = live[(slab * blocks + block) * pool + start + j]
                tile = tile_ref[0, j]
                picked.append(jnp.where(on > 0, tile, jnp.zeros_like(tile)))
            right = jnp.concatenate(picked, axis=0)
            total[slab] += jnp.dot(left, right, preferred_element_type=jnp.float32)

    for shard in range(count):
        for half in range(2):
            here = (step // per_shard == shard) & (block // 2 == half)
            pl.when(here)(functools.partial(add, tiles[2 * shard + half]))

    @pl.when(step == pl.num_programs(1) - 1)
    def _():
        if final:
            out[...] = (0.5 * total[...]).astype(out.dtype)
        else:
            out[...] = total[...]


def accumulate(shards, ids, acc, amps, tile_in, live, final):
    count = len(shards)
    rows = amps.shape[1]
    blocks, pool = tile_in.shape
    per_shard = 16 // WIDE

    def amp_map(j, block, step, ids, tile_in, live):
        k = ids[step // per_shard] * 16 + (step % per_shard) * WIDE + j
        return 0, 0, tile_in[block * pool + k]

    def tile_map(shard, half, block, step, ids, tile_in, live):
        part = jnp.clip(step - shard * per_shard, 0, per_shard - 1)
        if half == 0:
            return jnp.minimum(block, 1), jnp.where(block < 2, part, per_shard - 1), 0, 0
        return jnp.maximum(block - 2, 0), jnp.where(block < 2, 0, part), 0, 0

    def own(block, step, ids, tile_in, live):
        return 0, 0, block

    specs = [pl.BlockSpec((2, rows, 128), functools.partial(amp_map, j)) for j in range(WIDE)]
    flat = []
    for shard, halves in enumerate(shards):
        for half in range(2):
            specs.append(pl.BlockSpec((1, WIDE, 128, 128), functools.partial(tile_map, shard, half)))
            flat.append(halves[half])
    specs.append(pl.BlockSpec((2, rows, 128), own))
    flops = 2 * 2 * rows * 128 * 128 * 16 * blocks * count
    moved = blocks * 16 * count * (2 * rows * 128 * 2 + 128 * 128 * 2)
    return pl.pallas_call(
        functools.partial(body, count, final, blocks, pool),
        out_shape=jax.ShapeDtypeStruct((2, rows, blocks * 128), jnp.bfloat16 if final else jnp.float32),
        grid_spec=pltpu.PrefetchScalarGridSpec(
            num_scalar_prefetch=3,
            grid=(blocks, count * per_shard),
            in_specs=specs,
            out_specs=pl.BlockSpec((2, rows, 128), own),
            scratch_shapes=[pltpu.VMEM((2, rows, 128), jnp.float32)],
        ),
        compiler_params=pltpu.CompilerParams(vmem_limit_bytes=32 * 1024 * 1024),
        cost_estimate=pl.CostEstimate(flops=flops, bytes_accessed=moved, transcendentals=0),
    )(ids, tile_in.reshape(-1), live.reshape(-1), *([amps] * WIDE), *flat, acc)


def on_device(groups, amplitudes, integrals, tile_in, tile_list, tile_count):
    pool = tile_in.shape[1]
    me = lax.axis_index("grp")
    plus = [(i, (i + 1) % groups) for i in range(groups)]
    minus = [(i, (i - 1) % groups) for i in range(groups)]

    amps = lax.all_gather(amplitudes, "tile", axis=1, tiled=True)

    slots = jnp.arange(tile_list.shape[-1], dtype=jnp.int32)
    listed = tile_list[..., None] == jnp.arange(pool, dtype=jnp.int32)
    within = (slots < tile_count[..., None])[..., None]
    live = jnp.any(listed & within, axis=2).astype(jnp.int32)

    low, high = integrals[:2], integrals[2:]
    held = {0: (low, high)}
    up, down = (low, high), (low, high)
    for step in range(1, 4):
        up = tuple(lax.ppermute(x, "grp", plus) for x in up)
        down = tuple(lax.ppermute(x, "grp", minus) for x in down)
        held[-step], held[step] = up, down
    held[4] = (lax.ppermute(up[0], "grp", plus), lax.ppermute(down[1], "grp", minus))

    acc = jnp.zeros((2, amps.shape[1], tile_in.shape[0] * 128), jnp.float32)
    for offsets in ((0, -1, 1), (-2, 2), (-3, 3), (4,)):
        ids = jnp.stack([(me + o) % groups for o in offsets]).astype(jnp.int32)
        acc = accumulate([held[o] for o in offsets], ids, acc, amps, tile_in, live, offsets == (4,))
    return acc


def solution(mesh):
    placed = (
        P(None, ("grp", "tile"), None),
        P("tile", "grp", None, None),
        P("tile", None),
        P(None, "tile", None),
        P(None, "tile"),
    )
    return jax.shard_map(
        functools.partial(on_device, mesh.shape["grp"]),
        mesh=mesh,
        in_specs=placed,
        out_specs=P(None, "grp", "tile"),
        check_vma=False,
    )
```

time: 322 us -> 221 us (0.69)
  waiting for transfers between devices: 177 us -> 95 us
  Pallas kernels: 0 us -> 69.8 us
  local copies, waits for them, and re-layouts: 78.9 us -> 16.4 us
  matrix products: 48.9 us -> 0 us
  starting transfers between devices: 0.04 us -> 22.6 us
    all_gather x2 -> x1, waiting for transfers between devices: 176 us -> 0.01 us  [on_device(): amps = lax.all_gather(amplitudes, 'tile', axis=1, tiled=True)]
    ppermute x0 -> x14, waiting for transfers between devices: none -> 94.3 us  [the longest x6 94.3 us: on_device(): up = tuple((lax.ppermute(x, 'grp', plus) for x in up))]
    reshape x3 -> x0, local copies, waits for them, and re-layouts: 77.1 us -> none  [the longest x2 51.7 us: dense_tiles(): dense.astype(jnp.bfloat16)]
    pallas_call x0 -> x4, Pallas kernels: none -> 69.8 us  [accumulate(): pl.pallas_call(functools.partial(body, count, final, blocks, pool), out_s...]
    dot_general x4 -> x0, matrix products: 48.9 us -> none  [the longest x2 25.4 us: ladder(): jnp.einsum('hx,lxj->hlj', slab_rows, dense, preferred_element_type=jnp.fl...]
    ppermute x0 -> x14, starting transfers between devices: none -> 22.6 us  [the longest x6 17.4 us: on_device(): down = tuple((lax.ppermute(x, 'grp', minus) for x in down))]
    unnamed x2 -> x28, local copies, waits for them, and re-layouts: 0.01 us -> 14.5 us
  transfers between devices with their start and end apart: 2 -> 15, of which waited for: 1 -> 5; matrix products, arithmetic and copies ran while one was open for 32% -> 1% of each run, Pallas kernels for 0% -> 27%
where the time goes in v1:
time: 221 us; the launch traced here: 218 us
  waiting for transfers between devices  95 us (43%)
  Pallas kernels  69.8 us (32%)
  starting transfers between devices  22.6 us (10%)
  local copies, waits for them, and re-layouts  16.4 us (7%)
  between operations  13.7 us (6%)
    ppermute x6, waiting for transfers between devices, on_device(): up = tuple((lax.ppermute(x, 'grp', plus) for x in up))  94.3 us
    pallas_call x4, Pallas kernels, accumulate(): pl.pallas_call(functools.partial(body, count, final, blocks, pool), out_s...  69.8 us
    ppermute x6, starting transfers between devices, on_device(): down = tuple((lax.ppermute(x, 'grp', minus) for x in down))  17.4 us
    unnamed x28, local copies, waits for them, and re-layouts  14.5 us
  transfers between devices with their start and end apart: 15, of which 5 were waited for; matrix products, arithmetic and copies ran while one was open for 1% of the time, Pallas kernels for 27%

profile of v1, /device:TPU:1, one launch (start us, length us, event | category | flops | bytes accessed | tf_op | source)
XLA Modules:
  0.0 218.2 jit_solution(7487426641136936389)
XLA Ops:
  6.5 0.0 all-gather.2.cloned.1.call-start
  6.5 0.7 all-gather.2.cloned.1.call-update
  7.3 0.0 copy-start.13
  7.3 0.0 copy-start.12
  7.3 0.0 copy-start.11
  7.3 1.8 fusion.2
  9.1 2.5 %collective-permute-start = (bf16[2,16,128,128]{3,2,1,0:T(8,128)(2,1)S(1)}, bf16[2,16,128,128]{3,2,1,0:T(8,128)(2,1)S(1)}, u32[]{:S(2)}, u32[]{:S(2)}) collective-permute-start(bf16[2,16,128,128]{3,2,1,0:T(8,128)(2,1)S(1)} %get-tuple-element.6.refs_8_), channel_id=1, source_target_pairs={{0,32},{32,64},{64,96},{96,128},{128,160},{160,192},{192,224},{224... | collective-permute-start | bytes 3145736 | tf_op jit(solution)/shard_map/ppermute | solution.py:110
  11.6 4.0 %collective-permute-start.4 = (bf16[2,16,128,128]{3,2,1,0:T(8,128)(2,1)S(1)}, bf16[2,16,128,128]{3,2,1,0:T(8,128)(2,1)S(1)}, u32[]{:S(2)}, u32[]{:S(2)}) collective-permute-start(bf16[2,16,128,128]{3,2,1,0:T(8,128)(2,1)S(1)} %get-tuple-element.5.refs_9_), channel_id=1, source_target_pairs={{0,224},{32,0},{64,32},{96,64},{128,96},{160,128},{192,160},{224,1... | collective-permute-start | bytes 3145736 | tf_op jit(solution)/shard_map/ppermute | solution.py:111
  15.7 0.0 collective-permute-start.8
  15.7 2.7 %collective-permute-start.11 = (bf16[2,16,128,128]{3,2,1,0:T(8,128)(2,1)S(1)}, bf16[2,16,128,128]{3,2,1,0:T(8,128)(2,1)S(1)}, u32[]{:S(2)}, u32[]{:S(2)}) collective-permute-start(bf16[2,16,128,128]{3,2,1,0:T(8,128)(2,1)S(1)} %get-tuple-element.6.refs_8_), channel_id=1, source_target_pairs={{0,224},{32,0},{64,32},{96,64},{128,96},{160,128},{192,160},{224,1... | collective-permute-start | bytes 3145736 | tf_op jit(solution)/shard_map/ppermute | solution.py:111
  18.3 20.2 %collective-permute-done.refs_10_ = bf16[2,16,128,128]{3,2,1,0:T(8,128)(2,1)S(1)} collective-permute-done((bf16[2,16,128,128]{3,2,1,0:T(8,128)(2,1)S(1)}, bf16[2,16,128,128]{3,2,1,0:T(8,128)(2,1)S(1)}, u32[]{:S(2)}, u32[]{:S(2)}) %collective-permute-start) | collective-permute-done | bytes 1048608 | tf_op jit(solution)/shard_map/ppermute | solution.py:110
  38.6 0.0 collective-permute-start.1
  38.6 0.0 collective-permute-done.4.refs_13_
  38.6 2.7 %collective-permute-start.5 = (bf16[2,16,128,128]{3,2,1,0:T(8,128)(2,1)S(1)}, bf16[2,16,128,128]{3,2,1,0:T(8,128)(2,1)S(1)}, u32[]{:S(2)}, u32[]{:S(2)}) collective-permute-start(bf16[2,16,128,128]{3,2,1,0:T(8,128)(2,1)S(1)} %collective-permute-done.4.refs_13_), channel_id=1, source_target_pairs={{0,224},{32,0},{64,32},{96,64},{128,96},{160,128},{192,160},{224,1... | collective-permute-start | bytes 3145736 | tf_op jit(solution)/shard_map/ppermute | solution.py:111
  41.2 0.0 copy-start.1
  41.2 1.0 copy-done.1
  42.2 18.8 %collective-permute-done.8.refs_11_ = bf16[2,16,128,128]{3,2,1,0:T(8,128)(2,1)S(1)} collective-permute-done((bf16[2,16,128,128]{3,2,1,0:T(8,128)(2,1)S(1)}, bf16[2,16,128,128]{3,2,1,0:T(8,128)(2,1)S(1)}, u32[]{:S(2)}, u32[]{:S(2)}) %collective-permute-start.8) | collective-permute-done | bytes 1048608 | tf_op jit(solution)/shard_map/ppermute | solution.py:110
  61.0 0.0 collective-permute-start.9
  61.0 0.0 copy-start.3
  61.0 1.1 copy-done.3
  62.1 0.0 collective-permute-done.11.refs_12_
  62.1 2.7 %collective-permute-start.12 = (bf16[2,16,128,128]{3,2,1,0:T(8,128)(2,1)S(1)}, bf16[2,16,128,128]{3,2,1,0:T(8,128)(2,1)}, u32[]{:S(2)}, u32[]{:S(2)}) collective-permute-start(bf16[2,16,128,128]{3,2,1,0:T(8,128)(2,1)S(1)} %collective-permute-done.11.refs_12_), channel_id=1, source_target_pairs={{0,224},{32,0},{64,32},{96,64},{128,96},{160,128},{192,160},{224,1... | collective-permute-start | bytes 3145736 | tf_op jit(solution)/shard_map/ppermute | solution.py:111
  64.8 0.0 copy-start.5
  64.8 1.0 copy-done.5
  65.8 17.7 %collective-permute-done.1.refs_8_ = bf16[2,16,128,128]{3,2,1,0:T(8,128)(2,1)S(1)} collective-permute-done((bf16[2,16,128,128]{3,2,1,0:T(8,128)(2,1)S(1)}, bf16[2,16,128,128]{3,2,1,0:T(8,128)(2,1)S(1)}, u32[]{:S(2)}, u32[]{:S(2)}) %collective-permute-start.1) | collective-permute-done | bytes 1048608 | tf_op jit(solution)/shard_map/ppermute | solution.py:110
  83.5 0.0 collective-permute-start.2
  83.5 0.0 copy-start.7
  83.5 1.0 copy-done.7
  84.5 0.0 collective-permute-done.5.refs_11_
  84.5 2.7 %collective-permute-start.6 = (bf16[2,16,128,128]{3,2,1,0:T(8,128)(2,1)S(1)}, bf16[2,16,128,128]{3,2,1,0:T(8,128)(2,1)}, u32[]{:S(2)}, u32[]{:S(2)}) collective-permute-start(bf16[2,16,128,128]{3,2,1,0:T(8,128)(2,1)S(1)} %collective-permute-done.5.refs_11_), channel_id=1, source_target_pairs={{0,224},{32,0},{64,32},{96,64},{128,96},{160,128},{192,160},{224,1... | collective-permute-start | bytes 3145736 | tf_op jit(solution)/shard_map/ppermute | solution.py:111
  87.2 1.0 copy-done.9
  88.2 17.8 %collective-permute-done.9.refs_9_ = bf16[2,16,128,128]{3,2,1,0:T(8,128)(2,1)} collective-permute-done((bf16[2,16,128,128]{3,2,1,0:T(8,128)(2,1)S(1)}, bf16[2,16,128,128]{3,2,1,0:T(8,128)(2,1)}, u32[]{:S(2)}, u32[]{:S(2)}) %collective-permute-start.9) | collective-permute-done | bytes 1048608 | tf_op jit(solution)/shard_map/ppermute | solution.py:110
  106.0 0.0 collective-permute-start.10
  106.0 0.0 collective-permute-done.12.refs_10_
  106.0 2.7 %collective-permute-start.13 = (bf16[2,16,128,128]{3,2,1,0:T(8,128)(2,1)}, bf16[2,16,128,128]{3,2,1,0:T(8,128)(2,1)}, u32[]{:S(2)}, u32[]{:S(2)}) collective-permute-start(bf16[2,16,128,128]{3,2,1,0:T(8,128)(2,1)} %collective-permute-done.12.refs_10_), channel_id=1, source_target_pairs={{0,224},{32,0},{64,32},{96,64},{128,96},{160,128},{192,160},{224,1... | collective-permute-start | bytes 3145736 | tf_op jit(solution)/shard_map/ppermute | solution.py:111
  108.7 0.0 copy-done.13
  108.7 0.1 iota_compare_fusion.1
  108.7 19.7 %collective-permute-done.2.refs_8_ = bf16[2,16,128,128]{3,2,1,0:T(8,128)(2,1)} collective-permute-done((bf16[2,16,128,128]{3,2,1,0:T(8,128)(2,1)S(1)}, bf16[2,16,128,128]{3,2,1,0:T(8,128)(2,1)}, u32[]{:S(2)}, u32[]{:S(2)}) %collective-permute-start.2) | collective-permute-done | bytes 1048608 | tf_op jit(solution)/shard_map/ppermute | solution.py:110
  128.4 0.0 collective-permute-start.3
  128.4 0.0 collective-permute-done.6.refs_11_
  128.5 2.7 %collective-permute-start.7 = (bf16[2,16,128,128]{3,2,1,0:T(8,128)(2,1)}, bf16[2,16,128,128]{3,2,1,0:T(8,128)(2,1)}, u32[]{:S(2)}, u32[]{:S(2)}) collective-permute-start(bf16[2,16,128,128]{3,2,1,0:T(8,128)(2,1)} %collective-permute-done.6.refs_11_), channel_id=1, source_target_pairs={{0,224},{32,0},{64,32},{96,64},{128,96},{160,128},{192,160},{224,1... | collective-permute-start | bytes 3145736 | tf_op jit(solution)/shard_map/ppermute | solution.py:113
  131.1 0.0 copy-done.12
  131.1 0.4 fusion.1
  131.6 0.1 pad_add_fusion.1.ids
  131.7 0.1 pad_add_fusion.ids
  131.8 0.1 pad_add_fusion.2.ids
  131.9 0.1 broadcast_in_dim.2.refs_14_
  132.0 0.0 copy-done.11
  132.0 0.0 copy-start.2
  132.0 1.2 copy-done.2
  133.2 1.2 copy-done.4
  134.5 1.2 copy-done.6
  135.7 24.1 %shard_map.55.refs_12_ = f32[2,256,512]{2,1,0:T(8,128)S(1)} custom-call(s32[3]{0:T(128)S(1)} %pad_add_fusion.2.ids, s32[512]{0:T(512)S(1)} %bitcast.14, s32[1024]{0:T(1024)S(1)} %bitcast.10, bf16[2,256,16384]{2,1,0:T(8,128)(2,1)} %all-gather.2.cloned.1.call-done.refs_0_.refs_1_.refs_2_.refs_3_.refs_4_.refs_5_.refs_6_.refs_7_, ...), custom_call_target="tpu_custom_call" | custom-call | flops 3221225472 | bytes 31457280 | tf_op jit(solution)/shard_map/pallas_call | solution.py:78
  159.8 0.0 copy-done.8
  159.8 0.0 copy-done.10
  159.8 17.4 %shard_map.56.refs_12_ = f32[2,256,512]{2,1,0:T(8,128)S(1)} custom-call(s32[2]{0:T(128)S(1)} %pad_add_fusion.1.ids, s32[512]{0:T(512)S(1)} %bitcast.15, s32[1024]{0:T(1024)S(1)} %bitcast.11, bf16[2,256,16384]{2,1,0:T(8,128)(2,1)} %all-gather.2.cloned.1.call-done.refs_0_.refs_1_.refs_2_.refs_3_.refs_4_.refs_5_.refs_6_.refs_7_, ...), custom_call_target="tpu_custom_call" | custom-call | flops 2147483648 | bytes 20971520 | tf_op jit(solution)/shard_map/pallas_call | solution.py:78
  177.2 0.0 collective-permute-done.10.refs_9_
  177.2 0.0 collective-permute-done.13.refs_10_
  177.3 18.0 %shard_map.57.refs_10_ = f32[2,256,512]{2,1,0:T(8,128)S(1)} custom-call(s32[2]{0:T(128)S(1)} %pad_add_fusion.ids, s32[512]{0:T(512)S(1)} %bitcast.16, s32[1024]{0:T(1024)S(1)} %bitcast.12, bf16[2,256,16384]{2,1,0:T(8,128)(2,1)} %all-gather.2.cloned.1.call-done.refs_0_.refs_1_.refs_2_.refs_3_.refs_4_.refs_5_.refs_6_.refs_7_, ...), custom_call_target="tpu_custom_call" | custom-call | flops 2147483648 | bytes 20971520 | tf_op jit(solution)/shard_map/pallas_call | solution.py:78
  195.2 0.0 collective-permute-done.3.refs_8_
  195.2 0.0 collective-permute-done.7.refs_9_
  195.3 0.0 copy-start
  195.3 5.8 %copy-done = bf16[2,256,16384]{2,1,0:T(8,128)(2,1)S(1)} copy-done((bf16[2,256,16384]{2,1,0:T(8,128)(2,1)S(1)}, bf16[2,256,16384]{2,1,0:T(8,128)(2,1)}, u32[]{:S(2)}) %copy-start) | copy-done | bytes 16777240
  201.0 10.3 %shard_map.58 = bf16[2,256,512]{2,1,0:T(8,128)(2,1)} custom-call(s32[1]{0:T(128)} %bitcast.ids, s32[512]{0:T(512)S(1)} %bitcast.17, s32[1024]{0:T(1024)S(1)} %bitcast.13, bf16[2,256,16384]{2,1,0:T(8,128)(2,1)S(1)} %copy-done, bf16[2,256,16384]{2,1,0:T(8,128)(2,1)S(1)} %copy-done, bf16[2,256,16384]{2,1,0:T(8,128)(2,1)S(1)} %copy-done, ...), custom_call_target="tpu_custom_call" | custom-call | flops 1073741824 | bytes 10485760 | tf_op jit(solution)/shard_map/pallas_call | solution.py:78
  (7 shorter events, 0.0 us)
Async XLA Ops:
  6.5 125.3 %all-gather.2.cloned.1.call-start = ((), (), s32[]{:S(2)}) async-start(), calls=%async_computation | async-start | bytes 17301504 | tf_op jit(solution)/shard_map/all_gather | solution.py:99
  7.3 101.4 %copy-start.13 = (s32[2,4]{1,0:T(2,128)S(1)}, s32[2,4]{1,0:T(2,128)}, u32[]{:S(2)}) copy-start(s32[2,4]{1,0:T(2,128)} %param.9) | copy-start | bytes 100
  7.3 123.9 %copy-start.12 = (s32[2,4,128]{2,1,0:T(4,128)S(1)}, s32[2,4,128]{2,1,0:T(4,128)}, u32[]{:S(2)}) copy-start(s32[2,4,128]{2,1,0:T(4,128)} %param.8) | copy-start | bytes 12292
  7.3 124.7 %copy-start.11 = (s32[4,128]{1,0:T(4,128)S(1)}, s32[4,128]{1,0:T(4,128)}, u32[]{:S(2)}) copy-start(s32[4,128]{1,0:T(4,128)} %param.7) | copy-start | bytes 6148
  9.1 29.5 %collective-permute-start = (bf16[2,16,128,128]{3,2,1,0:T(8,128)(2,1)S(1)}, bf16[2,16,128,128]{3,2,1,0:T(8,128)(2,1)S(1)}, u32[]{:S(2)}, u32[]{:S(2)}) collective-permute-start(bf16[2,16,128,128]{3,2,1,0:T(8,128)(2,1)S(1)} %get-tuple-element.6.refs_8_), channel_id=1, source_target_pairs={{0,32},{32,64},{64,96},{96,128},{128,160},{160,192},{192,224},{224... | collective-permute-start | bytes 3145736 | tf_op jit(solution)/shard_map/ppermute | solution.py:110
  11.6 26.9 %collective-permute-start.4 = (bf16[2,16,128,128]{3,2,1,0:T(8,128)(2,1)S(1)}, bf16[2,16,128,128]{3,2,1,0:T(8,128)(2,1)S(1)}, u32[]{:S(2)}, u32[]{:S(2)}) collective-permute-start(bf16[2,16,128,128]{3,2,1,0:T(8,128)(2,1)S(1)} %get-tuple-element.5.refs_9_), channel_id=1, source_target_pairs={{0,224},{32,0},{64,32},{96,64},{128,96},{160,128},{192,160},{224,1... | collective-permute-start | bytes 3145736 | tf_op jit(solution)/shard_map/ppermute | solution.py:111
  15.7 45.4 %collective-permute-start.8 = (bf16[2,16,128,128]{3,2,1,0:T(8,128)(2,1)S(1)}, bf16[2,16,128,128]{3,2,1,0:T(8,128)(2,1)S(1)}, u32[]{:S(2)}, u32[]{:S(2)}) collective-permute-start(bf16[2,16,128,128]{3,2,1,0:T(8,128)(2,1)S(1)} %get-tuple-element.5.refs_9_), channel_id=1, source_target_pairs={{0,32},{32,64},{64,96},{96,128},{128,160},{160,192},{192,224},{224... | collective-permute-start | bytes 3145736 | tf_op jit(solution)/shard_map/ppermute | solution.py:110
  15.7 46.5 %collective-permute-start.11 = (bf16[2,16,128,128]{3,2,1,0:T(8,128)(2,1)S(1)}, bf16[2,16,128,128]{3,2,1,0:T(8,128)(2,1)S(1)}, u32[]{:S(2)}, u32[]{:S(2)}) collective-permute-start(bf16[2,16,128,128]{3,2,1,0:T(8,128)(2,1)S(1)} %get-tuple-element.6.refs_8_), channel_id=1, source_target_pairs={{0,224},{32,0},{64,32},{96,64},{128,96},{160,128},{192,160},{224,1... | collective-permute-start | bytes 3145736 | tf_op jit(solution)/shard_map/ppermute | solution.py:111
  38.6 44.9 %collective-permute-start.1 = (bf16[2,16,128,128]{3,2,1,0:T(8,128)(2,1)S(1)}, bf16[2,16,128,128]{3,2,1,0:T(8,128)(2,1)S(1)}, u32[]{:S(2)}, u32[]{:S(2)}) collective-permute-start(bf16[2,16,128,128]{3,2,1,0:T(8,128)(2,1)S(1)} %collective-permute-done.refs_10_), channel_id=1, source_target_pairs={{0,32},{32,64},{64,96},{96,128},{128,160},{160,192},{192,224},{224... | collective-permute-start | bytes 3145736 | tf_op jit(solution)/shard_map/ppermute | solution.py:110
  38.6 45.9 %collective-permute-start.5 = (bf16[2,16,128,128]{3,2,1,0:T(8,128)(2,1)S(1)}, bf16[2,16,128,128]{3,2,1,0:T(8,128)(2,1)S(1)}, u32[]{:S(2)}, u32[]{:S(2)}) collective-permute-start(bf16[2,16,128,128]{3,2,1,0:T(8,128)(2,1)S(1)} %collective-permute-done.4.refs_13_), channel_id=1, source_target_pairs={{0,224},{32,0},{64,32},{96,64},{128,96},{160,128},{192,160},{224,1... | collective-permute-start | bytes 3145736 | tf_op jit(solution)/shard_map/ppermute | solution.py:111
  41.2 1.0 copy-start.1
  61.0 44.9 %collective-permute-start.9 = (bf16[2,16,128,128]{3,2,1,0:T(8,128)(2,1)S(1)}, bf16[2,16,128,128]{3,2,1,0:T(8,128)(2,1)}, u32[]{:S(2)}, u32[]{:S(2)}) collective-permute-start(bf16[2,16,128,128]{3,2,1,0:T(8,128)(2,1)S(1)} %collective-permute-done.8.refs_11_), channel_id=1, source_target_pairs={{0,32},{32,64},{64,96},{96,128},{128,160},{160,192},{192,224},{224... | collective-permute-start | bytes 3145736 | tf_op jit(solution)/shard_map/ppermute | solution.py:110
  61.0 1.1 copy-start.3
  62.1 43.9 %collective-permute-start.12 = (bf16[2,16,128,128]{3,2,1,0:T(8,128)(2,1)S(1)}, bf16[2,16,128,128]{3,2,1,0:T(8,128)(2,1)}, u32[]{:S(2)}, u32[]{:S(2)}) collective-permute-start(bf16[2,16,128,128]{3,2,1,0:T(8,128)(2,1)S(1)} %collective-permute-done.11.refs_12_), channel_id=1, source_target_pairs={{0,224},{32,0},{64,32},{96,64},{128,96},{160,128},{192,160},{224,1... | collective-permute-start | bytes 3145736 | tf_op jit(solution)/shard_map/ppermute | solution.py:111
  64.8 1.0 copy-start.5
  83.5 44.9 %collective-permute-start.2 = (bf16[2,16,128,128]{3,2,1,0:T(8,128)(2,1)S(1)}, bf16[2,16,128,128]{3,2,1,0:T(8,128)(2,1)}, u32[]{:S(2)}, u32[]{:S(2)}) collective-permute-start(bf16[2,16,128,128]{3,2,1,0:T(8,128)(2,1)S(1)} %collective-permute-done.1.refs_8_), channel_id=1, source_target_pairs={{0,32},{32,64},{64,96},{96,128},{128,160},{160,192},{192,224},{224... | collective-permute-start | bytes 3145736 | tf_op jit(solution)/shard_map/ppermute | solution.py:110
  83.5 1.0 copy-start.7
  84.5 43.9 %collective-permute-start.6 = (bf16[2,16,128,128]{3,2,1,0:T(8,128)(2,1)S(1)}, bf16[2,16,128,128]{3,2,1,0:T(8,128)(2,1)}, u32[]{:S(2)}, u32[]{:S(2)}) collective-permute-start(bf16[2,16,128,128]{3,2,1,0:T(8,128)(2,1)S(1)} %collective-permute-done.5.refs_11_), channel_id=1, source_target_pairs={{0,224},{32,0},{64,32},{96,64},{128,96},{160,128},{192,160},{224,1... | collective-permute-start | bytes 3145736 | tf_op jit(solution)/shard_map/ppermute | solution.py:111
  87.2 1.0 copy-start.9
  106.0 71.3 %collective-permute-start.10 = (bf16[2,16,128,128]{3,2,1,0:T(8,128)(2,1)}, bf16[2,16,128,128]{3,2,1,0:T(8,128)(2,1)}, u32[]{:S(2)}, u32[]{:S(2)}) collective-permute-start(bf16[2,16,128,128]{3,2,1,0:T(8,128)(2,1)} %collective-permute-done.9.refs_9_), channel_id=1, source_target_pairs={{0,32},{32,64},{64,96},{96,128},{128,160},{160,192},{192,224},{224... | collective-permute-start | bytes 3145736 | tf_op jit(solution)/shard_map/ppermute | solution.py:110
  106.0 71.3 %collective-permute-start.13 = (bf16[2,16,128,128]{3,2,1,0:T(8,128)(2,1)}, bf16[2,16,128,128]{3,2,1,0:T(8,128)(2,1)}, u32[]{:S(2)}, u32[]{:S(2)}) collective-permute-start(bf16[2,16,128,128]{3,2,1,0:T(8,128)(2,1)} %collective-permute-done.12.refs_10_), channel_id=1, source_target_pairs={{0,224},{32,0},{64,32},{96,64},{128,96},{160,128},{192,160},{224,1... | collective-permute-start | bytes 3145736 | tf_op jit(solution)/shard_map/ppermute | solution.py:111
  128.4 66.8 %collective-permute-start.3 = (bf16[2,16,128,128]{3,2,1,0:T(8,128)(2,1)}, bf16[2,16,128,128]{3,2,1,0:T(8,128)(2,1)}, u32[]{:S(2)}, u32[]{:S(2)}) collective-permute-start(bf16[2,16,128,128]{3,2,1,0:T(8,128)(2,1)} %collective-permute-done.2.refs_8_), channel_id=1, source_target_pairs={{0,32},{32,64},{64,96},{96,128},{128,160},{160,192},{192,224},{224... | collective-permute-start | bytes 3145736 | tf_op jit(solution)/shard_map/ppermute | solution.py:113
  128.5 66.8 %collective-permute-start.7 = (bf16[2,16,128,128]{3,2,1,0:T(8,128)(2,1)}, bf16[2,16,128,128]{3,2,1,0:T(8,128)(2,1)}, u32[]{:S(2)}, u32[]{:S(2)}) collective-permute-start(bf16[2,16,128,128]{3,2,1,0:T(8,128)(2,1)} %collective-permute-done.6.refs_11_), channel_id=1, source_target_pairs={{0,224},{32,0},{64,32},{96,64},{128,96},{160,128},{192,160},{224,1... | collective-permute-start | bytes 3145736 | tf_op jit(solution)/shard_map/ppermute | solution.py:113
  132.0 1.2 copy-start.2
  133.2 1.2 copy-start.4
  134.5 1.2 copy-start.6
  135.7 24.1 %copy-start.8 = (bf16[2,16,128,128]{3,2,1,0:T(8,128)(2,1)S(1)}, bf16[2,16,128,128]{3,2,1,0:T(8,128)(2,1)}, u32[]{:S(2)}) copy-start(bf16[2,16,128,128]{3,2,1,0:T(8,128)(2,1)} %copy-done.7) | copy-start | bytes 3145732
  135.7 24.1 %copy-start.10 = (bf16[2,16,128,128]{3,2,1,0:T(8,128)(2,1)S(1)}, bf16[2,16,128,128]{3,2,1,0:T(8,128)(2,1)}, u32[]{:S(2)}) copy-start(bf16[2,16,128,128]{3,2,1,0:T(8,128)(2,1)} %copy-done.9) | copy-start | bytes 3145732
  195.3 5.8 %copy-start = (bf16[2,256,16384]{2,1,0:T(8,128)(2,1)S(1)}, bf16[2,256,16384]{2,1,0:T(8,128)(2,1)}, u32[]{:S(2)}) copy-start(bf16[2,256,16384]{2,1,0:T(8,128)(2,1)} %all-gather.2.cloned.1.call-done.refs_0_.refs_1_.refs_2_.refs_3_.refs_4_.refs_5_.refs_6_.refs_7_) | copy-start | bytes 50331652
Sparse Core Ops, SparseCore 0:
  10.0 81.7 all-gather.1

commit v2 on v0

v2 whole, which is shorter than its diff:
```python
import functools

import jax
import jax.numpy as jnp
from jax import lax
from jax.experimental import pallas as pl
from jax.experimental.pallas import tpu as pltpu
from jax.sharding import PartitionSpec as P

SIDE = 4
REL = (0, -1, 1, 2)
WIDE = 8


def swapped():
    return [(t, t ^ 1) for t in range(SIDE * SIDE * 2)]


def moved(phase, by):
    pairs = []
    for y in range(SIDE):
        for x in range(SIDE):
            for core in range(2):
                along_x = (phase + core) % 2 == 0
                to_y = y if along_x else (y + by) % SIDE
                to_x = (x + by) % SIDE if along_x else x
                pairs.append(((y * SIDE + x) * 2 + core, (to_y * SIDE + to_x) * 2 + core))
    return pairs


def turned(groups, tiles):
    half = groups // 2
    return [
        (g * tiles + t, ((g + half) % groups) * tiles + t)
        for g in range(groups)
        for t in range(tiles)
    ]


def body(pieces, low, tail, ordered, place, blocks_in, live, *refs):
    amps, tiles, out = refs[:pieces], refs[pieces:-1], refs[-1]
    block = low + pl.program_id(0)
    rows = 16 * 16
    first = lax.broadcasted_iota(jnp.int32, (16, 128), 0) < 8
    if tail is None:
        total = jnp.zeros((rows, 128), jnp.float32)
    else:
        tiles, total = tiles[:-1], tiles[-1][0]
    at = tail or 0
    for ref in tiles:
        for chunk in range(ref.shape[1] // WIDE):
            lefts = []
            for j in range(WIDE):
                entry = block * 64 + at + j
                column = pl.multiple_of(blocks_in[entry] * 128, 128)
                mask = jnp.where(first, live[2 * entry], live[2 * entry + 1]).astype(jnp.bfloat16)
                left = [(a[:, :, pl.ds(column, 128)] * mask[None]).reshape(-1, 128) for a in amps]
                lefts.append(jnp.concatenate(left, axis=0))
            left = jnp.concatenate(lefts, axis=1)
            right = ref[0, pl.ds(chunk * WIDE, WIDE)].reshape(WIDE * 128, 128)
            total += jnp.dot(left, right, preferred_element_type=jnp.float32)
            at += WIDE
    if ordered:
        for i in range(16):
            row = pl.multiple_of(place[i] * 16, 16)
            out[0, pl.ds(row, 16), :] = total[16 * i : 16 * (i + 1)]
    else:
        out[0] = total


def partial_ladder(group, amps, tiles, flips, tail, acc, ordered, place, blocks_in, live, low=0, high=8, light=1):
    rows = 256
    count = sum(x.shape[1] for x in tiles)

    def tile_map(flip, block, *_):
        return (low + block + 4 * flip) % 8, 0, 0, 0

    def out_map(block, *_):
        return block // 4, 0, block % 4

    specs = [pl.BlockSpec((2, *amps[0].shape[1:]), lambda *_: (group, 0, 0), pipeline_mode=pl.Buffered(1))] * len(amps)
    for x, flip in zip(tiles, flips, strict=True):
        specs.append(pl.BlockSpec((1, *x.shape[1:]), functools.partial(tile_map, flip)))
    if acc is not None:
        specs.append(pl.BlockSpec((1, rows, 128), out_map))
        tiles = [*tiles, acc]
    return pl.pallas_call(
        functools.partial(body, len(amps), low, tail, ordered),
        out_shape=jax.ShapeDtypeStruct(((high - low) // 4, rows, 512), jnp.float32),
        grid_spec=pltpu.PrefetchScalarGridSpec(
            num_scalar_prefetch=3,
            grid=(high - low,),
            in_specs=specs,
            out_specs=pl.BlockSpec((1, rows, 128), out_map),
        ),
        compiler_params=pltpu.CompilerParams(vmem_limit_bytes=24 * 1024 * 1024),
        cost_estimate=pl.CostEstimate(
            flops=2 * rows * count * 128 * 128 * (high - low) // light,
            bytes_accessed=(8 + count * (high - low) // 32) * 1024 * 1024 // light,
            transcendentals=0,
        ),
    )(place, blocks_in, live, *amps, *tiles)


def after(value, *done):
    return lax.optimization_barrier((value, done))[0]


def gather(shard, phase, steps):
    return [lax.ppermute(shard, "tile", moved(phase, step)) for step in steps]


def on_device(groups, tiles, amplitudes, integrals, tile_in, tile_list, tile_count):
    pool = tile_in.shape[1]
    me, tile = lax.axis_index("grp"), lax.axis_index("tile")
    y, x, core = tile // (2 * SIDE), (tile // 2) % SIDE, tile % 2
    plus = [(i, (i + 1) % groups) for i in range(groups)]
    minus = [(i, (i - 1) % groups) for i in range(groups)]
    both = ("grp", "tile")

    slots = jnp.arange(tile_list.shape[-1], dtype=jnp.int32)
    listed = tile_list[..., None] == jnp.arange(pool, dtype=jnp.int32)
    within = (slots < tile_count[..., None])[..., None]
    live = jnp.any(listed & within, axis=2).astype(jnp.int32)
    table = jnp.concatenate([tile_in[None], live], axis=0)
    other_table = lax.ppermute(table, "tile", swapped())
    table = jnp.concatenate([table, other_table], axis=1)
    table = jnp.roll(table, (2 - me) * 16, axis=2)
    low_near, high_near, low_half, high_half = (
        table[..., a:b] for a, b in ((16, 32), (48, 64), (8, 16), (64, 72))
    )
    zero = core == 0
    table = jnp.concatenate(
        [
            table[..., 32:48],
            jnp.where(zero, low_near, high_near),
            jnp.where(zero, high_near, low_near),
            jnp.where(zero, low_half, high_half),
            jnp.where(zero, high_half, low_half),
        ],
        axis=2,
    )
    blocks_in = table[0].reshape(-1)
    live = jnp.transpose(table[1:], (1, 2, 0)).reshape(-1).astype(jnp.float32)
    rel = jnp.array(REL, jnp.int32)
    along_1, along_2 = jnp.where(core == 0, x, y), jnp.where(core == 0, y, x)
    step_1, step_2 = jnp.where(core == 0, 1, SIDE), jnp.where(core == 0, SIDE, 1)
    place = ((along_2 + rel) % SIDE)[:, None] * step_2 + ((along_1 + rel) % SIDE)[None, :] * step_1
    place = place.reshape(-1).astype(jnp.int32)

    own = amplitudes.reshape(16, amplitudes.shape[-1])
    far = lax.ppermute(own, both, turned(groups, tiles))

    onward = [
        (g * tiles + t, ((g + (-1 if t % 2 else 1)) % groups) * tiles + t)
        for g in range(groups)
        for t in range(tiles)
    ]
    held = jnp.concatenate([integrals, lax.ppermute(integrals, "tile", swapped())], axis=0)
    own_near = gather(own, 0, (1, -1, 2))
    held, far, *own_near = lax.optimization_barrier((held, far, *own_near))
    near = lax.ppermute(held, both, onward)
    far_near = gather(far, 0, (1, -1, 2))
    fore = jnp.stack([own, own_near[0], far, far_near[0]])
    aft = jnp.stack([own_near[1], own_near[2], far_near[1], far_near[2]])
    fore_before = lax.ppermute(fore, "tile", moved(1, 1))
    aft_behind = lax.ppermute(aft, "tile", moved(1, -1))
    aft_before = lax.ppermute(aft, "tile", moved(1, 1))
    fore_behind = lax.ppermute(fore, "tile", moved(1, -1))
    fore_beyond = lax.ppermute(fore_before, "tile", moved(1, 1))
    aft_beyond = lax.ppermute(aft_behind, "tile", moved(1, -1))
    amps = [fore, aft, fore_before, aft_before, fore_behind, aft_behind, fore_beyond, aft_beyond]
    near = after(near, fore_before, aft_behind, fore_behind, aft_before)
    half = jnp.where(zero, near[:, 8:], near[:, :8])
    half = lax.ppermute(half, both, onward)
    near_other = lax.ppermute(near, "tile", swapped())

    facts = (place, blocks_in, live)
    first, flips, last_flips = [held, near, near_other], (0, 0, 1), (0, 1)
    back = partial_ladder(1, amps, first, flips, None, None, False, *facts)
    half_other = lax.ppermute(half, "tile", swapped())
    last = [half, half_other]
    back_1 = partial_ladder(1, amps, last, last_flips, 48, back[1:], True, *facts, low=4)
    back_1 = lax.ppermute(back_1[0].astype(jnp.float16), both, turned(groups, tiles))
    back_0 = partial_ladder(1, amps, last, last_flips, 48, back[:1], True, *facts, high=4)
    back_0 = lax.ppermute(back_0[0].astype(jnp.float16), both, turned(groups, tiles))
    every, flips = [*first, *last], (0, 0, 1, 0, 1)
    here_1 = partial_ladder(0, amps, every, flips, None, None, True, *facts, low=4)[0]
    here_0 = partial_ladder(0, amps, every, flips, None, None, True, *facts, high=4)[0]

    other = lax.ppermute((0.5 * (here_1 + back_1.astype(jnp.float32))).astype(jnp.bfloat16), "tile", swapped())
    same = (0.5 * (here_0 + back_0.astype(jnp.float32))).astype(jnp.bfloat16)
    even = jnp.where(zero, same, other).reshape(SIDE * SIDE, 2, 1, 8, 512)
    odd = jnp.where(zero, other, same).reshape(SIDE * SIDE, 2, 1, 8, 512)
    result = jnp.concatenate([even, odd], axis=2).transpose(1, 0, 2, 3, 4)
    return result.reshape(2, 256, 512)


def solution(mesh):
    placed = (
        P(None, ("grp", "tile"), None),
        P("tile", "grp", None, None),
        P("tile", None),
        P(None, "tile", None),
        P(None, "tile"),
    )
    return jax.shard_map(
        functools.partial(on_device, mesh.shape["grp"], mesh.shape["tile"]),
        mesh=mesh,
        in_specs=placed,
        out_specs=P(None, "grp", "tile"),
        check_vma=False,
    )
```

time: 322 us -> 197 us (0.61)
  waiting for transfers between devices: 177 us -> 86.7 us
  local copies, waits for them, and re-layouts: 78.9 us -> 12.5 us
  matrix products: 48.9 us -> 0 us
  starting transfers between devices: 0.04 us -> 47.4 us
  Pallas kernels: 0 us -> 43.3 us
  between operations: 13.5 us -> 0.33 us
  other arithmetic: 1.35 us -> 6.08 us
    all_gather x2 -> x0, waiting for transfers between devices: 176 us -> none  [the longest x1 176 us: on_device(): gathered = lax.all_gather(integrals, 'grp', axis=1, tiled=True)]
    ppermute x0 -> x22, waiting for transfers between devices: none -> 86.7 us  [the longest x1 24.1 us: on_device(): half = lax.ppermute(half, both, onward)]
    reshape x3 -> x0, local copies, waits for them, and re-layouts: 77.1 us -> none  [the longest x2 51.7 us: dense_tiles(): dense.astype(jnp.bfloat16)]
    dot_general x4 -> x0, matrix products: 48.9 us -> none  [the longest x2 25.4 us: ladder(): jnp.einsum('hx,lxj->hlj', slab_rows, dense, preferred_element_type=jnp.fl...]
    ppermute x0 -> x22, starting transfers between devices: none -> 47.4 us  [the longest x1 9.67 us: on_device(): near = lax.ppermute(held, both, onward)]
    pallas_call x0 -> x5, Pallas kernels: none -> 43.3 us  [partial_ladder(): pl.pallas_call(functools.partial(body, len(amps), low, tail, ordered), ou...]
    unnamed x2 -> x28, local copies, waits for them, and re-layouts: 0.01 us -> 11 us
  transfers between devices with their start and end apart: 2 -> 22, of which waited for: 1 -> 11; matrix products, arithmetic and copies ran while one was open for 32% -> 3% of each run, Pallas kernels for 0% -> 19%
where the time goes in v2:
time: 197 us; the launch traced here: 196 us
  waiting for transfers between devices  86.7 us (44%)
  starting transfers between devices  47.4 us (24%)
  Pallas kernels  43.3 us (22%)
  local copies, waits for them, and re-layouts  12.5 us (6%)
  other arithmetic  6.08 us (3%)
    pallas_call x5, Pallas kernels, partial_ladder(): pl.pallas_call(functools.partial(body, len(amps), low, tail, ordered), ou...  43.3 us
    ppermute x1, waiting for transfers between devices, on_device(): half = lax.ppermute(half, both, onward)  24.1 us
    ppermute x1, waiting for transfers between devices, on_device(): aft_behind = lax.ppermute(aft, 'tile', moved(1, -1))  19 us
    ppermute x1, waiting for transfers between devices, on_device(): fore_behind = lax.ppermute(fore, 'tile', moved(1, -1))  18.6 us
    unnamed x28, local copies, waits for them, and re-layouts  11 us
    ppermute x1, starting transfers between devices, on_device(): near = lax.ppermute(held, both, onward)  9.67 us
    ppermute x1, waiting for transfers between devices, on_device(): far = lax.ppermute(own, both, turned(groups, tiles))  7.79 us
    ppermute x6, waiting for transfers between devices, gather(): return [lax.ppermute(shard, 'tile', moved(phase, step)) for step in steps]  6.93 us
  transfers between devices with their start and end apart: 22, of which 11 were waited for; matrix products, arithmetic and copies ran while one was open for 3% of the time, Pallas kernels for 19%

profile of v2, /device:TPU:1, one launch (start us, length us, event | category | flops | bytes accessed | tf_op | source)
XLA Modules:
  0.0 196.4 jit_solution(18444915049343646539)
XLA Ops:
  0.0 3.2 %collective-permute-start.1 = (bf16[4,16,128,128]{3,2,1,0:T(8,128)(2,1)}, bf16[4,16,128,128]{3,2,1,0:T(8,128)(2,1)S(1)}, u32[]{:S(2)}, u32[]{:S(2)}) collective-permute-start(bf16[4,16,128,128]{3,2,1,0:T(8,128)(2,1)} %param.7), channel_id=1, source_target_pairs={{0,1},{1,0},{2,3},{3,2},{4,5},{5,4},{6,7},{7,6},{8,9},{9,8},{10,11... | collective-permute-start | bytes 6291464 | tf_op jit(solution)/shard_map/ppermute | solution.py:159
  3.2 1.2 collective-permute-start.5
  4.4 0.8 collective-permute-start.4
  5.2 0.7 collective-permute-start.3
  5.9 6.9 %collective-permute-start.2 = (bf16[16,16384]{1,0:T(8,128)(2,1)}, bf16[16,16384]{1,0:T(8,128)(2,1)S(1)}, u32[]{:S(2)}, u32[]{:S(2)}) collective-permute-start(bf16[16,16384]{1,0:T(8,128)(2,1)} %bitcast.42), channel_id=1, source_target_pairs={{0,128},{1,129},{2,130},{3,131},{4,132},{5,133},{6,134},{7,135},{8... | collective-permute-start | bytes 1572872 | tf_op jit(solution)/shard_map/ppermute | solution.py:152
  12.8 0.0 collective-permute-done.1
  12.8 2.0 pad_maximum_fusion.refs_8_
  14.8 0.0 collective-permute-done.5
  14.8 2.8 %collective-permute-done.4 = bf16[16,16384]{1,0:T(8,128)(2,1)S(1)} collective-permute-done((bf16[16,16384]{1,0:T(8,128)(2,1)}, bf16[16,16384]{1,0:T(8,128)(2,1)S(1)}, u32[]{:S(2)}, u32[]{:S(2)}) %collective-permute-start.4) | collective-permute-done | bytes 524320 | tf_op jit(solution)/shard_map/ppermute | solution.py:110
  17.6 1.4 collective-permute-done.3
  18.9 7.8 %collective-permute-done.2 = bf16[16,16384]{1,0:T(8,128)(2,1)S(1)} collective-permute-done((bf16[16,16384]{1,0:T(8,128)(2,1)}, bf16[16,16384]{1,0:T(8,128)(2,1)S(1)}, u32[]{:S(2)}, u32[]{:S(2)}) %collective-permute-start.2) | collective-permute-done | bytes 524320 | tf_op jit(solution)/shard_map/ppermute | solution.py:152
  26.7 2.3 %collective-permute-start.8 = (bf16[16,16384]{1,0:T(8,128)(2,1)S(1)}, bf16[16,16384]{1,0:T(8,128)(2,1)S(1)}, u32[]{:S(2)}, u32[]{:S(2)}) collective-permute-start(bf16[16,16384]{1,0:T(8,128)(2,1)S(1)} %collective-permute-done.2), channel_id=1, source_target_pairs={{0,4},{1,17},{2,6},{3,19},{4,0},{5,21},{6,2},{7,23},{8,12},{9,25},... | collective-permute-start | bytes 1572872 | tf_op jit(solution)/shard_map/ppermute | solution.py:110
  29.0 0.3 collective-permute-start.7
  29.4 9.7 %collective-permute-start.15 = (bf16[8,16,128,128]{3,2,1,0:T(8,128)(2,1)S(1)}, bf16[8,16,128,128]{3,2,1,0:T(8,128)(2,1)}, u32[]{:S(2)}, u32[]{:S(2)}) collective-permute-start(bf16[8,16,128,128]{3,2,1,0:T(8,128)(2,1)S(1)} %pad_maximum_fusion.refs_8_), channel_id=1, source_target_pairs={{0,32},{1,225},{2,34},{3,227},{4,36},{5,229},{6,38},{7,231},{8,40}... | collective-permute-start | bytes 12582920 | tf_op jit(solution)/shard_map/ppermute | solution.py:162
  39.0 2.8 %collective-permute-done.6 = bf16[16,16384]{1,0:T(8,128)(2,1)S(1)} collective-permute-done((bf16[16,16384]{1,0:T(8,128)(2,1)S(1)}, bf16[16,16384]{1,0:T(8,128)(2,1)S(1)}, u32[]{:S(2)}, u32[]{:S(2)}) %collective-permute-start.6) | collective-permute-done | bytes 524320 | tf_op jit(solution)/shard_map/ppermute | solution.py:110
  41.9 0.3 pad_maximum_fusion.1.refs_0_
  42.1 3.2 %collective-permute-start.11 = (bf16[4,16,16384]{2,1,0:T(8,128)(2,1)S(1)}, bf16[4,16,16384]{2,1,0:T(8,128)(2,1)S(1)}, u32[]{:S(2)}, u32[]{:S(2)}) collective-permute-start(bf16[4,16,16384]{2,1,0:T(8,128)(2,1)S(1)} %pad_maximum_fusion.1.refs_0_), channel_id=1, source_target_pairs={{0,24},{1,7},{2,26},{3,1},{4,28},{5,3},{6,30},{7,5},{8,0},{9,15},{... | collective-permute-start | bytes 6291464 | tf_op jit(solution)/shard_map/ppermute | solution.py:169
  45.3 0.3 pad_maximum_fusion.2.refs_1_
  45.6 2.7 %collective-permute-start.12 = (bf16[4,16,16384]{2,1,0:T(8,128)(2,1)S(1)}, bf16[4,16,16384]{2,1,0:T(8,128)(2,1)}, u32[]{:S(2)}, u32[]{:S(2)}) collective-permute-start(bf16[4,16,16384]{2,1,0:T(8,128)(2,1)S(1)} %pad_maximum_fusion.2.refs_1_), channel_id=1, source_target_pairs={{0,24},{1,7},{2,26},{3,1},{4,28},{5,3},{6,30},{7,5},{8,0},{9,15},{... | collective-permute-start | bytes 6291464 | tf_op jit(solution)/shard_map/ppermute | solution.py:167
  48.3 1.4 copy-done
  49.7 18.6 %collective-permute-done.11.refs_4_ = bf16[4,16,16384]{2,1,0:T(8,128)(2,1)S(1)} collective-permute-done((bf16[4,16,16384]{2,1,0:T(8,128)(2,1)S(1)}, bf16[4,16,16384]{2,1,0:T(8,128)(2,1)S(1)}, u32[]{:S(2)}, u32[]{:S(2)}) %collective-permute-start.11) | collective-permute-done | bytes 2097184 | tf_op jit(solution)/shard_map/ppermute | solution.py:169
  68.3 1.3 copy-done.5
  69.6 2.2 %collective-permute-done.9.refs_2_ = bf16[4,16,16384]{2,1,0:T(8,128)(2,1)} collective-permute-done((bf16[4,16,16384]{2,1,0:T(8,128)(2,1)S(1)}, bf16[4,16,16384]{2,1,0:T(8,128)(2,1)}, u32[]{:S(2)}, u32[]{:S(2)}) %collective-permute-start.9) | collective-permute-done | bytes 2097184 | tf_op jit(solution)/shard_map/ppermute | solution.py:166
  71.8 19.0 %collective-permute-done.12.refs_5_ = bf16[4,16,16384]{2,1,0:T(8,128)(2,1)} collective-permute-done((bf16[4,16,16384]{2,1,0:T(8,128)(2,1)S(1)}, bf16[4,16,16384]{2,1,0:T(8,128)(2,1)}, u32[]{:S(2)}, u32[]{:S(2)}) %collective-permute-start.12) | collective-permute-done | bytes 2097184 | tf_op jit(solution)/shard_map/ppermute | solution.py:167
  90.7 3.4 %collective-permute-done.10.refs_3_ = bf16[4,16,16384]{2,1,0:T(8,128)(2,1)S(1)} collective-permute-done((bf16[4,16,16384]{2,1,0:T(8,128)(2,1)S(1)}, bf16[4,16,16384]{2,1,0:T(8,128)(2,1)S(1)}, u32[]{:S(2)}, u32[]{:S(2)}) %collective-permute-start.10) | collective-permute-done | bytes 2097184 | tf_op jit(solution)/shard_map/ppermute | solution.py:168
  94.2 1.4 copy-done.7
  95.5 0.9 collective-permute-start.16
  96.4 2.5 %slice_select_fusion = bf16[8,8,128,128]{3,2,1,0:T(8,128)(2,1)S(1)} fusion(bf16[8,16,128,128]{3,2,1,0:T(8,128)(2,1)} %collective-permute-done.15.refs_9_, pred[]{:T(512)S(6)} %eq.16), kind=kLoop, calls=%fused_computation.3 | loop fusion | flops 1048576 | bytes 6291457 | tf_op jit(solution)/shard_map/jit(_where)/select_n | solution.py:174
  98.9 5.7 %collective-permute-start.17 = (bf16[8,8,128,128]{3,2,1,0:T(8,128)(2,1)S(1)}, bf16[8,8,128,128]{3,2,1,0:T(8,128)(2,1)}, u32[]{:S(2)}, u32[]{:S(2)}) collective-permute-start(bf16[8,8,128,128]{3,2,1,0:T(8,128)(2,1)S(1)} %slice_select_fusion), channel_id=1, source_target_pairs={{0,32},{1,225},{2,34},{3,227},{4,36},{5,229},{6,38},{7,231},{8,40}... | collective-permute-start | bytes 6291464 | tf_op jit(solution)/shard_map/ppermute | solution.py:175
  104.5 0.1 collective-permute-start.13
  104.6 2.6 %collective-permute-start.14 = (bf16[4,16,16384]{2,1,0:T(8,128)(2,1)}, bf16[4,16,16384]{2,1,0:T(8,128)(2,1)}, u32[]{:S(2)}, u32[]{:S(2)}) collective-permute-start(bf16[4,16,16384]{2,1,0:T(8,128)(2,1)} %collective-permute-done.12.refs_5_), channel_id=1, source_target_pairs={{0,24},{1,7},{2,26},{3,1},{4,28},{5,3},{6,30},{7,5},{8,0},{9,15},{... | collective-permute-start | bytes 6291464 | tf_op jit(solution)/shard_map/ppermute | solution.py:171
  107.2 24.1 %collective-permute-done.17.refs_11_.refs_8_ = bf16[8,8,128,128]{3,2,1,0:T(8,128)(2,1)} collective-permute-done((bf16[8,8,128,128]{3,2,1,0:T(8,128)(2,1)S(1)}, bf16[8,8,128,128]{3,2,1,0:T(8,128)(2,1)}, u32[]{:S(2)}, u32[]{:S(2)}) %collective-permute-start.17) | collective-permute-done | bytes 2097184 | tf_op jit(solution)/shard_map/ppermute | solution.py:175
  131.4 0.5 collective-permute-start.18
  131.9 0.1 iota_compare_fusion.1
  132.0 0.4 fusion.5
  132.3 0.1 collective-permute-start
  132.5 0.1 broadcast_add_fusion
  132.6 0.1 add.75.place
  132.7 3.0 %collective-permute-done = s32[3,4,128]{2,1,0:T(4,128)S(1)} collective-permute-done((s32[3,4,128]{2,1,0:T(4,128)S(1)}, s32[3,4,128]{2,1,0:T(4,128)S(1)}, u32[]{:S(2)}, u32[]{:S(2)}) %collective-permute-start) | collective-permute-done | bytes 6176 | tf_op jit(solution)/shard_map/ppermute | solution.py:126
  135.7 0.1 fusion.8
  135.8 0.1 slice_select_fusion.1
  135.8 0.1 slice_select_fusion.3
  135.9 0.1 concatenate.22
  136.0 0.1 reshape_squeeze.3.blocks_in
  136.1 0.2 copy.14
  136.3 0.2 convert_element_type.37.live
  136.5 1.6 copy-done.1
  138.1 2.2 %copy-done.3 = bf16[8,16,128,128]{3,2,1,0:T(8,128)(2,1)S(1)} copy-done((bf16[8,16,128,128]{3,2,1,0:T(8,128)(2,1)S(1)}, bf16[8,16,128,128]{3,2,1,0:T(8,128)(2,1)}, u32[]{:S(2)}) %copy-start.3) | copy-done | bytes 4194328
  140.3 1.6 copy-done.6
  141.8 1.6 copy-done.8
  143.4 12.6 %shard_map.65 = f32[2,256,512]{2,1,0:T(8,128)S(1)} custom-call(s32[16]{0:T(128)S(1)} %add.75.place, s32[512]{0:T(512)S(1)} %reshape_squeeze.3.blocks_in, f32[1024]{0:T(1024)S(1)} %convert_element_type.37.live, bf16[4,16,16384]{2,1,0:T(8,128)(2,1)S(1)} %pad_maximum_fusion.1.refs_0_, bf16[4,16,16384]{2,1,0:T(8,128)(2,1)S(1)} %copy-done.1, ...), custom_call_target="tpu_custom_call" | custom-call | flops 3221225472 | bytes 20971520 | tf_op jit(solution)/shard_map/pallas_call | solution.py:87
  156.0 0.1 fusion.16
  156.1 5.8 %shard_map.68 = f32[1,256,512]{2,1,0:T(8,128)S(1)} custom-call(s32[16]{0:T(128)S(1)} %add.75.place, s32[512]{0:T(512)S(1)} %reshape_squeeze.3.blocks_in, f32[1024]{0:T(1024)S(1)} %convert_element_type.37.live, bf16[4,16,16384]{2,1,0:T(8,128)(2,1)S(1)} %pad_maximum_fusion.1.refs_0_, bf16[4,16,16384]{2,1,0:T(8,128)(2,1)S(1)} %copy-done.1, ...), custom_call_target="tpu_custom_call" | custom-call | flops 536870912 | bytes 10485760 | tf_op jit(solution)/shard_map/pallas_call | solution.py:87
  161.9 5.1 %collective-permute-start.20 = (f16[256,512]{1,0:T(8,128)(2,1)S(1)}, f16[256,512]{1,0:T(8,128)(2,1)S(1)}, u32[]{:S(2)}, u32[]{:S(2)}) collective-permute-start(f16[256,512]{1,0:T(8,128)(2,1)S(1)} %convert_bitcast_fusion), channel_id=1, source_target_pairs={{0,128},{1,129},{2,130},{3,131},{4,132},{5,133},{6,134},{7,135},{8... | collective-permute-start | bytes 786440 | tf_op jit(solution)/shard_map/ppermute | solution.py:184
  167.0 6.0 %shard_map.66 = f32[1,256,512]{2,1,0:T(8,128)S(1)} custom-call(s32[16]{0:T(128)S(1)} %add.75.place, s32[512]{0:T(512)S(1)} %reshape_squeeze.3.blocks_in, f32[1024]{0:T(1024)S(1)} %convert_element_type.37.live, bf16[4,16,16384]{2,1,0:T(8,128)(2,1)S(1)} %pad_maximum_fusion.1.refs_0_, bf16[4,16,16384]{2,1,0:T(8,128)(2,1)S(1)} %copy-done.1, ...), custom_call_target="tpu_custom_call" | custom-call | flops 536870912 | bytes 10485760 | tf_op jit(solution)/shard_map/pallas_call | solution.py:87
  173.1 0.4 collective-permute-start.19
  173.6 9.5 %shard_map.67 = f32[1,256,512]{2,1,0:T(8,128)S(1)} custom-call(s32[16]{0:T(128)S(1)} %add.75.place, s32[512]{0:T(512)S(1)} %reshape_squeeze.3.blocks_in, f32[1024]{0:T(1024)S(1)} %convert_element_type.37.live, bf16[4,16,16384]{2,1,0:T(8,128)(2,1)S(1)} %pad_maximum_fusion.1.refs_0_, bf16[4,16,16384]{2,1,0:T(8,128)(2,1)S(1)} %copy-done.1, ...), custom_call_target="tpu_custom_call" | custom-call | flops 2147483648 | bytes 16777216 | tf_op jit(solution)/shard_map/pallas_call | solution.py:87
  183.1 0.1 fusion.1
  183.2 1.0 collective-permute-start.21
  184.1 9.5 %shard_map.64 = f32[1,256,512]{2,1,0:T(8,128)S(1)} custom-call(s32[16]{0:T(128)S(1)} %add.75.place, s32[512]{0:T(512)S(1)} %reshape_squeeze.3.blocks_in, f32[1024]{0:T(1024)S(1)} %convert_element_type.37.live, bf16[4,16,16384]{2,1,0:T(8,128)(2,1)S(1)} %pad_maximum_fusion.1.refs_0_, bf16[4,16,16384]{2,1,0:T(8,128)(2,1)S(1)} %copy-done.1, ...), custom_call_target="tpu_custom_call" | custom-call | flops 2147483648 | bytes 16777216 | tf_op jit(solution)/shard_map/pallas_call | solution.py:87
  193.6 1.7 collective-permute-done.19
  195.4 0.1 broadcast_select_fusion.1
  195.5 0.1 maximum_bitcast_fusion
  195.6 0.9 copy.15
  (40 shorter events, 0.2 us)
Async XLA Ops:
  0.0 12.8 %collective-permute-start.1 = (bf16[4,16,128,128]{3,2,1,0:T(8,128)(2,1)}, bf16[4,16,128,128]{3,2,1,0:T(8,128)(2,1)S(1)}, u32[]{:S(2)}, u32[]{:S(2)}) collective-permute-start(bf16[4,16,128,128]{3,2,1,0:T(8,128)(2,1)} %param.7), channel_id=1, source_target_pairs={{0,1},{1,0},{2,3},{3,2},{4,5},{5,4},{6,7},{7,6},{8,9},{9,8},{10,11... | collective-permute-start | bytes 6291464 | tf_op jit(solution)/shard_map/ppermute | solution.py:159
  3.2 38.6 %copy-start.9 = (bf16[2,8,16384]{2,1,0:T(8,128)(2,1)S(1)}, bf16[2,8,16384]{2,1,0:T(8,128)(2,1)}, u32[]{:S(2)}) copy-start(bf16[2,8,16384]{2,1,0:T(8,128)(2,1)} %param.6) | copy-start | bytes 1572868
  3.2 11.5 %collective-permute-start.5 = (bf16[16,16384]{1,0:T(8,128)(2,1)}, bf16[16,16384]{1,0:T(8,128)(2,1)S(1)}, u32[]{:S(2)}, u32[]{:S(2)}) collective-permute-start(bf16[16,16384]{1,0:T(8,128)(2,1)} %bitcast.39), channel_id=1, source_target_pairs={{0,4},{1,17},{2,6},{3,19},{4,0},{5,21},{6,2},{7,23},{8,12},{9,25},... | collective-permute-start | bytes 1572872 | tf_op jit(solution)/shard_map/ppermute | solution.py:110
  4.4 13.1 %collective-permute-start.4 = (bf16[16,16384]{1,0:T(8,128)(2,1)}, bf16[16,16384]{1,0:T(8,128)(2,1)S(1)}, u32[]{:S(2)}, u32[]{:S(2)}) collective-permute-start(bf16[16,16384]{1,0:T(8,128)(2,1)} %bitcast.40), channel_id=1, source_target_pairs={{0,6},{1,25},{2,0},{3,27},{4,2},{5,29},{6,4},{7,31},{8,14},{9,1},{... | collective-permute-start | bytes 1572872 | tf_op jit(solution)/shard_map/ppermute | solution.py:110
  5.2 13.7 %collective-permute-start.3 = (bf16[16,16384]{1,0:T(8,128)(2,1)}, bf16[16,16384]{1,0:T(8,128)(2,1)S(1)}, u32[]{:S(2)}, u32[]{:S(2)}) collective-permute-start(bf16[16,16384]{1,0:T(8,128)(2,1)} %bitcast.41), channel_id=1, source_target_pairs={{0,2},{1,9},{2,4},{3,11},{4,6},{5,13},{6,0},{7,15},{8,10},{9,17},{... | collective-permute-start | bytes 1572872 | tf_op jit(solution)/shard_map/ppermute | solution.py:110
  5.9 20.8 %collective-permute-start.2 = (bf16[16,16384]{1,0:T(8,128)(2,1)}, bf16[16,16384]{1,0:T(8,128)(2,1)S(1)}, u32[]{:S(2)}, u32[]{:S(2)}) collective-permute-start(bf16[16,16384]{1,0:T(8,128)(2,1)} %bitcast.42), channel_id=1, source_target_pairs={{0,128},{1,129},{2,130},{3,131},{4,132},{5,133},{6,134},{7,135},{8... | collective-permute-start | bytes 1572872 | tf_op jit(solution)/shard_map/ppermute | solution.py:152
  14.8 27.4 %copy-start.2 = (bf16[8,16,128,128]{3,2,1,0:T(8,128)(2,1)}, bf16[8,16,128,128]{3,2,1,0:T(8,128)(2,1)S(1)}, u32[]{:S(2)}) copy-start(bf16[8,16,128,128]{3,2,1,0:T(8,128)(2,1)S(1)} %pad_maximum_fusion.refs_8_) | copy-start | bytes 12582916
  26.7 15.2 %collective-permute-start.6 = (bf16[16,16384]{1,0:T(8,128)(2,1)S(1)}, bf16[16,16384]{1,0:T(8,128)(2,1)S(1)}, u32[]{:S(2)}, u32[]{:S(2)}) collective-permute-start(bf16[16,16384]{1,0:T(8,128)(2,1)S(1)} %collective-permute-done.2), channel_id=1, source_target_pairs={{0,2},{1,9},{2,4},{3,11},{4,6},{5,13},{6,0},{7,15},{8,10},{9,17},{... | collective-permute-start | bytes 1572872 | tf_op jit(solution)/shard_map/ppermute | solution.py:110
  26.7 18.6 %collective-permute-start.8 = (bf16[16,16384]{1,0:T(8,128)(2,1)S(1)}, bf16[16,16384]{1,0:T(8,128)(2,1)S(1)}, u32[]{:S(2)}, u32[]{:S(2)}) collective-permute-start(bf16[16,16384]{1,0:T(8,128)(2,1)S(1)} %collective-permute-done.2), channel_id=1, source_target_pairs={{0,4},{1,17},{2,6},{3,19},{4,0},{5,21},{6,2},{7,23},{8,12},{9,25},... | collective-permute-start | bytes 1572872 | tf_op jit(solution)/shard_map/ppermute | solution.py:110
  29.0 16.3 %collective-permute-start.7 = (bf16[16,16384]{1,0:T(8,128)(2,1)S(1)}, bf16[16,16384]{1,0:T(8,128)(2,1)S(1)}, u32[]{:S(2)}, u32[]{:S(2)}) collective-permute-start(bf16[16,16384]{1,0:T(8,128)(2,1)S(1)} %collective-permute-done.2), channel_id=1, source_target_pairs={{0,6},{1,25},{2,0},{3,27},{4,2},{5,29},{6,4},{7,31},{8,14},{9,1},{... | collective-permute-start | bytes 1572872 | tf_op jit(solution)/shard_map/ppermute | solution.py:110
  29.4 66.1 %collective-permute-start.15 = (bf16[8,16,128,128]{3,2,1,0:T(8,128)(2,1)S(1)}, bf16[8,16,128,128]{3,2,1,0:T(8,128)(2,1)}, u32[]{:S(2)}, u32[]{:S(2)}) collective-permute-start(bf16[8,16,128,128]{3,2,1,0:T(8,128)(2,1)S(1)} %pad_maximum_fusion.refs_8_), channel_id=1, source_target_pairs={{0,32},{1,225},{2,34},{3,227},{4,36},{5,229},{6,38},{7,231},{8,40}... | collective-permute-start | bytes 12582920 | tf_op jit(solution)/shard_map/ppermute | solution.py:162
  42.1 26.1 %collective-permute-start.11 = (bf16[4,16,16384]{2,1,0:T(8,128)(2,1)S(1)}, bf16[4,16,16384]{2,1,0:T(8,128)(2,1)S(1)}, u32[]{:S(2)}, u32[]{:S(2)}) collective-permute-start(bf16[4,16,16384]{2,1,0:T(8,128)(2,1)S(1)} %pad_maximum_fusion.1.refs_0_), channel_id=1, source_target_pairs={{0,24},{1,7},{2,26},{3,1},{4,28},{5,3},{6,30},{7,5},{8,0},{9,15},{... | collective-permute-start | bytes 6291464 | tf_op jit(solution)/shard_map/ppermute | solution.py:169
  45.3 26.5 %collective-permute-start.9 = (bf16[4,16,16384]{2,1,0:T(8,128)(2,1)S(1)}, bf16[4,16,16384]{2,1,0:T(8,128)(2,1)}, u32[]{:S(2)}, u32[]{:S(2)}) collective-permute-start(bf16[4,16,16384]{2,1,0:T(8,128)(2,1)S(1)} %pad_maximum_fusion.1.refs_0_), channel_id=1, source_target_pairs={{0,8},{1,3},{2,10},{3,5},{4,12},{5,7},{6,14},{7,1},{8,16},{9,11},{... | collective-permute-start | bytes 6291464 | tf_op jit(solution)/shard_map/ppermute | solution.py:166
  45.6 45.2 %collective-permute-start.12 = (bf16[4,16,16384]{2,1,0:T(8,128)(2,1)S(1)}, bf16[4,16,16384]{2,1,0:T(8,128)(2,1)}, u32[]{:S(2)}, u32[]{:S(2)}) collective-permute-start(bf16[4,16,16384]{2,1,0:T(8,128)(2,1)S(1)} %pad_maximum_fusion.2.refs_1_), channel_id=1, source_target_pairs={{0,24},{1,7},{2,26},{3,1},{4,28},{5,3},{6,30},{7,5},{8,0},{9,15},{... | collective-permute-start | bytes 6291464 | tf_op jit(solution)/shard_map/ppermute | solution.py:167
  48.3 45.8 %collective-permute-start.10 = (bf16[4,16,16384]{2,1,0:T(8,128)(2,1)S(1)}, bf16[4,16,16384]{2,1,0:T(8,128)(2,1)S(1)}, u32[]{:S(2)}, u32[]{:S(2)}) collective-permute-start(bf16[4,16,16384]{2,1,0:T(8,128)(2,1)S(1)} %pad_maximum_fusion.2.refs_1_), channel_id=1, source_target_pairs={{0,8},{1,3},{2,10},{3,5},{4,12},{5,7},{6,14},{7,1},{8,16},{9,11},{... | collective-permute-start | bytes 6291464 | tf_op jit(solution)/shard_map/ppermute | solution.py:168
  48.3 1.4 copy-start
  68.3 1.3 copy-start.5
  94.2 1.4 copy-start.7
  95.5 41.0 %collective-permute-start.16 = (bf16[8,16,128,128]{3,2,1,0:T(8,128)(2,1)}, bf16[8,16,128,128]{3,2,1,0:T(8,128)(2,1)}, u32[]{:S(2)}, u32[]{:S(2)}) collective-permute-start(bf16[8,16,128,128]{3,2,1,0:T(8,128)(2,1)} %collective-permute-done.15.refs_9_), channel_id=1, source_target_pairs={{0,1},{1,0},{2,3},{3,2},{4,5},{5,4},{6,7},{7,6},{8,9},{9,8},{10,11... | collective-permute-start | bytes 12582920 | tf_op jit(solution)/shard_map/ppermute | solution.py:176
  96.4 35.5 %copy-start.12 = (s32[2,4]{1,0:T(2,128)S(1)}, s32[2,4]{1,0:T(2,128)}, u32[]{:S(2)}) copy-start(s32[2,4]{1,0:T(2,128)} %param.10) | copy-start | bytes 100
  96.4 35.6 %copy-start.11 = (s32[2,4,128]{2,1,0:T(4,128)S(1)}, s32[2,4,128]{2,1,0:T(4,128)}, u32[]{:S(2)}) copy-start(s32[2,4,128]{2,1,0:T(4,128)} %param.9) | copy-start | bytes 12292
  96.4 36.0 %copy-start.10 = (s32[4,128]{1,0:T(4,128)S(1)}, s32[4,128]{1,0:T(4,128)}, u32[]{:S(2)}) copy-start(s32[4,128]{1,0:T(4,128)} %param.8) | copy-start | bytes 6148
  96.4 36.1 %copy-start.13 = (s32[4]{0:T(128)S(1)}, s32[4]{0:T(128)}, u32[]{:S(2)}) copy-start(s32[4]{0:T(128)} %constant.97.clone) | copy-start | bytes 52
  98.9 32.5 %collective-permute-start.17 = (bf16[8,8,128,128]{3,2,1,0:T(8,128)(2,1)S(1)}, bf16[8,8,128,128]{3,2,1,0:T(8,128)(2,1)}, u32[]{:S(2)}, u32[]{:S(2)}) collective-permute-start(bf16[8,8,128,128]{3,2,1,0:T(8,128)(2,1)S(1)} %slice_select_fusion), channel_id=1, source_target_pairs={{0,32},{1,225},{2,34},{3,227},{4,36},{5,229},{6,38},{7,231},{8,40}... | collective-permute-start | bytes 6291464 | tf_op jit(solution)/shard_map/ppermute | solution.py:175
  104.5 31.9 %collective-permute-start.13 = (bf16[4,16,16384]{2,1,0:T(8,128)(2,1)}, bf16[4,16,16384]{2,1,0:T(8,128)(2,1)}, u32[]{:S(2)}, u32[]{:S(2)}) collective-permute-start(bf16[4,16,16384]{2,1,0:T(8,128)(2,1)} %collective-permute-done.9.refs_2_), channel_id=1, source_target_pairs={{0,8},{1,3},{2,10},{3,5},{4,12},{5,7},{6,14},{7,1},{8,16},{9,11},{... | collective-permute-start | bytes 6291464 | tf_op jit(solution)/shard_map/ppermute | solution.py:170
  104.6 31.8 %collective-permute-start.14 = (bf16[4,16,16384]{2,1,0:T(8,128)(2,1)}, bf16[4,16,16384]{2,1,0:T(8,128)(2,1)}, u32[]{:S(2)}, u32[]{:S(2)}) collective-permute-start(bf16[4,16,16384]{2,1,0:T(8,128)(2,1)} %collective-permute-done.12.refs_5_), channel_id=1, source_target_pairs={{0,24},{1,7},{2,26},{3,1},{4,28},{5,3},{6,30},{7,5},{8,0},{9,15},{... | collective-permute-start | bytes 6291464 | tf_op jit(solution)/shard_map/ppermute | solution.py:171
  131.4 24.7 %collective-permute-start.18 = (bf16[8,8,128,128]{3,2,1,0:T(8,128)(2,1)}, bf16[8,8,128,128]{3,2,1,0:T(8,128)(2,1)}, u32[]{:S(2)}, u32[]{:S(2)}) collective-permute-start(bf16[8,8,128,128]{3,2,1,0:T(8,128)(2,1)} %collective-permute-done.17.refs_11_.refs_8_), channel_id=1, source_target_pairs={{0,1},{1,0},{2,3},{3,2},{4,5},{5,4},{6,7},{7,6},{8,9},{9,8},{10,11... | collective-permute-start | bytes 6291464 | tf_op jit(solution)/shard_map/ppermute | solution.py:181
  132.3 3.3 %collective-permute-start = (s32[3,4,128]{2,1,0:T(4,128)S(1)}, s32[3,4,128]{2,1,0:T(4,128)S(1)}, u32[]{:S(2)}, u32[]{:S(2)}) collective-permute-start(s32[3,4,128]{2,1,0:T(4,128)S(1)} %pad_add_fusion), channel_id=1, source_target_pairs={{0,1},{1,0},{2,3},{3,2},{4,5},{5,4},{6,7},{7,6},{8,9},{9,8},{10,11... | collective-permute-start | bytes 18440 | tf_op jit(solution)/shard_map/ppermute | solution.py:126
  136.5 1.6 copy-start.1
  138.1 2.2 %copy-start.3 = (bf16[8,16,128,128]{3,2,1,0:T(8,128)(2,1)S(1)}, bf16[8,16,128,128]{3,2,1,0:T(8,128)(2,1)}, u32[]{:S(2)}) copy-start(bf16[8,16,128,128]{3,2,1,0:T(8,128)(2,1)} %copy-done.2) | copy-start | bytes 12582916
  140.3 1.6 copy-start.6
  141.8 1.6 copy-start.8
  161.9 21.1 %collective-permute-start.20 = (f16[256,512]{1,0:T(8,128)(2,1)S(1)}, f16[256,512]{1,0:T(8,128)(2,1)S(1)}, u32[]{:S(2)}, u32[]{:S(2)}) collective-permute-start(f16[256,512]{1,0:T(8,128)(2,1)S(1)} %convert_bitcast_fusion), channel_id=1, source_target_pairs={{0,128},{1,129},{2,130},{3,131},{4,132},{5,133},{6,134},{7,135},{8... | collective-permute-start | bytes 786440 | tf_op jit(solution)/shard_map/ppermute | solution.py:184
  167.0 6.5 %copy-start.4 = (bf16[8,16,128,128]{3,2,1,0:T(8,128)(2,1)S(1)}, bf16[8,16,128,128]{3,2,1,0:T(8,128)(2,1)}, u32[]{:S(2)}) copy-start(bf16[8,16,128,128]{3,2,1,0:T(8,128)(2,1)} %copy-done.2) | copy-start | bytes 12582916
  173.1 22.2 %collective-permute-start.19 = (f16[256,512]{1,0:T(8,128)(2,1)S(1)}, f16[256,512]{1,0:T(8,128)(2,1)S(1)}, u32[]{:S(2)}, u32[]{:S(2)}) collective-permute-start(f16[256,512]{1,0:T(8,128)(2,1)S(1)} %convert_bitcast_fusion.1), channel_id=1, source_target_pairs={{0,128},{1,129},{2,130},{3,131},{4,132},{5,133},{6,134},{7,135},{8... | collective-permute-start | bytes 786440 | tf_op jit(solution)/shard_map/ppermute | solution.py:186
  183.2 12.2 %collective-permute-start.21 = (bf16[256,512]{1,0:T(8,128)(2,1)S(1)}, bf16[256,512]{1,0:T(8,128)(2,1)S(1)}, u32[]{:S(2)}, u32[]{:S(2)}) collective-permute-start(bf16[256,512]{1,0:T(8,128)(2,1)S(1)} %fusion.1), channel_id=1, source_target_pairs={{0,1},{1,0},{2,3},{3,2},{4,5},{5,4},{6,7},{7,6},{8,9},{9,8},{10,11... | collective-permute-start | bytes 786440 | tf_op jit(solution)/shard_map/ppermute | solution.py:191

commit v3 on v2

--- a/solution.py
+++ b/solution.py
@@ -68,9 +68,11 @@
         out[0] = total
 
 
-def partial_ladder(group, amps, tiles, flips, tail, acc, ordered, place, blocks_in, live, low=0, high=8, light=1):
+def partial_ladder(amps, tiles, flips, tail, acc, ordered, place, blocks_in, live, low=0, high=8, light=1, pin=False):
     rows = 256
     count = sum(x.shape[1] for x in tiles)
+    if pin:
+        amps, tiles = ([pltpu.with_memory_space_constraint(x, pltpu.HBM) for x in xs] for xs in (amps, tiles))
 
     def tile_map(flip, block, *_):
         return (low + block + 4 * flip) % 8, 0, 0, 0
@@ -78,7 +80,7 @@
     def out_map(block, *_):
         return block // 4, 0, block % 4
 
-    specs = [pl.BlockSpec((2, *amps[0].shape[1:]), lambda *_: (group, 0, 0), pipeline_mode=pl.Buffered(1))] * len(amps)
+    specs = [pl.BlockSpec(memory_space=pltpu.VMEM)] * len(amps)
     for x, flip in zip(tiles, flips, strict=True):
         specs.append(pl.BlockSpec((1, *x.shape[1:]), functools.partial(tile_map, flip)))
     if acc is not None:
@@ -110,6 +112,17 @@
     return [lax.ppermute(shard, "tile", moved(phase, step)) for step in steps]
 
 
+def spread(own, before, behind, opposite):
+    fore, aft = jnp.stack([own, before]), jnp.stack([behind, opposite])
+    fore_before = lax.ppermute(fore, "tile", moved(1, 1))
+    aft_behind = lax.ppermute(aft, "tile", moved(1, -1))
+    aft_before = lax.ppermute(aft, "tile", moved(1, 1))
+    fore_behind = lax.ppermute(fore, "tile", moved(1, -1))
+    fore_beyond = lax.ppermute(fore_before, "tile", moved(1, 1))
+    aft_beyond = lax.ppermute(aft_behind, "tile", moved(1, -1))
+    return [fore, aft, fore_before, aft_before, fore_behind, aft_behind, fore_beyond, aft_beyond]
+
+
 def on_device(groups, tiles, amplitudes, integrals, tile_in, tile_list, tile_count):
     pool = tile_in.shape[1]
     me, tile = lax.axis_index("grp"), lax.axis_index("tile")
@@ -124,24 +137,6 @@
     live = jnp.any(listed & within, axis=2).astype(jnp.int32)
     table = jnp.concatenate([tile_in[None], live], axis=0)
     other_table = lax.ppermute(table, "tile", swapped())
-    table = jnp.concatenate([table, other_table], axis=1)
-    table = jnp.roll(table, (2 - me) * 16, axis=2)
-    low_near, high_near, low_half, high_half = (
-        table[..., a:b] for a, b in ((16, 32), (48, 64), (8, 16), (64, 72))
-    )
-    zero = core == 0
-    table = jnp.concatenate(
-        [
-            table[..., 32:48],
-            jnp.where(zero, low_near, high_near),
-            jnp.where(zero, high_near, low_near),
-            jnp.where(zero, low_half, high_half),
-            jnp.where(zero, high_half, low_half),
-        ],
-        axis=2,
-    )
-    blocks_in = table[0].reshape(-1)
-    live = jnp.transpose(table[1:], (1, 2, 0)).reshape(-1).astype(jnp.float32)
     rel = jnp.array(REL, jnp.int32)
     along_1, along_2 = jnp.where(core == 0, x, y), jnp.where(core == 0, y, x)
     step_1, step_2 = jnp.where(core == 0, 1, SIDE), jnp.where(core == 0, SIDE, 1)
@@ -157,36 +152,38 @@
         for t in range(tiles)
     ]
     held = jnp.concatenate([integrals, lax.ppermute(integrals, "tile", swapped())], axis=0)
+    zero = core == 0
+    stays, goes = (jnp.where(zero, held[:, i : i + 8], held[:, 8 - i : 16 - i]) for i in (0, 8))
     own_near = gather(own, 0, (1, -1, 2))
-    held, far, *own_near = lax.optimization_barrier((held, far, *own_near))
-    near = lax.ppermute(held, both, onward)
-    far_near = gather(far, 0, (1, -1, 2))
-    fore = jnp.stack([own, own_near[0], far, far_near[0]])
-    aft = jnp.stack([own_near[1], own_near[2], far_near[1], far_near[2]])
-    fore_before = lax.ppermute(fore, "tile", moved(1, 1))
-    aft_behind = lax.ppermute(aft, "tile", moved(1, -1))
-    aft_before = lax.ppermute(aft, "tile", moved(1, 1))
-    fore_behind = lax.ppermute(fore, "tile", moved(1, -1))
-    fore_beyond = lax.ppermute(fore_before, "tile", moved(1, 1))
-    aft_beyond = lax.ppermute(aft_behind, "tile", moved(1, -1))
-    amps = [fore, aft, fore_before, aft_before, fore_behind, aft_behind, fore_beyond, aft_beyond]
-    near = after(near, fore_before, aft_behind, fore_behind, aft_before)
-    half = jnp.where(zero, near[:, 8:], near[:, :8])
-    half = lax.ppermute(half, both, onward)
-    near_other = lax.ppermute(near, "tile", swapped())
-
+    stays, goes, far, other_table, *own_near = lax.optimization_barrier((stays, goes, far, other_table, *own_near))
+    table = jnp.concatenate([table, other_table], axis=1)
+    table = jnp.roll(table, (2 - me) * 16, axis=2)
+    zero = core == 0
+    parts = [table[..., a : a + 8] for a in range(0, 80, 8)]
+    order = ((4, 5), (5, 4), (2, 7), (3, 6), (7, 2), (6, 3), (1, 8), (8, 1))
+    table = jnp.concatenate([jnp.where(zero, parts[i], parts[j]) for i, j in order], axis=2)
+    blocks_in = table[0].reshape(-1)
+    live = jnp.transpose(table[1:], (1, 2, 0)).reshape(-1).astype(jnp.float32)
+    near_goes = lax.ppermute(goes, both, onward)
+    near_stays = lax.ppermute(stays, both, onward)
+    half = lax.ppermute(near_goes, both, onward)
+    far_amps = spread(far, *gather(far, 0, (1, -1, 2)))
+    near_goes, near_stays, own, *own_near = lax.optimization_barrier(
+        (near_goes, near_stays, own, *own_near, *far_amps)
+    )[:6]
+    own_amps = spread(own, *own_near)
+    others = [lax.ppermute(x, "tile", swapped()) for x in (near_stays, near_goes)]
     facts = (place, blocks_in, live)
-    first, flips, last_flips = [held, near, near_other], (0, 0, 1), (0, 1)
-    back = partial_ladder(1, amps, first, flips, None, None, False, *facts)
-    half_other = lax.ppermute(half, "tile", swapped())
+    first, flips, last_flips = [stays, goes, near_stays, near_goes, *others], (0, 0, 0, 0, 1, 1), (0, 1)
+    back = partial_ladder(far_amps, first, flips, None, None, False, *facts, pin=True)
+    half_other = lax.ppermute(after(half, back, *own_amps[2:6]), "tile", swapped())
     last = [half, half_other]
-    back_1 = partial_ladder(1, amps, last, last_flips, 48, back[1:], True, *facts, low=4)
+    back_1 = partial_ladder(far_amps, last, last_flips, 48, back[1:], True, *facts, low=4)
     back_1 = lax.ppermute(back_1[0].astype(jnp.float16), both, turned(groups, tiles))
-    back_0 = partial_ladder(1, amps, last, last_flips, 48, back[:1], True, *facts, high=4)
+    back_0 = partial_ladder(far_amps, last, last_flips, 48, back[:1], True, *facts, high=4)
     back_0 = lax.ppermute(back_0[0].astype(jnp.float16), both, turned(groups, tiles))
-    every, flips = [*first, *last], (0, 0, 1, 0, 1)
-    here_1 = partial_ladder(0, amps, every, flips, None, None, True, *facts, low=4)[0]
-    here_0 = partial_ladder(0, amps, every, flips, None, None, True, *facts, high=4)[0]
+    every, flips = [*first, *last], (*flips, *last_flips)
+    here_0, here_1 = partial_ladder(own_amps, every, flips, None, None, True, *facts)
 
     other = lax.ppermute((0.5 * (here_1 + back_1.astype(jnp.float32))).astype(jnp.bfloat16), "tile", swapped())
     same = (0.5 * (here_0 + back_0.astype(jnp.float32))).astype(jnp.bfloat16)

time: 197 us -> 172 us (0.87)
  waiting for transfers between devices: 86.7 us -> 40 us
  starting transfers between devices: 47.4 us -> 74.5 us
  local copies, waits for them, and re-layouts: 12.5 us -> 4.62 us
  other arithmetic: 6.08 us -> 9.33 us
    ppermute x10 -> x18, waiting for transfers between devices: 67.3 us -> 33.8 us  [the longest x2 13.9 us: spread(): fore_before = lax.ppermute(fore, 'tile', moved(1, 1))]
    ppermute x1, starting transfers between devices: 0.43 us -> 18.5 us  [on_device(): lax.ppermute(back_0[0].astype(jnp.float16), both, turned(groups, tiles))]
    ppermute x10 -> x18, starting transfers between devices: 25.3 us -> 38.9 us  [the longest x1 8.39 us: on_device(): near_goes = lax.ppermute(goes, both, onward)]
    unnamed x28 -> x25, local copies, waits for them, and re-layouts: 11 us -> 2.86 us
    ppermute x6, waiting for transfers between devices: 6.93 us -> 1.89 us  [gather(): return [lax.ppermute(shard, 'tile', moved(phase, step)) for step in steps]]
    ppermute x1, starting transfers between devices: 5.13 us -> 0.1 us  [on_device(): lax.ppermute(back_1[0].astype(jnp.float16), both, turned(groups, tiles))]
    ppermute x1, waiting for transfers between devices: 7.79 us -> 3.15 us  [on_device(): far = lax.ppermute(own, both, turned(groups, tiles))]
    another operation x2 -> x4, other arithmetic: 0.53 us -> 4.6 us  [spread(): fore, aft = (jnp.stack([own, before]), jnp.stack([behind, opposite]))]
  transfers between devices with their start and end apart: 22 -> 30, of which waited for: 11 -> 10; matrix products, arithmetic and copies ran while one was open for 3% -> 7% of each run, Pallas kernels for 19% -> 24%
where the time goes in v3:
time: 172 us; the launch traced here: 170 us
  starting transfers between devices  74.5 us (43%)
  Pallas kernels  41.5 us (24%)
  waiting for transfers between devices  40 us (23%)
  other arithmetic  9.33 us (5%)
  local copies, waits for them, and re-layouts  4.62 us (3%)
    pallas_call x4, Pallas kernels, partial_ladder(): pl.pallas_call(functools.partial(body, len(amps), low, tail, ordered), ou...  41.5 us
    ppermute x1, starting transfers between devices, on_device(): lax.ppermute(back_0[0].astype(jnp.float16), both, turned(groups, tiles))  18.5 us
    ppermute x2, waiting for transfers between devices, spread(): fore_before = lax.ppermute(fore, 'tile', moved(1, 1))  13.9 us
    ppermute x2, waiting for transfers between devices, spread(): aft_behind = lax.ppermute(aft, 'tile', moved(1, -1))  9.41 us
    ppermute x1, starting transfers between devices, on_device(): near_goes = lax.ppermute(goes, both, onward)  8.39 us
    ppermute x6, starting transfers between devices, gather(): return [lax.ppermute(shard, 'tile', moved(phase, step)) for step in steps]  7.03 us
    ppermute x2, starting transfers between devices, spread(): fore_behind = lax.ppermute(fore, 'tile', moved(1, -1))  6.8 us
    ppermute x1, starting transfers between devices, on_device(): half = lax.ppermute(near_goes, both, onward)  6.69 us
  transfers between devices with their start and end apart: 30, of which 10 were waited for; matrix products, arithmetic and copies ran while one was open for 7% of the time, Pallas kernels for 24%

profile of v3, /device:TPU:1, one launch (start us, length us, event | category | flops | bytes accessed | tf_op | source)
XLA Modules:
  0.0 170.3 jit_solution(17600542288505887110)
XLA Ops:
  0.0 3.2 %collective-permute-start = (bf16[4,16,128,128]{3,2,1,0:T(8,128)(2,1)}, bf16[4,16,128,128]{3,2,1,0:T(8,128)(2,1)S(1)}, u32[]{:S(2)}, u32[]{:S(2)}) collective-permute-start(bf16[4,16,128,128]{3,2,1,0:T(8,128)(2,1)} %param.7), channel_id=1, source_target_pairs={{0,1},{1,0},{2,3},{3,2},{4,5},{5,4},{6,7},{7,6},{8,9},{9,8},{10,11... | collective-permute-start | bytes 6291464 | tf_op jit(solution)/shard_map/ppermute | solution.py:154
  3.2 5.2 %collective-permute-start.1 = (bf16[16,16384]{1,0:T(8,128)(2,1)}, bf16[16,16384]{1,0:T(8,128)(2,1)}, u32[]{:S(2)}, u32[]{:S(2)}) collective-permute-start(bf16[16,16384]{1,0:T(8,128)(2,1)} %bitcast.43), channel_id=1, source_target_pairs={{0,128},{1,129},{2,130},{3,131},{4,132},{5,133},{6,134},{7,135},{8... | collective-permute-start | bytes 1572872 | tf_op jit(solution)/shard_map/ppermute | solution.py:147
  8.4 1.3 collective-permute-start.3
  9.7 1.4 collective-permute-start.4
  11.2 1.6 collective-permute-start.5
  12.8 0.8 iota_compare_fusion.1
  13.5 1.0 fusion.7
  14.6 0.7 pad_add_fusion
  15.3 1.8 %constant_dynamic-update-slice_fusion.1 = bf16[8,16,128,128]{3,2,1,0:T(8,128)(2,1)S(1)} fusion(bf16[4,16,128,128]{3,2,1,0:T(8,128)(2,1)} %param.7), kind=kLoop, calls=%fused_computation.45 | loop fusion | bytes 4194304
  17.1 1.0 collective-permute-start.2
  18.2 0.3 constant_dynamic-update-slice_fusion
  18.4 1.6 broadcast_select_fusion
  20.1 3.1 %collective-permute-done.1 = bf16[16,16384]{1,0:T(8,128)(2,1)} collective-permute-done((bf16[16,16384]{1,0:T(8,128)(2,1)}, bf16[16,16384]{1,0:T(8,128)(2,1)}, u32[]{:S(2)}, u32[]{:S(2)}) %collective-permute-start.1) | collective-permute-done | bytes 524320 | tf_op jit(solution)/shard_map/ppermute | solution.py:147
  23.2 1.9 %collective-permute-done.5 = bf16[16,16384]{1,0:T(8,128)(2,1)} collective-permute-done((bf16[16,16384]{1,0:T(8,128)(2,1)}, bf16[16,16384]{1,0:T(8,128)(2,1)}, u32[]{:S(2)}, u32[]{:S(2)}) %collective-permute-start.5) | collective-permute-done | bytes 524320 | tf_op jit(solution)/shard_map/ppermute | solution.py:112
  25.1 1.5 collective-permute-start.9
  26.6 1.1 collective-permute-start.10
  27.8 8.4 %collective-permute-start.6 = (bf16[8,8,128,128]{3,2,1,0:T(8,128)(2,1)S(1)}, bf16[8,8,128,128]{3,2,1,0:T(8,128)(2,1)}, u32[]{:S(2)}, u32[]{:S(2)}) collective-permute-start(bf16[8,8,128,128]{3,2,1,0:T(8,128)(2,1)S(1)} %get-tuple-element.20.refs_9_), channel_id=1, source_target_pairs={{0,32},{1,225},{2,34},{3,227},{4,36},{5,229},{6,38},{7,231},{8,40}... | collective-permute-start | bytes 6291464 | tf_op jit(solution)/shard_map/ppermute | solution.py:167
  36.2 4.4 %collective-permute-start.7 = (bf16[8,8,128,128]{3,2,1,0:T(8,128)(2,1)}, bf16[8,8,128,128]{3,2,1,0:T(8,128)(2,1)}, u32[]{:S(2)}, u32[]{:S(2)}) collective-permute-start(bf16[8,8,128,128]{3,2,1,0:T(8,128)(2,1)} %get-tuple-element.21.refs_8_), channel_id=1, source_target_pairs={{0,32},{1,225},{2,34},{3,227},{4,36},{5,229},{6,38},{7,231},{8,40}... | collective-permute-start | bytes 6291464 | tf_op jit(solution)/shard_map/ppermute | solution.py:168
  40.6 0.0 copy-start.11
  40.6 0.1 pad_maximum_fusion.1.refs_1_
  40.7 2.6 %collective-permute-start.14 = (bf16[2,16,16384]{2,1,0:T(8,128)(2,1)S(1)}, bf16[2,16,16384]{2,1,0:T(8,128)(2,1)}, u32[]{:S(2)}, u32[]{:S(2)}) collective-permute-start(bf16[2,16,16384]{2,1,0:T(8,128)(2,1)S(1)} %pad_maximum_fusion.1.refs_1_), channel_id=1, source_target_pairs={{0,24},{1,7},{2,26},{3,1},{4,28},{5,3},{6,30},{7,5},{8,0},{9,15},{... | collective-permute-start | bytes 3145736 | tf_op jit(solution)/shard_map/ppermute | solution.py:118
  43.3 2.1 %pad_maximum_fusion.refs_0_ = bf16[2,16,16384]{2,1,0:T(8,128)(2,1)} fusion(bf16[1,16,16384]{2,1,0:T(8,128)(2,1)S(1)} %bitcast.50, bf16[1,16,16384]{2,1,0:T(8,128)(2,1)} %bitcast.3), kind=kLoop, calls=%fused_computation.2 | loop fusion | flops 524288 | bytes 2097152 | tf_op jit(solution)/shard_map/stack | solution.py:116
  45.4 0.2 collective-permute-start.11
  45.6 9.4 %collective-permute-done.14.refs_5_ = bf16[2,16,16384]{2,1,0:T(8,128)(2,1)} collective-permute-done((bf16[2,16,16384]{2,1,0:T(8,128)(2,1)S(1)}, bf16[2,16,16384]{2,1,0:T(8,128)(2,1)}, u32[]{:S(2)}, u32[]{:S(2)}) %collective-permute-start.14) | collective-permute-done | bytes 1048608 | tf_op jit(solution)/shard_map/ppermute | solution.py:118
  55.0 3.5 %collective-permute-start.13 = (bf16[2,16,16384]{2,1,0:T(8,128)(2,1)}, bf16[2,16,16384]{2,1,0:T(8,128)(2,1)}, u32[]{:S(2)}, u32[]{:S(2)}) collective-permute-start(bf16[2,16,16384]{2,1,0:T(8,128)(2,1)} %pad_maximum_fusion.refs_0_), channel_id=1, source_target_pairs={{0,24},{1,7},{2,26},{3,1},{4,28},{5,3},{6,30},{7,5},{8,0},{9,15},{... | collective-permute-start | bytes 3145736 | tf_op jit(solution)/shard_map/ppermute | solution.py:120
  58.5 1.0 copy-done.4
  59.5 0.0 collective-permute-start.16
  59.5 10.2 %collective-permute-done.11.refs_2_ = bf16[2,16,16384]{2,1,0:T(8,128)(2,1)} collective-permute-done((bf16[2,16,16384]{2,1,0:T(8,128)(2,1)}, bf16[2,16,16384]{2,1,0:T(8,128)(2,1)}, u32[]{:S(2)}, u32[]{:S(2)}) %collective-permute-start.11) | collective-permute-done | bytes 1048608 | tf_op jit(solution)/shard_map/ppermute | solution.py:117
  69.8 6.7 %collective-permute-start.25 = (bf16[8,8,128,128]{3,2,1,0:T(8,128)(2,1)}, bf16[8,8,128,128]{3,2,1,0:T(8,128)(2,1)S(1)}, u32[]{:S(2)}, u32[]{:S(2)}) collective-permute-start(bf16[8,8,128,128]{3,2,1,0:T(8,128)(2,1)} %collective-permute-done.6.refs_11_), channel_id=1, source_target_pairs={{0,32},{1,225},{2,34},{3,227},{4,36},{5,229},{6,38},{7,231},{8,40}... | collective-permute-start | bytes 6291464 | tf_op jit(solution)/shard_map/ppermute | solution.py:169
  76.5 6.7 %collective-permute-done.7.refs_10_ = bf16[8,8,128,128]{3,2,1,0:T(8,128)(2,1)} collective-permute-done((bf16[8,8,128,128]{3,2,1,0:T(8,128)(2,1)}, bf16[8,8,128,128]{3,2,1,0:T(8,128)(2,1)}, u32[]{:S(2)}, u32[]{:S(2)}) %collective-permute-start.7) | collective-permute-done | bytes 2097184 | tf_op jit(solution)/shard_map/ppermute | solution.py:168
  83.2 2.0 %collective-permute-done.15.refs_6_ = bf16[2,16,16384]{2,1,0:T(8,128)(2,1)} collective-permute-done((bf16[2,16,16384]{2,1,0:T(8,128)(2,1)}, bf16[2,16,16384]{2,1,0:T(8,128)(2,1)}, u32[]{:S(2)}, u32[]{:S(2)}) %collective-permute-start.15) | collective-permute-done | bytes 1048608 | tf_op jit(solution)/shard_map/ppermute | solution.py:121
  85.2 2.5 %collective-permute-start.23 = (bf16[8,8,128,128]{3,2,1,0:T(8,128)(2,1)}, bf16[8,8,128,128]{3,2,1,0:T(8,128)(2,1)}, u32[]{:S(2)}, u32[]{:S(2)}) collective-permute-start(bf16[8,8,128,128]{3,2,1,0:T(8,128)(2,1)} %collective-permute-done.7.refs_10_), channel_id=1, source_target_pairs={{0,1},{1,0},{2,3},{3,2},{4,5},{5,4},{6,7},{7,6},{8,9},{9,8},{10,11... | collective-permute-start | bytes 6291464 | tf_op jit(solution)/shard_map/ppermute | solution.py:175
  87.7 2.3 %pad_maximum_fusion.3.refs_1_ = bf16[2,16,16384]{2,1,0:T(8,128)(2,1)} fusion(bf16[1,16,16384]{2,1,0:T(8,128)(2,1)} %bitcast.10, bf16[1,16,16384]{2,1,0:T(8,128)(2,1)} %bitcast.49), kind=kLoop, calls=%fused_computation.5 | loop fusion | flops 524288 | bytes 2097152 | tf_op jit(solution)/shard_map/stack | solution.py:116
  90.0 1.3 collective-permute-start.18
  91.4 1.9 %collective-permute-start.20 = (bf16[2,16,16384]{2,1,0:T(8,128)(2,1)}, bf16[2,16,16384]{2,1,0:T(8,128)(2,1)}, u32[]{:S(2)}, u32[]{:S(2)}) collective-permute-start(bf16[2,16,16384]{2,1,0:T(8,128)(2,1)} %pad_maximum_fusion.3.refs_1_), channel_id=1, source_target_pairs={{0,24},{1,7},{2,26},{3,1},{4,28},{5,3},{6,30},{7,5},{8,0},{9,15},{... | collective-permute-start | bytes 3145736 | tf_op jit(solution)/shard_map/ppermute | solution.py:118
  93.3 0.1 pad_maximum_fusion.2.refs_0_
  93.4 0.1 collective-permute-start.17
  93.5 1.3 collective-permute-done.24.refs_13_
  94.9 3.3 %collective-permute-start.19 = (bf16[2,16,16384]{2,1,0:T(8,128)(2,1)S(1)}, bf16[2,16,16384]{2,1,0:T(8,128)(2,1)}, u32[]{:S(2)}, u32[]{:S(2)}) collective-permute-start(bf16[2,16,16384]{2,1,0:T(8,128)(2,1)S(1)} %pad_maximum_fusion.2.refs_0_), channel_id=1, source_target_pairs={{0,24},{1,7},{2,26},{3,1},{4,28},{5,3},{6,30},{7,5},{8,0},{9,15},{... | collective-permute-start | bytes 3145736 | tf_op jit(solution)/shard_map/ppermute | solution.py:120
  98.1 0.1 broadcast_add_fusion
  98.2 0.1 add.75.place
  98.3 0.1 fusion.10
  98.4 0.1 slice_select_fusion
  98.5 0.1 concatenate.23
  98.6 0.1 copy.14
  98.8 0.2 convert_element_type.37.live
  98.9 0.1 reshape_squeeze.3.blocks_in
  99.0 14.6 %shard_map.64 = f32[2,256,512]{2,1,0:T(8,128)S(1)} custom-call(s32[16]{0:T(128)S(1)} %add.75.place, s32[512]{0:T(512)S(1)} %reshape_squeeze.3.blocks_in, f32[1024]{0:T(1024)S(1)} %convert_element_type.37.live, bf16[2,16,16384]{2,1,0:T(8,128)(2,1)} %pad_maximum_fusion.refs_0_, bf16[2,16,16384]{2,1,0:T(8,128)(2,1)} %copy-done.2, ...), custom_call_target="tpu_custom_call" | custom-call | flops 3221225472 | bytes 20971520 | tf_op jit(solution)/shard_map/pallas_call | solution.py:89
  113.7 3.6 %collective-permute-done.17.refs_2_ = bf16[2,16,16384]{2,1,0:T(8,128)(2,1)} collective-permute-done((bf16[2,16,16384]{2,1,0:T(8,128)(2,1)S(1)}, bf16[2,16,16384]{2,1,0:T(8,128)(2,1)}, u32[]{:S(2)}, u32[]{:S(2)}) %collective-permute-start.17) | collective-permute-done | bytes 1048608 | tf_op jit(solution)/shard_map/ppermute | solution.py:117
  117.3 0.8 collective-permute-start.26
  118.1 3.3 %collective-permute-start.22 = (bf16[2,16,16384]{2,1,0:T(8,128)(2,1)}, bf16[2,16,16384]{2,1,0:T(8,128)(2,1)S(1)}, u32[]{:S(2)}, u32[]{:S(2)}) collective-permute-start(bf16[2,16,16384]{2,1,0:T(8,128)(2,1)} %collective-permute-done.20.refs_5_), channel_id=1, source_target_pairs={{0,24},{1,7},{2,26},{3,1},{4,28},{5,3},{6,30},{7,5},{8,0},{9,15},{... | collective-permute-start | bytes 3145736 | tf_op jit(solution)/shard_map/ppermute | solution.py:122
  121.4 0.1 fusion.18
  121.4 0.4 collective-permute-done.26.refs_15_.refs_9_
  121.9 5.6 %shard_map.66 = f32[1,256,512]{2,1,0:T(8,128)S(1)} custom-call(s32[16]{0:T(128)S(1)} %add.75.place, s32[512]{0:T(512)S(1)} %reshape_squeeze.3.blocks_in, f32[1024]{0:T(1024)S(1)} %convert_element_type.37.live, bf16[2,16,16384]{2,1,0:T(8,128)(2,1)} %pad_maximum_fusion.refs_0_, bf16[2,16,16384]{2,1,0:T(8,128)(2,1)S(1)} %copy-done.3, ...), custom_call_target="tpu_custom_call" | custom-call | flops 536870912 | bytes 10485760 | tf_op jit(solution)/shard_map/pallas_call | solution.py:89
  127.5 18.5 %collective-permute-start.27 = (f16[256,512]{1,0:T(8,128)(2,1)S(1)}, f16[256,512]{1,0:T(8,128)(2,1)S(1)}, u32[]{:S(2)}, u32[]{:S(2)}) collective-permute-start(f16[256,512]{1,0:T(8,128)(2,1)S(1)} %convert_bitcast_fusion.1), channel_id=1, source_target_pairs={{0,128},{1,129},{2,130},{3,131},{4,132},{5,133},{6,134},{7,135},{8... | collective-permute-start | bytes 786440 | tf_op jit(solution)/shard_map/ppermute | solution.py:184
  146.0 5.6 %shard_map.67 = f32[1,256,512]{2,1,0:T(8,128)S(1)} custom-call(s32[16]{0:T(128)S(1)} %add.75.place, s32[512]{0:T(512)S(1)} %reshape_squeeze.3.blocks_in, f32[1024]{0:T(1024)S(1)} %convert_element_type.37.live, bf16[2,16,16384]{2,1,0:T(8,128)(2,1)} %pad_maximum_fusion.refs_0_, bf16[2,16,16384]{2,1,0:T(8,128)(2,1)S(1)} %copy-done.3, ...), custom_call_target="tpu_custom_call" | custom-call | flops 536870912 | bytes 10485760 | tf_op jit(solution)/shard_map/pallas_call | solution.py:89
  151.6 0.1 collective-permute-start.28
  151.7 15.7 %shard_map.65 = f32[2,256,512]{2,1,0:T(8,128)S(1)} custom-call(s32[16]{0:T(128)S(1)} %add.75.place, s32[512]{0:T(512)S(1)} %reshape_squeeze.3.blocks_in, f32[1024]{0:T(1024)S(1)} %convert_element_type.37.live, bf16[2,16,16384]{2,1,0:T(8,128)(2,1)S(1)} %pad_maximum_fusion.2.refs_0_, bf16[2,16,16384]{2,1,0:T(8,128)(2,1)} %pad_maximum_fusion.3.refs_1_, ...), custom_call_target="tpu_custom_call" | custom-call | flops 4294967296 | bytes 25165824 | tf_op jit(solution)/shard_map/pallas_call | solution.py:89
  167.5 0.1 fusion.2
  167.6 0.5 collective-permute-start.29
  168.1 1.2 collective-permute-done.29
  169.3 0.1 broadcast_select_fusion.3
  169.4 0.1 maximum_bitcast_fusion
  169.5 0.9 copy.15
  (53 shorter events, 0.2 us)
Async XLA Ops:
  0.0 17.1 %collective-permute-start = (bf16[4,16,128,128]{3,2,1,0:T(8,128)(2,1)}, bf16[4,16,128,128]{3,2,1,0:T(8,128)(2,1)S(1)}, u32[]{:S(2)}, u32[]{:S(2)}) collective-permute-start(bf16[4,16,128,128]{3,2,1,0:T(8,128)(2,1)} %param.7), channel_id=1, source_target_pairs={{0,1},{1,0},{2,3},{3,2},{4,5},{5,4},{6,7},{7,6},{8,9},{9,8},{10,11... | collective-permute-start | bytes 6291464 | tf_op jit(solution)/shard_map/ppermute | solution.py:154
  3.2 20.0 %collective-permute-start.1 = (bf16[16,16384]{1,0:T(8,128)(2,1)}, bf16[16,16384]{1,0:T(8,128)(2,1)}, u32[]{:S(2)}, u32[]{:S(2)}) collective-permute-start(bf16[16,16384]{1,0:T(8,128)(2,1)} %bitcast.43), channel_id=1, source_target_pairs={{0,128},{1,129},{2,130},{3,131},{4,132},{5,133},{6,134},{7,135},{8... | collective-permute-start | bytes 1572872 | tf_op jit(solution)/shard_map/ppermute | solution.py:147
  8.4 14.8 %collective-permute-start.3 = (bf16[16,16384]{1,0:T(8,128)(2,1)}, bf16[16,16384]{1,0:T(8,128)(2,1)S(1)}, u32[]{:S(2)}, u32[]{:S(2)}) collective-permute-start(bf16[16,16384]{1,0:T(8,128)(2,1)} %bitcast.44), channel_id=1, source_target_pairs={{0,2},{1,9},{2,4},{3,11},{4,6},{5,13},{6,0},{7,15},{8,10},{9,17},{... | collective-permute-start | bytes 1572872 | tf_op jit(solution)/shard_map/ppermute | solution.py:112
  9.7 13.5 %collective-permute-start.4 = (bf16[16,16384]{1,0:T(8,128)(2,1)}, bf16[16,16384]{1,0:T(8,128)(2,1)S(1)}, u32[]{:S(2)}, u32[]{:S(2)}) collective-permute-start(bf16[16,16384]{1,0:T(8,128)(2,1)} %bitcast.45), channel_id=1, source_target_pairs={{0,6},{1,25},{2,0},{3,27},{4,2},{5,29},{6,4},{7,31},{8,14},{9,1},{... | collective-permute-start | bytes 1572872 | tf_op jit(solution)/shard_map/ppermute | solution.py:112
  11.2 14.0 %collective-permute-start.5 = (bf16[16,16384]{1,0:T(8,128)(2,1)}, bf16[16,16384]{1,0:T(8,128)(2,1)}, u32[]{:S(2)}, u32[]{:S(2)}) collective-permute-start(bf16[16,16384]{1,0:T(8,128)(2,1)} %bitcast.46), channel_id=1, source_target_pairs={{0,4},{1,17},{2,6},{3,19},{4,0},{5,21},{6,2},{7,23},{8,12},{9,25},... | collective-permute-start | bytes 1572872 | tf_op jit(solution)/shard_map/ppermute | solution.py:112
  17.1 3.0 %collective-permute-start.2 = (s32[3,4,128]{2,1,0:T(4,128)S(1)}, s32[3,4,128]{2,1,0:T(4,128)S(1)}, u32[]{:S(2)}, u32[]{:S(2)}) collective-permute-start(s32[3,4,128]{2,1,0:T(4,128)S(1)} %pad_add_fusion), channel_id=1, source_target_pairs={{0,1},{1,0},{2,3},{3,2},{4,5},{5,4},{6,7},{7,6},{8,9},{9,8},{10,11... | collective-permute-start | bytes 18440 | tf_op jit(solution)/shard_map/ppermute | solution.py:139
  20.1 25.3 %copy-start = (bf16[8,8,128,128]{3,2,1,0:T(8,128)(2,1)}, bf16[8,8,128,128]{3,2,1,0:T(8,128)(2,1)S(1)}, u32[]{:S(2)}) copy-start(bf16[8,8,128,128]{3,2,1,0:T(8,128)(2,1)S(1)} %get-tuple-element.20.refs_9_) | copy-start | bytes 6291460
  23.2 17.3 %copy-start.7 = (bf16[16,16384]{1,0:T(8,128)(2,1)}, bf16[16,16384]{1,0:T(8,128)(2,1)S(1)}, u32[]{:S(2)}) copy-start(bf16[16,16384]{1,0:T(8,128)(2,1)S(1)} %collective-permute-done.3) | copy-start | bytes 1572868
  23.2 17.3 %copy-start.9 = (bf16[16,16384]{1,0:T(8,128)(2,1)}, bf16[16,16384]{1,0:T(8,128)(2,1)S(1)}, u32[]{:S(2)}) copy-start(bf16[16,16384]{1,0:T(8,128)(2,1)S(1)} %collective-permute-done.4) | copy-start | bytes 1572868
  25.1 15.4 %collective-permute-start.9 = (bf16[16,16384]{1,0:T(8,128)(2,1)}, bf16[16,16384]{1,0:T(8,128)(2,1)S(1)}, u32[]{:S(2)}, u32[]{:S(2)}) collective-permute-start(bf16[16,16384]{1,0:T(8,128)(2,1)} %collective-permute-done.1), channel_id=1, source_target_pairs={{0,6},{1,25},{2,0},{3,27},{4,2},{5,29},{6,4},{7,31},{8,14},{9,1},{... | collective-permute-start | bytes 1572872 | tf_op jit(solution)/shard_map/ppermute | solution.py:112
  26.6 13.9 %collective-permute-start.10 = (bf16[16,16384]{1,0:T(8,128)(2,1)}, bf16[16,16384]{1,0:T(8,128)(2,1)S(1)}, u32[]{:S(2)}, u32[]{:S(2)}) collective-permute-start(bf16[16,16384]{1,0:T(8,128)(2,1)} %collective-permute-done.1), channel_id=1, source_target_pairs={{0,4},{1,17},{2,6},{3,19},{4,0},{5,21},{6,2},{7,23},{8,12},{9,25},... | collective-permute-start | bytes 1572872 | tf_op jit(solution)/shard_map/ppermute | solution.py:112
  27.8 15.5 %collective-permute-start.8 = (bf16[16,16384]{1,0:T(8,128)(2,1)}, bf16[16,16384]{1,0:T(8,128)(2,1)S(1)}, u32[]{:S(2)}, u32[]{:S(2)}) collective-permute-start(bf16[16,16384]{1,0:T(8,128)(2,1)} %collective-permute-done.1), channel_id=1, source_target_pairs={{0,2},{1,9},{2,4},{3,11},{4,6},{5,13},{6,0},{7,15},{8,10},{9,17},{... | collective-permute-start | bytes 1572872 | tf_op jit(solution)/shard_map/ppermute | solution.py:112
  27.8 42.0 %collective-permute-start.6 = (bf16[8,8,128,128]{3,2,1,0:T(8,128)(2,1)S(1)}, bf16[8,8,128,128]{3,2,1,0:T(8,128)(2,1)}, u32[]{:S(2)}, u32[]{:S(2)}) collective-permute-start(bf16[8,8,128,128]{3,2,1,0:T(8,128)(2,1)S(1)} %get-tuple-element.20.refs_9_), channel_id=1, source_target_pairs={{0,32},{1,225},{2,34},{3,227},{4,36},{5,229},{6,38},{7,231},{8,40}... | collective-permute-start | bytes 6291464 | tf_op jit(solution)/shard_map/ppermute | solution.py:167
  36.2 47.0 %collective-permute-start.7 = (bf16[8,8,128,128]{3,2,1,0:T(8,128)(2,1)}, bf16[8,8,128,128]{3,2,1,0:T(8,128)(2,1)}, u32[]{:S(2)}, u32[]{:S(2)}) collective-permute-start(bf16[8,8,128,128]{3,2,1,0:T(8,128)(2,1)} %get-tuple-element.21.refs_8_), channel_id=1, source_target_pairs={{0,32},{1,225},{2,34},{3,227},{4,36},{5,229},{6,38},{7,231},{8,40}... | collective-permute-start | bytes 6291464 | tf_op jit(solution)/shard_map/ppermute | solution.py:168
  40.6 29.2 %copy-start.11 = (s32[4]{0:T(128)S(1)}, s32[4]{0:T(128)}, u32[]{:S(2)}) copy-start(s32[4]{0:T(128)} %constant.97.clone) | copy-start | bytes 52
  40.7 49.3 %copy-start.2 = (bf16[2,16,16384]{2,1,0:T(8,128)(2,1)}, bf16[2,16,16384]{2,1,0:T(8,128)(2,1)S(1)}, u32[]{:S(2)}) copy-start(bf16[2,16,16384]{2,1,0:T(8,128)(2,1)S(1)} %pad_maximum_fusion.1.refs_1_) | copy-start | bytes 3145732
  40.7 14.3 %collective-permute-start.14 = (bf16[2,16,16384]{2,1,0:T(8,128)(2,1)S(1)}, bf16[2,16,16384]{2,1,0:T(8,128)(2,1)}, u32[]{:S(2)}, u32[]{:S(2)}) collective-permute-start(bf16[2,16,16384]{2,1,0:T(8,128)(2,1)S(1)} %pad_maximum_fusion.1.refs_1_), channel_id=1, source_target_pairs={{0,24},{1,7},{2,26},{3,1},{4,28},{5,3},{6,30},{7,5},{8,0},{9,15},{... | collective-permute-start | bytes 3145736 | tf_op jit(solution)/shard_map/ppermute | solution.py:118
  43.3 15.3 %collective-permute-start.12 = (bf16[2,16,16384]{2,1,0:T(8,128)(2,1)S(1)}, bf16[2,16,16384]{2,1,0:T(8,128)(2,1)S(1)}, u32[]{:S(2)}, u32[]{:S(2)}) collective-permute-start(bf16[2,16,16384]{2,1,0:T(8,128)(2,1)S(1)} %pad_maximum_fusion.1.refs_1_), channel_id=1, source_target_pairs={{0,8},{1,3},{2,10},{3,5},{4,12},{5,7},{6,14},{7,1},{8,16},{9,11},{... | collective-permute-start | bytes 3145736 | tf_op jit(solution)/shard_map/ppermute | solution.py:119
  45.4 24.4 %collective-permute-start.11 = (bf16[2,16,16384]{2,1,0:T(8,128)(2,1)}, bf16[2,16,16384]{2,1,0:T(8,128)(2,1)}, u32[]{:S(2)}, u32[]{:S(2)}) collective-permute-start(bf16[2,16,16384]{2,1,0:T(8,128)(2,1)} %pad_maximum_fusion.refs_0_), channel_id=1, source_target_pairs={{0,8},{1,3},{2,10},{3,5},{4,12},{5,7},{6,14},{7,1},{8,16},{9,11},{... | collective-permute-start | bytes 3145736 | tf_op jit(solution)/shard_map/ppermute | solution.py:117
  55.0 21.5 %collective-permute-start.13 = (bf16[2,16,16384]{2,1,0:T(8,128)(2,1)}, bf16[2,16,16384]{2,1,0:T(8,128)(2,1)}, u32[]{:S(2)}, u32[]{:S(2)}) collective-permute-start(bf16[2,16,16384]{2,1,0:T(8,128)(2,1)} %pad_maximum_fusion.refs_0_), channel_id=1, source_target_pairs={{0,24},{1,7},{2,26},{3,1},{4,28},{5,3},{6,30},{7,5},{8,0},{9,15},{... | collective-permute-start | bytes 3145736 | tf_op jit(solution)/shard_map/ppermute | solution.py:120
  58.5 1.0 copy-start.4
  59.5 23.7 %collective-permute-start.16 = (bf16[2,16,16384]{2,1,0:T(8,128)(2,1)}, bf16[2,16,16384]{2,1,0:T(8,128)(2,1)}, u32[]{:S(2)}, u32[]{:S(2)}) collective-permute-start(bf16[2,16,16384]{2,1,0:T(8,128)(2,1)} %collective-permute-done.14.refs_5_), channel_id=1, source_target_pairs={{0,24},{1,7},{2,26},{3,1},{4,28},{5,3},{6,30},{7,5},{8,0},{9,15},{... | collective-permute-start | bytes 3145736 | tf_op jit(solution)/shard_map/ppermute | solution.py:122
  69.8 15.5 %collective-permute-start.15 = (bf16[2,16,16384]{2,1,0:T(8,128)(2,1)}, bf16[2,16,16384]{2,1,0:T(8,128)(2,1)}, u32[]{:S(2)}, u32[]{:S(2)}) collective-permute-start(bf16[2,16,16384]{2,1,0:T(8,128)(2,1)} %collective-permute-done.11.refs_2_), channel_id=1, source_target_pairs={{0,8},{1,3},{2,10},{3,5},{4,12},{5,7},{6,14},{7,1},{8,16},{9,11},{... | collective-permute-start | bytes 3145736 | tf_op jit(solution)/shard_map/ppermute | solution.py:121
  69.8 23.5 %copy-start.6 = (bf16[2,8,16384]{2,1,0:T(8,128)(2,1)S(1)}, bf16[2,8,16384]{2,1,0:T(8,128)(2,1)}, u32[]{:S(2)}) copy-start(bf16[2,8,16384]{2,1,0:T(8,128)(2,1)} %param.6) | copy-start | bytes 1572868
  69.8 23.5 %copy-start.8 = (bf16[16,16384]{1,0:T(8,128)(2,1)S(1)}, bf16[16,16384]{1,0:T(8,128)(2,1)}, u32[]{:S(2)}) copy-start(bf16[16,16384]{1,0:T(8,128)(2,1)} %copy-done.7) | copy-start | bytes 1572868
  69.8 47.5 %collective-permute-start.25 = (bf16[8,8,128,128]{3,2,1,0:T(8,128)(2,1)}, bf16[8,8,128,128]{3,2,1,0:T(8,128)(2,1)S(1)}, u32[]{:S(2)}, u32[]{:S(2)}) collective-permute-start(bf16[8,8,128,128]{3,2,1,0:T(8,128)(2,1)} %collective-permute-done.6.refs_11_), channel_id=1, source_target_pairs={{0,32},{1,225},{2,34},{3,227},{4,36},{5,229},{6,38},{7,231},{8,40}... | collective-permute-start | bytes 6291464 | tf_op jit(solution)/shard_map/ppermute | solution.py:169
  85.2 8.2 %collective-permute-start.23 = (bf16[8,8,128,128]{3,2,1,0:T(8,128)(2,1)}, bf16[8,8,128,128]{3,2,1,0:T(8,128)(2,1)}, u32[]{:S(2)}, u32[]{:S(2)}) collective-permute-start(bf16[8,8,128,128]{3,2,1,0:T(8,128)(2,1)} %collective-permute-done.7.refs_10_), channel_id=1, source_target_pairs={{0,1},{1,0},{2,3},{3,2},{4,5},{5,4},{6,7},{7,6},{8,9},{9,8},{10,11... | collective-permute-start | bytes 6291464 | tf_op jit(solution)/shard_map/ppermute | solution.py:175
  87.7 7.1 %collective-permute-start.24 = (bf16[8,8,128,128]{3,2,1,0:T(8,128)(2,1)}, bf16[8,8,128,128]{3,2,1,0:T(8,128)(2,1)}, u32[]{:S(2)}, u32[]{:S(2)}) collective-permute-start(bf16[8,8,128,128]{3,2,1,0:T(8,128)(2,1)} %collective-permute-done.6.refs_11_), channel_id=1, source_target_pairs={{0,1},{1,0},{2,3},{3,2},{4,5},{5,4},{6,7},{7,6},{8,9},{9,8},{10,11... | collective-permute-start | bytes 6291464 | tf_op jit(solution)/shard_map/ppermute | solution.py:175
  87.7 10.6 %copy-start.10 = (s32[4,128]{1,0:T(4,128)S(1)}, s32[4,128]{1,0:T(4,128)}, u32[]{:S(2)}) copy-start(s32[4,128]{1,0:T(4,128)} %param.8) | copy-start | bytes 6148
  90.0 23.7 %collective-permute-start.18 = (bf16[2,16,16384]{2,1,0:T(8,128)(2,1)}, bf16[2,16,16384]{2,1,0:T(8,128)(2,1)}, u32[]{:S(2)}, u32[]{:S(2)}) collective-permute-start(bf16[2,16,16384]{2,1,0:T(8,128)(2,1)} %pad_maximum_fusion.3.refs_1_), channel_id=1, source_target_pairs={{0,8},{1,3},{2,10},{3,5},{4,12},{5,7},{6,14},{7,1},{8,16},{9,11},{... | collective-permute-start | bytes 3145736 | tf_op jit(solution)/shard_map/ppermute | solution.py:119
  91.4 22.3 %collective-permute-start.20 = (bf16[2,16,16384]{2,1,0:T(8,128)(2,1)}, bf16[2,16,16384]{2,1,0:T(8,128)(2,1)}, u32[]{:S(2)}, u32[]{:S(2)}) collective-permute-start(bf16[2,16,16384]{2,1,0:T(8,128)(2,1)} %pad_maximum_fusion.3.refs_1_), channel_id=1, source_target_pairs={{0,24},{1,7},{2,26},{3,1},{4,28},{5,3},{6,30},{7,5},{8,0},{9,15},{... | collective-permute-start | bytes 3145736 | tf_op jit(solution)/shard_map/ppermute | solution.py:118
  93.4 23.9 %collective-permute-start.17 = (bf16[2,16,16384]{2,1,0:T(8,128)(2,1)S(1)}, bf16[2,16,16384]{2,1,0:T(8,128)(2,1)}, u32[]{:S(2)}, u32[]{:S(2)}) collective-permute-start(bf16[2,16,16384]{2,1,0:T(8,128)(2,1)S(1)} %pad_maximum_fusion.2.refs_0_), channel_id=1, source_target_pairs={{0,8},{1,3},{2,10},{3,5},{4,12},{5,7},{6,14},{7,1},{8,16},{9,11},{... | collective-permute-start | bytes 3145736 | tf_op jit(solution)/shard_map/ppermute | solution.py:117
  94.9 22.5 %collective-permute-start.19 = (bf16[2,16,16384]{2,1,0:T(8,128)(2,1)S(1)}, bf16[2,16,16384]{2,1,0:T(8,128)(2,1)}, u32[]{:S(2)}, u32[]{:S(2)}) collective-permute-start(bf16[2,16,16384]{2,1,0:T(8,128)(2,1)S(1)} %pad_maximum_fusion.2.refs_0_), channel_id=1, source_target_pairs={{0,24},{1,7},{2,26},{3,1},{4,28},{5,3},{6,30},{7,5},{8,0},{9,15},{... | collective-permute-start | bytes 3145736 | tf_op jit(solution)/shard_map/ppermute | solution.py:120
  113.7 8.2 %copy-start.3 = (bf16[2,16,16384]{2,1,0:T(8,128)(2,1)S(1)}, bf16[2,16,16384]{2,1,0:T(8,128)(2,1)}, u32[]{:S(2)}) copy-start(bf16[2,16,16384]{2,1,0:T(8,128)(2,1)} %copy-done.2) | copy-start | bytes 3145732
  113.7 8.2 %copy-start.5 = (bf16[2,16,16384]{2,1,0:T(8,128)(2,1)S(1)}, bf16[2,16,16384]{2,1,0:T(8,128)(2,1)}, u32[]{:S(2)}) copy-start(bf16[2,16,16384]{2,1,0:T(8,128)(2,1)} %copy-done.4) | copy-start | bytes 3145732
  117.3 4.5 %collective-permute-start.26 = (bf16[8,8,128,128]{3,2,1,0:T(8,128)(2,1)S(1)}, bf16[8,8,128,128]{3,2,1,0:T(8,128)(2,1)S(1)}, u32[]{:S(2)}, u32[]{:S(2)}) collective-permute-start(bf16[8,8,128,128]{3,2,1,0:T(8,128)(2,1)S(1)} %collective-permute-done.25.refs_14_.refs_8_), channel_id=1, source_target_pairs={{0,1},{1,0},{2,3},{3,2},{4,5},{5,4},{6,7},{7,6},{8,9},{9,8},{10,11... | collective-permute-start | bytes 6291464 | tf_op jit(solution)/shard_map/ppermute | solution.py:179
  118.1 33.6 %collective-permute-start.22 = (bf16[2,16,16384]{2,1,0:T(8,128)(2,1)}, bf16[2,16,16384]{2,1,0:T(8,128)(2,1)S(1)}, u32[]{:S(2)}, u32[]{:S(2)}) collective-permute-start(bf16[2,16,16384]{2,1,0:T(8,128)(2,1)} %collective-permute-done.20.refs_5_), channel_id=1, source_target_pairs={{0,24},{1,7},{2,26},{3,1},{4,28},{5,3},{6,30},{7,5},{8,0},{9,15},{... | collective-permute-start | bytes 3145736 | tf_op jit(solution)/shard_map/ppermute | solution.py:122
  121.4 30.3 %collective-permute-start.21 = (bf16[2,16,16384]{2,1,0:T(8,128)(2,1)}, bf16[2,16,16384]{2,1,0:T(8,128)(2,1)S(1)}, u32[]{:S(2)}, u32[]{:S(2)}) collective-permute-start(bf16[2,16,16384]{2,1,0:T(8,128)(2,1)} %collective-permute-done.17.refs_2_), channel_id=1, source_target_pairs={{0,8},{1,3},{2,10},{3,5},{4,12},{5,7},{6,14},{7,1},{8,16},{9,11},{... | collective-permute-start | bytes 3145736 | tf_op jit(solution)/shard_map/ppermute | solution.py:121
  127.5 40.6 %collective-permute-start.27 = (f16[256,512]{1,0:T(8,128)(2,1)S(1)}, f16[256,512]{1,0:T(8,128)(2,1)S(1)}, u32[]{:S(2)}, u32[]{:S(2)}) collective-permute-start(f16[256,512]{1,0:T(8,128)(2,1)S(1)} %convert_bitcast_fusion.1), channel_id=1, source_target_pairs={{0,128},{1,129},{2,130},{3,131},{4,132},{5,133},{6,134},{7,135},{8... | collective-permute-start | bytes 786440 | tf_op jit(solution)/shard_map/ppermute | solution.py:184
  146.0 5.8 %copy-start.1 = (bf16[8,8,128,128]{3,2,1,0:T(8,128)(2,1)S(1)}, bf16[8,8,128,128]{3,2,1,0:T(8,128)(2,1)}, u32[]{:S(2)}) copy-start(bf16[8,8,128,128]{3,2,1,0:T(8,128)(2,1)} %copy-done) | copy-start | bytes 6291460
  151.6 15.9 %collective-permute-start.28 = (f16[256,512]{1,0:T(8,128)(2,1)S(1)}, f16[256,512]{1,0:T(8,128)(2,1)S(1)}, u32[]{:S(2)}, u32[]{:S(2)}) collective-permute-start(f16[256,512]{1,0:T(8,128)(2,1)S(1)} %convert_bitcast_fusion), channel_id=1, source_target_pairs={{0,128},{1,129},{2,130},{3,131},{4,132},{5,133},{6,134},{7,135},{8... | collective-permute-start | bytes 786440 | tf_op jit(solution)/shard_map/ppermute | solution.py:182
  167.6 1.7 collective-permute-start.29

commit v4 on v3

--- a/solution.py
+++ b/solution.py
@@ -169,7 +169,7 @@
     half = lax.ppermute(near_goes, both, onward)
     far_amps = spread(far, *gather(far, 0, (1, -1, 2)))
     near_goes, near_stays, own, *own_near = lax.optimization_barrier(
-        (near_goes, near_stays, own, *own_near, *far_amps)
+        (near_goes, near_stays, own, *own_near, *far_amps[:6])
     )[:6]
     own_amps = spread(own, *own_near)
     others = [lax.ppermute(x, "tile", swapped()) for x in (near_stays, near_goes)]
@@ -178,10 +178,9 @@
     back = partial_ladder(far_amps, first, flips, None, None, False, *facts, pin=True)
     half_other = lax.ppermute(after(half, back, *own_amps[2:6]), "tile", swapped())
     last = [half, half_other]
-    back_1 = partial_ladder(far_amps, last, last_flips, 48, back[1:], True, *facts, low=4)
-    back_1 = lax.ppermute(back_1[0].astype(jnp.float16), both, turned(groups, tiles))
-    back_0 = partial_ladder(far_amps, last, last_flips, 48, back[:1], True, *facts, high=4)
-    back_0 = lax.ppermute(back_0[0].astype(jnp.float16), both, turned(groups, tiles))
+    back = partial_ladder(far_amps, last, last_flips, 48, back, True, *facts).astype(jnp.float16)
+    back_1 = lax.ppermute(back[1], both, turned(groups, tiles))
+    back_0 = lax.ppermute(back[0], both, turned(groups, tiles))
     every, flips = [*first, *last], (*flips, *last_flips)
     here_0, here_1 = partial_ladder(own_amps, every, flips, None, None, True, *facts)
 

time: 172 us -> 167 us (0.971)
  starting transfers between devices: 74.5 us -> 58.7 us
  waiting for transfers between devices: 40 us -> 52.6 us
  Pallas kernels: 41.5 us -> 39 us
    ppermute x2, waiting for transfers between devices: 0.01 us -> 10.4 us  [spread(): aft_before = lax.ppermute(aft, 'tile', moved(1, 1))]
    ppermute x2, waiting for transfers between devices: 9.41 us -> 0.01 us  [spread(): aft_behind = lax.ppermute(aft, 'tile', moved(1, -1))]
    ppermute x2, starting transfers between devices: 18.6 us -> 10.9 us  [the longest x1 10.6 us: on_device(): back_1 = lax.ppermute(back[1], both, turned(groups, tiles))]
    ppermute x2, waiting for transfers between devices: 0.01 us -> 5.57 us  [the longest x1 3.54 us: on_device(): back_0 = lax.ppermute(back[0], both, turned(groups, tiles))]
    ppermute x1, waiting for transfers between devices: 6.67 us -> 11.9 us  [on_device(): near_stays = lax.ppermute(stays, both, onward)]
    ppermute x2, waiting for transfers between devices: 0.01 us -> 4.31 us  [spread(): fore_behind = lax.ppermute(fore, 'tile', moved(1, -1))]
    ppermute x2, starting transfers between devices: 6.8 us -> 3.71 us  [spread(): fore_behind = lax.ppermute(fore, 'tile', moved(1, -1))]
    ppermute x1, starting transfers between devices: 6.69 us -> 4.2 us  [on_device(): half = lax.ppermute(near_goes, both, onward)]
  transfers between devices with their start and end apart: 30 -> 30, of which waited for: 10 -> 11; matrix products, arithmetic and copies ran while one was open for 7% -> 7% of each run, Pallas kernels for 24% -> 24%
where the time goes in v4:
time: 167 us; the launch traced here: 165 us
  starting transfers between devices  58.7 us (35%)
  waiting for transfers between devices  52.6 us (31%)
  Pallas kernels  39 us (23%)
  other arithmetic  9.39 us (6%)
  local copies, waits for them, and re-layouts  4.66 us (3%)
    pallas_call x3, Pallas kernels, partial_ladder(): pl.pallas_call(functools.partial(body, len(amps), low, tail, ordered), ou...  39 us
    ppermute x2, waiting for transfers between devices, spread(): fore_before = lax.ppermute(fore, 'tile', moved(1, 1))  13.3 us
    ppermute x1, waiting for transfers between devices, on_device(): near_stays = lax.ppermute(stays, both, onward)  11.9 us
    ppermute x1, starting transfers between devices, on_device(): back_1 = lax.ppermute(back[1], both, turned(groups, tiles))  10.6 us
    ppermute x2, waiting for transfers between devices, spread(): aft_before = lax.ppermute(aft, 'tile', moved(1, 1))  10.4 us
    ppermute x1, starting transfers between devices, on_device(): near_goes = lax.ppermute(goes, both, onward)  8.38 us
    ppermute x6, starting transfers between devices, gather(): return [lax.ppermute(shard, 'tile', moved(phase, step)) for step in steps]  7.03 us
    ppermute x1, starting transfers between devices, on_device(): far = lax.ppermute(own, both, turned(groups, tiles))  5.17 us
  transfers between devices with their start and end apart: 30, of which 11 were waited for; matrix products, arithmetic and copies ran while one was open for 7% of the time, Pallas kernels for 24%

profile of v4, /device:TPU:1, one launch (start us, length us, event | category | flops | bytes accessed | tf_op | source)
XLA Modules:
  0.0 164.6 jit_solution(3094022611646460378)
XLA Ops:
  0.0 3.2 %collective-permute-start = (bf16[4,16,128,128]{3,2,1,0:T(8,128)(2,1)}, bf16[4,16,128,128]{3,2,1,0:T(8,128)(2,1)S(1)}, u32[]{:S(2)}, u32[]{:S(2)}) collective-permute-start(bf16[4,16,128,128]{3,2,1,0:T(8,128)(2,1)} %param.7), channel_id=1, source_target_pairs={{0,1},{1,0},{2,3},{3,2},{4,5},{5,4},{6,7},{7,6},{8,9},{9,8},{10,11... | collective-permute-start | bytes 6291464 | tf_op jit(solution)/shard_map/ppermute | solution.py:154
  3.2 5.2 %collective-permute-start.1 = (bf16[16,16384]{1,0:T(8,128)(2,1)}, bf16[16,16384]{1,0:T(8,128)(2,1)}, u32[]{:S(2)}, u32[]{:S(2)}) collective-permute-start(bf16[16,16384]{1,0:T(8,128)(2,1)} %bitcast.43), channel_id=1, source_target_pairs={{0,128},{1,129},{2,130},{3,131},{4,132},{5,133},{6,134},{7,135},{8... | collective-permute-start | bytes 1572872 | tf_op jit(solution)/shard_map/ppermute | solution.py:147
  8.4 1.3 collective-permute-start.3
  9.7 1.4 collective-permute-start.4
  11.2 1.6 collective-permute-start.5
  12.8 0.8 iota_compare_fusion.1
  13.5 1.0 fusion.7
  14.6 0.7 pad_add_fusion
  15.3 1.8 %constant_dynamic-update-slice_fusion.1 = bf16[8,16,128,128]{3,2,1,0:T(8,128)(2,1)S(1)} fusion(bf16[4,16,128,128]{3,2,1,0:T(8,128)(2,1)} %param.7), kind=kLoop, calls=%fused_computation.45 | loop fusion | bytes 4194304
  17.1 1.0 collective-permute-start.2
  18.2 0.3 constant_dynamic-update-slice_fusion
  18.4 1.6 broadcast_select_fusion
  20.1 3.2 %collective-permute-done.1 = bf16[16,16384]{1,0:T(8,128)(2,1)} collective-permute-done((bf16[16,16384]{1,0:T(8,128)(2,1)}, bf16[16,16384]{1,0:T(8,128)(2,1)}, u32[]{:S(2)}, u32[]{:S(2)}) %collective-permute-start.1) | collective-permute-done | bytes 524320 | tf_op jit(solution)/shard_map/ppermute | solution.py:147
  23.2 1.9 %collective-permute-done.5 = bf16[16,16384]{1,0:T(8,128)(2,1)} collective-permute-done((bf16[16,16384]{1,0:T(8,128)(2,1)}, bf16[16,16384]{1,0:T(8,128)(2,1)}, u32[]{:S(2)}, u32[]{:S(2)}) %collective-permute-start.5) | collective-permute-done | bytes 524320 | tf_op jit(solution)/shard_map/ppermute | solution.py:112
  25.1 1.5 collective-permute-start.9
  26.6 1.1 collective-permute-start.10
  27.8 8.4 %collective-permute-start.6 = (bf16[8,8,128,128]{3,2,1,0:T(8,128)(2,1)S(1)}, bf16[8,8,128,128]{3,2,1,0:T(8,128)(2,1)}, u32[]{:S(2)}, u32[]{:S(2)}) collective-permute-start(bf16[8,8,128,128]{3,2,1,0:T(8,128)(2,1)S(1)} %get-tuple-element.20.refs_9_), channel_id=1, source_target_pairs={{0,32},{1,225},{2,34},{3,227},{4,36},{5,229},{6,38},{7,231},{8,40}... | collective-permute-start | bytes 6291464 | tf_op jit(solution)/shard_map/ppermute | solution.py:167
  36.2 4.4 %collective-permute-start.7 = (bf16[8,8,128,128]{3,2,1,0:T(8,128)(2,1)}, bf16[8,8,128,128]{3,2,1,0:T(8,128)(2,1)}, u32[]{:S(2)}, u32[]{:S(2)}) collective-permute-start(bf16[8,8,128,128]{3,2,1,0:T(8,128)(2,1)} %get-tuple-element.21.refs_8_), channel_id=1, source_target_pairs={{0,32},{1,225},{2,34},{3,227},{4,36},{5,229},{6,38},{7,231},{8,40}... | collective-permute-start | bytes 6291464 | tf_op jit(solution)/shard_map/ppermute | solution.py:168
  40.6 0.0 copy-start.16
  40.6 0.1 pad_maximum_fusion.1.refs_1_
  40.7 1.3 collective-permute-start.12
  42.0 1.5 collective-permute-start.14
  43.4 2.1 %pad_maximum_fusion.refs_0_ = bf16[2,16,16384]{2,1,0:T(8,128)(2,1)} fusion(bf16[1,16,16384]{2,1,0:T(8,128)(2,1)S(1)} %bitcast.49, bf16[1,16,16384]{2,1,0:T(8,128)(2,1)} %bitcast.3), kind=kLoop, calls=%fused_computation.2 | loop fusion | flops 524288 | bytes 2097152 | tf_op jit(solution)/shard_map/stack | solution.py:116
  45.6 10.4 %collective-permute-done.12.refs_3_ = bf16[2,16,16384]{2,1,0:T(8,128)(2,1)S(1)} collective-permute-done((bf16[2,16,16384]{2,1,0:T(8,128)(2,1)S(1)}, bf16[2,16,16384]{2,1,0:T(8,128)(2,1)S(1)}, u32[]{:S(2)}, u32[]{:S(2)}) %collective-permute-start.12) | collective-permute-done | bytes 1048608 | tf_op jit(solution)/shard_map/ppermute | solution.py:119
  56.0 1.0 copy-done.6
  57.0 1.3 collective-permute-start.13
  58.3 0.8 collective-permute-start.25
  59.1 8.2 %collective-permute-done.11.refs_2_ = bf16[2,16,16384]{2,1,0:T(8,128)(2,1)} collective-permute-done((bf16[2,16,16384]{2,1,0:T(8,128)(2,1)}, bf16[2,16,16384]{2,1,0:T(8,128)(2,1)}, u32[]{:S(2)}, u32[]{:S(2)}) %collective-permute-start.11) | collective-permute-done | bytes 1048608 | tf_op jit(solution)/shard_map/ppermute | solution.py:117
  67.3 4.0 %collective-permute-done.13.refs_4_ = bf16[2,16,16384]{2,1,0:T(8,128)(2,1)} collective-permute-done((bf16[2,16,16384]{2,1,0:T(8,128)(2,1)}, bf16[2,16,16384]{2,1,0:T(8,128)(2,1)}, u32[]{:S(2)}, u32[]{:S(2)}) %collective-permute-start.13) | collective-permute-done | bytes 1048608 | tf_op jit(solution)/shard_map/ppermute | solution.py:120
  71.3 11.9 %collective-permute-done.7.refs_10_ = bf16[8,8,128,128]{3,2,1,0:T(8,128)(2,1)} collective-permute-done((bf16[8,8,128,128]{3,2,1,0:T(8,128)(2,1)}, bf16[8,8,128,128]{3,2,1,0:T(8,128)(2,1)}, u32[]{:S(2)}, u32[]{:S(2)}) %collective-permute-start.7) | collective-permute-done | bytes 2097184 | tf_op jit(solution)/shard_map/ppermute | solution.py:168
  83.2 1.5 collective-permute-start.21
  84.7 2.3 %pad_maximum_fusion.3.refs_1_ = bf16[2,16,16384]{2,1,0:T(8,128)(2,1)} fusion(bf16[1,16,16384]{2,1,0:T(8,128)(2,1)} %bitcast.10, bf16[1,16,16384]{2,1,0:T(8,128)(2,1)} %bitcast.9), kind=kLoop, calls=%fused_computation.5 | loop fusion | flops 524288 | bytes 2097152 | tf_op jit(solution)/shard_map/stack | solution.py:116
  87.0 4.2 %collective-permute-start.23 = (bf16[8,8,128,128]{3,2,1,0:T(8,128)(2,1)}, bf16[8,8,128,128]{3,2,1,0:T(8,128)(2,1)}, u32[]{:S(2)}, u32[]{:S(2)}) collective-permute-start(bf16[8,8,128,128]{3,2,1,0:T(8,128)(2,1)} %collective-permute-done.6.refs_11_), channel_id=1, source_target_pairs={{0,32},{1,225},{2,34},{3,227},{4,36},{5,229},{6,38},{7,231},{8,40}... | collective-permute-start | bytes 6291464 | tf_op jit(solution)/shard_map/ppermute | solution.py:169
  91.2 0.1 pad_maximum_fusion.2.refs_0_
  91.3 1.6 collective-permute-start.16
  92.9 1.2 collective-permute-start.18
  94.1 0.3 collective-permute-start.15
  94.4 2.4 %collective-permute-start.17 = (bf16[2,16,16384]{2,1,0:T(8,128)(2,1)S(1)}, bf16[2,16,16384]{2,1,0:T(8,128)(2,1)}, u32[]{:S(2)}, u32[]{:S(2)}) collective-permute-start(bf16[2,16,16384]{2,1,0:T(8,128)(2,1)S(1)} %pad_maximum_fusion.2.refs_0_), channel_id=1, source_target_pairs={{0,24},{1,7},{2,26},{3,1},{4,28},{5,3},{6,30},{7,5},{8,0},{9,15},{... | collective-permute-start | bytes 3145736 | tf_op jit(solution)/shard_map/ppermute | solution.py:120
  96.9 0.1 broadcast_add_fusion
  96.9 0.1 add.75.place
  97.0 0.1 fusion.10
  97.1 0.1 slice_select_fusion
  97.2 0.1 concatenate.23
  97.3 0.1 copy.14
  97.5 0.2 convert_element_type.28.live
  97.7 0.1 reshape_squeeze.3.blocks_in
  97.8 14.9 %shard_map.64.refs_10_ = f32[2,256,512]{2,1,0:T(8,128)S(1)} custom-call(s32[16]{0:T(128)S(1)} %add.75.place, s32[512]{0:T(512)S(1)} %reshape_squeeze.3.blocks_in, f32[1024]{0:T(1024)S(1)} %convert_element_type.28.live, bf16[2,16,16384]{2,1,0:T(8,128)(2,1)} %pad_maximum_fusion.refs_0_, bf16[2,16,16384]{2,1,0:T(8,128)(2,1)} %copy-done.2, ...), custom_call_target="tpu_custom_call" | custom-call | flops 3221225472 | bytes 20971520 | tf_op jit(solution)/shard_map/pallas_call | solution.py:89
  112.7 5.1 %collective-permute-done.15.refs_2_ = bf16[2,16,16384]{2,1,0:T(8,128)(2,1)} collective-permute-done((bf16[2,16,16384]{2,1,0:T(8,128)(2,1)S(1)}, bf16[2,16,16384]{2,1,0:T(8,128)(2,1)}, u32[]{:S(2)}, u32[]{:S(2)}) %collective-permute-start.15) | collective-permute-done | bytes 1048608 | tf_op jit(solution)/shard_map/ppermute | solution.py:117
  117.8 0.3 collective-permute-done.17.refs_4_
  118.1 2.4 %collective-permute-start.20 = (bf16[2,16,16384]{2,1,0:T(8,128)(2,1)}, bf16[2,16,16384]{2,1,0:T(8,128)(2,1)S(1)}, u32[]{:S(2)}, u32[]{:S(2)}) collective-permute-start(bf16[2,16,16384]{2,1,0:T(8,128)(2,1)} %collective-permute-done.18.refs_5_), channel_id=1, source_target_pairs={{0,24},{1,7},{2,26},{3,1},{4,28},{5,3},{6,30},{7,5},{8,0},{9,15},{... | collective-permute-start | bytes 3145736 | tf_op jit(solution)/shard_map/ppermute | solution.py:122
  120.5 2.0 %collective-permute-done.26.refs_15_.refs_9_ = bf16[8,8,128,128]{3,2,1,0:T(8,128)(2,1)S(1)} collective-permute-done((bf16[8,8,128,128]{3,2,1,0:T(8,128)(2,1)}, bf16[8,8,128,128]{3,2,1,0:T(8,128)(2,1)S(1)}, u32[]{:S(2)}, u32[]{:S(2)}) %collective-permute-start.26) | collective-permute-done | bytes 2097184 | tf_op jit(solution)/shard_map/ppermute | solution.py:179
  122.5 8.4 %shard_map.66 = f32[2,256,512]{2,1,0:T(8,128)S(1)} custom-call(s32[16]{0:T(128)S(1)} %add.75.place, s32[512]{0:T(512)S(1)} %reshape_squeeze.3.blocks_in, f32[1024]{0:T(1024)S(1)} %convert_element_type.28.live, bf16[2,16,16384]{2,1,0:T(8,128)(2,1)} %pad_maximum_fusion.refs_0_, bf16[2,16,16384]{2,1,0:T(8,128)(2,1)S(1)} %copy-done.3, ...), custom_call_target="tpu_custom_call" | custom-call | flops 1073741824 | bytes 12582912 | tf_op jit(solution)/shard_map/pallas_call | solution.py:89
  131.0 0.1 convert_element_type.29
  131.1 0.1 slice_bitcast_fusion.3
  131.2 10.6 %collective-permute-start.28 = (f16[256,512]{1,0:T(8,128)(2,1)S(1)}, f16[256,512]{1,0:T(8,128)(2,1)S(1)}, u32[]{:S(2)}, u32[]{:S(2)}) collective-permute-start(f16[256,512]{1,0:T(8,128)(2,1)S(1)} %get-tuple-element.38), channel_id=1, source_target_pairs={{0,128},{1,129},{2,130},{3,131},{4,132},{5,133},{6,134},{7,135},{8... | collective-permute-start | bytes 786440 | tf_op jit(solution)/shard_map/ppermute | solution.py:182
  141.8 0.3 collective-permute-start.27
  142.2 15.7 %shard_map.65 = f32[2,256,512]{2,1,0:T(8,128)S(1)} custom-call(s32[16]{0:T(128)S(1)} %add.75.place, s32[512]{0:T(512)S(1)} %reshape_squeeze.3.blocks_in, f32[1024]{0:T(1024)S(1)} %convert_element_type.28.live, bf16[2,16,16384]{2,1,0:T(8,128)(2,1)S(1)} %pad_maximum_fusion.2.refs_0_, bf16[2,16,16384]{2,1,0:T(8,128)(2,1)} %pad_maximum_fusion.3.refs_1_, ...), custom_call_target="tpu_custom_call" | custom-call | flops 4294967296 | bytes 25165824 | tf_op jit(solution)/shard_map/pallas_call | solution.py:89
  157.8 2.0 %collective-permute-done.28 = f16[256,512]{1,0:T(8,128)(2,1)S(1)} collective-permute-done((f16[256,512]{1,0:T(8,128)(2,1)S(1)}, f16[256,512]{1,0:T(8,128)(2,1)S(1)}, u32[]{:S(2)}, u32[]{:S(2)}) %collective-permute-start.28) | collective-permute-done | bytes 262176 | tf_op jit(solution)/shard_map/ppermute | solution.py:182
  159.9 0.1 fusion.2
  160.0 0.1 collective-permute-start.29
  160.1 3.5 %collective-permute-done.27 = f16[256,512]{1,0:T(8,128)(2,1)S(1)} collective-permute-done((f16[256,512]{1,0:T(8,128)(2,1)S(1)}, f16[256,512]{1,0:T(8,128)(2,1)S(1)}, u32[]{:S(2)}, u32[]{:S(2)}) %collective-permute-start.27) | collective-permute-done | bytes 262176 | tf_op jit(solution)/shard_map/ppermute | solution.py:183
  163.6 0.1 broadcast_select_fusion.3
  163.7 0.1 maximum_bitcast_fusion
  163.8 0.9 copy.15
  (61 shorter events, 0.2 us)
Async XLA Ops:
  0.0 17.1 %collective-permute-start = (bf16[4,16,128,128]{3,2,1,0:T(8,128)(2,1)}, bf16[4,16,128,128]{3,2,1,0:T(8,128)(2,1)S(1)}, u32[]{:S(2)}, u32[]{:S(2)}) collective-permute-start(bf16[4,16,128,128]{3,2,1,0:T(8,128)(2,1)} %param.7), channel_id=1, source_target_pairs={{0,1},{1,0},{2,3},{3,2},{4,5},{5,4},{6,7},{7,6},{8,9},{9,8},{10,11... | collective-permute-start | bytes 6291464 | tf_op jit(solution)/shard_map/ppermute | solution.py:154
  3.2 20.0 %collective-permute-start.1 = (bf16[16,16384]{1,0:T(8,128)(2,1)}, bf16[16,16384]{1,0:T(8,128)(2,1)}, u32[]{:S(2)}, u32[]{:S(2)}) collective-permute-start(bf16[16,16384]{1,0:T(8,128)(2,1)} %bitcast.43), channel_id=1, source_target_pairs={{0,128},{1,129},{2,130},{3,131},{4,132},{5,133},{6,134},{7,135},{8... | collective-permute-start | bytes 1572872 | tf_op jit(solution)/shard_map/ppermute | solution.py:147
  8.4 14.8 %collective-permute-start.3 = (bf16[16,16384]{1,0:T(8,128)(2,1)}, bf16[16,16384]{1,0:T(8,128)(2,1)S(1)}, u32[]{:S(2)}, u32[]{:S(2)}) collective-permute-start(bf16[16,16384]{1,0:T(8,128)(2,1)} %bitcast.44), channel_id=1, source_target_pairs={{0,2},{1,9},{2,4},{3,11},{4,6},{5,13},{6,0},{7,15},{8,10},{9,17},{... | collective-permute-start | bytes 1572872 | tf_op jit(solution)/shard_map/ppermute | solution.py:112
  9.7 13.5 %collective-permute-start.4 = (bf16[16,16384]{1,0:T(8,128)(2,1)}, bf16[16,16384]{1,0:T(8,128)(2,1)}, u32[]{:S(2)}, u32[]{:S(2)}) collective-permute-start(bf16[16,16384]{1,0:T(8,128)(2,1)} %bitcast.45), channel_id=1, source_target_pairs={{0,6},{1,25},{2,0},{3,27},{4,2},{5,29},{6,4},{7,31},{8,14},{9,1},{... | collective-permute-start | bytes 1572872 | tf_op jit(solution)/shard_map/ppermute | solution.py:112
  11.2 14.0 %collective-permute-start.5 = (bf16[16,16384]{1,0:T(8,128)(2,1)}, bf16[16,16384]{1,0:T(8,128)(2,1)}, u32[]{:S(2)}, u32[]{:S(2)}) collective-permute-start(bf16[16,16384]{1,0:T(8,128)(2,1)} %bitcast.46), channel_id=1, source_target_pairs={{0,4},{1,17},{2,6},{3,19},{4,0},{5,21},{6,2},{7,23},{8,12},{9,25},... | collective-permute-start | bytes 1572872 | tf_op jit(solution)/shard_map/ppermute | solution.py:112
  17.1 2.9 %collective-permute-start.2 = (s32[3,4,128]{2,1,0:T(4,128)S(1)}, s32[3,4,128]{2,1,0:T(4,128)S(1)}, u32[]{:S(2)}, u32[]{:S(2)}) collective-permute-start(s32[3,4,128]{2,1,0:T(4,128)S(1)} %pad_add_fusion), channel_id=1, source_target_pairs={{0,1},{1,0},{2,3},{3,2},{4,5},{5,4},{6,7},{7,6},{8,9},{9,8},{10,11... | collective-permute-start | bytes 18440 | tf_op jit(solution)/shard_map/ppermute | solution.py:139
  20.1 25.5 %copy-start = (bf16[8,8,128,128]{3,2,1,0:T(8,128)(2,1)}, bf16[8,8,128,128]{3,2,1,0:T(8,128)(2,1)S(1)}, u32[]{:S(2)}) copy-start(bf16[8,8,128,128]{3,2,1,0:T(8,128)(2,1)S(1)} %get-tuple-element.20.refs_9_) | copy-start | bytes 6291460
  23.2 17.3 %copy-start.13 = (bf16[16,16384]{1,0:T(8,128)(2,1)}, bf16[16,16384]{1,0:T(8,128)(2,1)S(1)}, u32[]{:S(2)}) copy-start(bf16[16,16384]{1,0:T(8,128)(2,1)S(1)} %collective-permute-done.3) | copy-start | bytes 1572868
  25.1 15.4 %collective-permute-start.9 = (bf16[16,16384]{1,0:T(8,128)(2,1)}, bf16[16,16384]{1,0:T(8,128)(2,1)S(1)}, u32[]{:S(2)}, u32[]{:S(2)}) collective-permute-start(bf16[16,16384]{1,0:T(8,128)(2,1)} %collective-permute-done.1), channel_id=1, source_target_pairs={{0,6},{1,25},{2,0},{3,27},{4,2},{5,29},{6,4},{7,31},{8,14},{9,1},{... | collective-permute-start | bytes 1572872 | tf_op jit(solution)/shard_map/ppermute | solution.py:112
  26.6 13.9 %collective-permute-start.10 = (bf16[16,16384]{1,0:T(8,128)(2,1)}, bf16[16,16384]{1,0:T(8,128)(2,1)S(1)}, u32[]{:S(2)}, u32[]{:S(2)}) collective-permute-start(bf16[16,16384]{1,0:T(8,128)(2,1)} %collective-permute-done.1), channel_id=1, source_target_pairs={{0,4},{1,17},{2,6},{3,19},{4,0},{5,21},{6,2},{7,23},{8,12},{9,25},... | collective-permute-start | bytes 1572872 | tf_op jit(solution)/shard_map/ppermute | solution.py:112
  27.8 15.7 %collective-permute-start.8 = (bf16[16,16384]{1,0:T(8,128)(2,1)}, bf16[16,16384]{1,0:T(8,128)(2,1)S(1)}, u32[]{:S(2)}, u32[]{:S(2)}) collective-permute-start(bf16[16,16384]{1,0:T(8,128)(2,1)} %collective-permute-done.1), channel_id=1, source_target_pairs={{0,2},{1,9},{2,4},{3,11},{4,6},{5,13},{6,0},{7,15},{8,10},{9,17},{... | collective-permute-start | bytes 1572872 | tf_op jit(solution)/shard_map/ppermute | solution.py:112
  27.8 43.5 %collective-permute-start.6 = (bf16[8,8,128,128]{3,2,1,0:T(8,128)(2,1)S(1)}, bf16[8,8,128,128]{3,2,1,0:T(8,128)(2,1)}, u32[]{:S(2)}, u32[]{:S(2)}) collective-permute-start(bf16[8,8,128,128]{3,2,1,0:T(8,128)(2,1)S(1)} %get-tuple-element.20.refs_9_), channel_id=1, source_target_pairs={{0,32},{1,225},{2,34},{3,227},{4,36},{5,229},{6,38},{7,231},{8,40}... | collective-permute-start | bytes 6291464 | tf_op jit(solution)/shard_map/ppermute | solution.py:167
  36.2 47.0 %collective-permute-start.7 = (bf16[8,8,128,128]{3,2,1,0:T(8,128)(2,1)}, bf16[8,8,128,128]{3,2,1,0:T(8,128)(2,1)}, u32[]{:S(2)}, u32[]{:S(2)}) collective-permute-start(bf16[8,8,128,128]{3,2,1,0:T(8,128)(2,1)} %get-tuple-element.21.refs_8_), channel_id=1, source_target_pairs={{0,32},{1,225},{2,34},{3,227},{4,36},{5,229},{6,38},{7,231},{8,40}... | collective-permute-start | bytes 6291464 | tf_op jit(solution)/shard_map/ppermute | solution.py:168
  40.6 17.7 %copy-start.16 = (s32[4]{0:T(128)S(1)}, s32[4]{0:T(128)}, u32[]{:S(2)}) copy-start(s32[4]{0:T(128)} %constant.97.clone) | copy-start | bytes 52
  40.7 46.3 %copy-start.2 = (bf16[2,16,16384]{2,1,0:T(8,128)(2,1)}, bf16[2,16,16384]{2,1,0:T(8,128)(2,1)S(1)}, u32[]{:S(2)}) copy-start(bf16[2,16,16384]{2,1,0:T(8,128)(2,1)S(1)} %pad_maximum_fusion.1.refs_1_) | copy-start | bytes 3145732
  40.7 15.3 %collective-permute-start.12 = (bf16[2,16,16384]{2,1,0:T(8,128)(2,1)S(1)}, bf16[2,16,16384]{2,1,0:T(8,128)(2,1)S(1)}, u32[]{:S(2)}, u32[]{:S(2)}) collective-permute-start(bf16[2,16,16384]{2,1,0:T(8,128)(2,1)S(1)} %pad_maximum_fusion.1.refs_1_), channel_id=1, source_target_pairs={{0,8},{1,3},{2,10},{3,5},{4,12},{5,7},{6,14},{7,1},{8,16},{9,11},{... | collective-permute-start | bytes 3145736 | tf_op jit(solution)/shard_map/ppermute | solution.py:119
  42.0 16.3 %collective-permute-start.14 = (bf16[2,16,16384]{2,1,0:T(8,128)(2,1)S(1)}, bf16[2,16,16384]{2,1,0:T(8,128)(2,1)}, u32[]{:S(2)}, u32[]{:S(2)}) collective-permute-start(bf16[2,16,16384]{2,1,0:T(8,128)(2,1)S(1)} %pad_maximum_fusion.1.refs_1_), channel_id=1, source_target_pairs={{0,24},{1,7},{2,26},{3,1},{4,28},{5,3},{6,30},{7,5},{8,0},{9,15},{... | collective-permute-start | bytes 3145736 | tf_op jit(solution)/shard_map/ppermute | solution.py:118
  45.6 21.7 %collective-permute-start.11 = (bf16[2,16,16384]{2,1,0:T(8,128)(2,1)}, bf16[2,16,16384]{2,1,0:T(8,128)(2,1)}, u32[]{:S(2)}, u32[]{:S(2)}) collective-permute-start(bf16[2,16,16384]{2,1,0:T(8,128)(2,1)} %pad_maximum_fusion.refs_0_), channel_id=1, source_target_pairs={{0,8},{1,3},{2,10},{3,5},{4,12},{5,7},{6,14},{7,1},{8,16},{9,11},{... | collective-permute-start | bytes 3145736 | tf_op jit(solution)/shard_map/ppermute | solution.py:117
  56.0 1.0 copy-start.6
  57.0 14.3 %collective-permute-start.13 = (bf16[2,16,16384]{2,1,0:T(8,128)(2,1)}, bf16[2,16,16384]{2,1,0:T(8,128)(2,1)}, u32[]{:S(2)}, u32[]{:S(2)}) collective-permute-start(bf16[2,16,16384]{2,1,0:T(8,128)(2,1)} %pad_maximum_fusion.refs_0_), channel_id=1, source_target_pairs={{0,24},{1,7},{2,26},{3,1},{4,28},{5,3},{6,30},{7,5},{8,0},{9,15},{... | collective-permute-start | bytes 3145736 | tf_op jit(solution)/shard_map/ppermute | solution.py:120
  58.3 32.9 %copy-start.12 = (bf16[2,8,16384]{2,1,0:T(8,128)(2,1)S(1)}, bf16[2,8,16384]{2,1,0:T(8,128)(2,1)}, u32[]{:S(2)}) copy-start(bf16[2,8,16384]{2,1,0:T(8,128)(2,1)} %param.6) | copy-start | bytes 1572868
  58.3 32.9 %copy-start.14 = (bf16[16,16384]{1,0:T(8,128)(2,1)S(1)}, bf16[16,16384]{1,0:T(8,128)(2,1)}, u32[]{:S(2)}) copy-start(bf16[16,16384]{1,0:T(8,128)(2,1)} %copy-done.13) | copy-start | bytes 1572868
  58.3 33.0 %collective-permute-start.25 = (bf16[2,16,16384]{2,1,0:T(8,128)(2,1)}, bf16[2,16,16384]{2,1,0:T(8,128)(2,1)S(1)}, u32[]{:S(2)}, u32[]{:S(2)}) collective-permute-start(bf16[2,16,16384]{2,1,0:T(8,128)(2,1)} %collective-permute-done.14.refs_5_), channel_id=1, source_target_pairs={{0,24},{1,7},{2,26},{3,1},{4,28},{5,3},{6,30},{7,5},{8,0},{9,15},{... | collective-permute-start | bytes 3145736 | tf_op jit(solution)/shard_map/ppermute | solution.py:122
  67.3 25.7 %collective-permute-start.24 = (bf16[2,16,16384]{2,1,0:T(8,128)(2,1)}, bf16[2,16,16384]{2,1,0:T(8,128)(2,1)S(1)}, u32[]{:S(2)}, u32[]{:S(2)}) collective-permute-start(bf16[2,16,16384]{2,1,0:T(8,128)(2,1)} %collective-permute-done.11.refs_2_), channel_id=1, source_target_pairs={{0,8},{1,3},{2,10},{3,5},{4,12},{5,7},{6,14},{7,1},{8,16},{9,11},{... | collective-permute-start | bytes 3145736 | tf_op jit(solution)/shard_map/ppermute | solution.py:121
  83.2 10.9 %collective-permute-start.21 = (bf16[8,8,128,128]{3,2,1,0:T(8,128)(2,1)}, bf16[8,8,128,128]{3,2,1,0:T(8,128)(2,1)S(1)}, u32[]{:S(2)}, u32[]{:S(2)}) collective-permute-start(bf16[8,8,128,128]{3,2,1,0:T(8,128)(2,1)} %collective-permute-done.7.refs_10_), channel_id=1, source_target_pairs={{0,1},{1,0},{2,3},{3,2},{4,5},{5,4},{6,7},{7,6},{8,9},{9,8},{10,11... | collective-permute-start | bytes 6291464 | tf_op jit(solution)/shard_map/ppermute | solution.py:175
  84.7 9.7 %collective-permute-start.22 = (bf16[8,8,128,128]{3,2,1,0:T(8,128)(2,1)}, bf16[8,8,128,128]{3,2,1,0:T(8,128)(2,1)}, u32[]{:S(2)}, u32[]{:S(2)}) collective-permute-start(bf16[8,8,128,128]{3,2,1,0:T(8,128)(2,1)} %collective-permute-done.6.refs_11_), channel_id=1, source_target_pairs={{0,1},{1,0},{2,3},{3,2},{4,5},{5,4},{6,7},{7,6},{8,9},{9,8},{10,11... | collective-permute-start | bytes 6291464 | tf_op jit(solution)/shard_map/ppermute | solution.py:175
  84.7 12.3 %copy-start.15 = (s32[4,128]{1,0:T(4,128)S(1)}, s32[4,128]{1,0:T(4,128)}, u32[]{:S(2)}) copy-start(s32[4,128]{1,0:T(4,128)} %param.8) | copy-start | bytes 6148
  87.0 31.1 %collective-permute-start.23 = (bf16[8,8,128,128]{3,2,1,0:T(8,128)(2,1)}, bf16[8,8,128,128]{3,2,1,0:T(8,128)(2,1)}, u32[]{:S(2)}, u32[]{:S(2)}) collective-permute-start(bf16[8,8,128,128]{3,2,1,0:T(8,128)(2,1)} %collective-permute-done.6.refs_11_), channel_id=1, source_target_pairs={{0,32},{1,225},{2,34},{3,227},{4,36},{5,229},{6,38},{7,231},{8,40}... | collective-permute-start | bytes 6291464 | tf_op jit(solution)/shard_map/ppermute | solution.py:169
  91.3 3.1 %copy-start.8 = (bf16[2,16,16384]{2,1,0:T(8,128)(2,1)}, bf16[2,16,16384]{2,1,0:T(8,128)(2,1)S(1)}, u32[]{:S(2)}) copy-start(bf16[2,16,16384]{2,1,0:T(8,128)(2,1)S(1)} %collective-permute-done.25.refs_7_) | copy-start | bytes 3145732
  91.3 21.4 %collective-permute-start.16 = (bf16[2,16,16384]{2,1,0:T(8,128)(2,1)}, bf16[2,16,16384]{2,1,0:T(8,128)(2,1)}, u32[]{:S(2)}, u32[]{:S(2)}) collective-permute-start(bf16[2,16,16384]{2,1,0:T(8,128)(2,1)} %pad_maximum_fusion.3.refs_1_), channel_id=1, source_target_pairs={{0,8},{1,3},{2,10},{3,5},{4,12},{5,7},{6,14},{7,1},{8,16},{9,11},{... | collective-permute-start | bytes 3145736 | tf_op jit(solution)/shard_map/ppermute | solution.py:119
  92.9 1.5 copy-start.10
  92.9 19.8 %collective-permute-start.18 = (bf16[2,16,16384]{2,1,0:T(8,128)(2,1)}, bf16[2,16,16384]{2,1,0:T(8,128)(2,1)}, u32[]{:S(2)}, u32[]{:S(2)}) collective-permute-start(bf16[2,16,16384]{2,1,0:T(8,128)(2,1)} %pad_maximum_fusion.3.refs_1_), channel_id=1, source_target_pairs={{0,24},{1,7},{2,26},{3,1},{4,28},{5,3},{6,30},{7,5},{8,0},{9,15},{... | collective-permute-start | bytes 3145736 | tf_op jit(solution)/shard_map/ppermute | solution.py:118
  94.1 3.6 %copy-start.4 = (bf16[8,8,128,128]{3,2,1,0:T(8,128)(2,1)}, bf16[8,8,128,128]{3,2,1,0:T(8,128)(2,1)S(1)}, u32[]{:S(2)}) copy-start(bf16[8,8,128,128]{3,2,1,0:T(8,128)(2,1)S(1)} %collective-permute-done.21.refs_12_) | copy-start | bytes 6291460
  94.1 23.7 %collective-permute-start.15 = (bf16[2,16,16384]{2,1,0:T(8,128)(2,1)S(1)}, bf16[2,16,16384]{2,1,0:T(8,128)(2,1)}, u32[]{:S(2)}, u32[]{:S(2)}) collective-permute-start(bf16[2,16,16384]{2,1,0:T(8,128)(2,1)S(1)} %pad_maximum_fusion.2.refs_0_), channel_id=1, source_target_pairs={{0,8},{1,3},{2,10},{3,5},{4,12},{5,7},{6,14},{7,1},{8,16},{9,11},{... | collective-permute-start | bytes 3145736 | tf_op jit(solution)/shard_map/ppermute | solution.py:117
  94.4 23.7 %collective-permute-start.17 = (bf16[2,16,16384]{2,1,0:T(8,128)(2,1)S(1)}, bf16[2,16,16384]{2,1,0:T(8,128)(2,1)}, u32[]{:S(2)}, u32[]{:S(2)}) collective-permute-start(bf16[2,16,16384]{2,1,0:T(8,128)(2,1)S(1)} %pad_maximum_fusion.2.refs_0_), channel_id=1, source_target_pairs={{0,24},{1,7},{2,26},{3,1},{4,28},{5,3},{6,30},{7,5},{8,0},{9,15},{... | collective-permute-start | bytes 3145736 | tf_op jit(solution)/shard_map/ppermute | solution.py:120
  97.7 24.8 %copy-start.3 = (bf16[2,16,16384]{2,1,0:T(8,128)(2,1)S(1)}, bf16[2,16,16384]{2,1,0:T(8,128)(2,1)}, u32[]{:S(2)}) copy-start(bf16[2,16,16384]{2,1,0:T(8,128)(2,1)} %copy-done.2) | copy-start | bytes 3145732
  97.7 24.8 %copy-start.7 = (bf16[2,16,16384]{2,1,0:T(8,128)(2,1)S(1)}, bf16[2,16,16384]{2,1,0:T(8,128)(2,1)}, u32[]{:S(2)}) copy-start(bf16[2,16,16384]{2,1,0:T(8,128)(2,1)} %copy-done.6) | copy-start | bytes 3145732
  97.7 24.8 %copy-start.9 = (bf16[2,16,16384]{2,1,0:T(8,128)(2,1)S(1)}, bf16[2,16,16384]{2,1,0:T(8,128)(2,1)}, u32[]{:S(2)}) copy-start(bf16[2,16,16384]{2,1,0:T(8,128)(2,1)} %copy-done.8) | copy-start | bytes 3145732
  97.7 24.8 %copy-start.11 = (bf16[2,16,16384]{2,1,0:T(8,128)(2,1)S(1)}, bf16[2,16,16384]{2,1,0:T(8,128)(2,1)}, u32[]{:S(2)}) copy-start(bf16[2,16,16384]{2,1,0:T(8,128)(2,1)} %copy-done.10) | copy-start | bytes 3145732
  118.1 4.4 %collective-permute-start.26 = (bf16[8,8,128,128]{3,2,1,0:T(8,128)(2,1)}, bf16[8,8,128,128]{3,2,1,0:T(8,128)(2,1)S(1)}, u32[]{:S(2)}, u32[]{:S(2)}) collective-permute-start(bf16[8,8,128,128]{3,2,1,0:T(8,128)(2,1)} %collective-permute-done.23.refs_14_.refs_8_), channel_id=1, source_target_pairs={{0,1},{1,0},{2,3},{3,2},{4,5},{5,4},{6,7},{7,6},{8,9},{9,8},{10,11... | collective-permute-start | bytes 6291464 | tf_op jit(solution)/shard_map/ppermute | solution.py:179
  118.1 24.0 %collective-permute-start.20 = (bf16[2,16,16384]{2,1,0:T(8,128)(2,1)}, bf16[2,16,16384]{2,1,0:T(8,128)(2,1)S(1)}, u32[]{:S(2)}, u32[]{:S(2)}) collective-permute-start(bf16[2,16,16384]{2,1,0:T(8,128)(2,1)} %collective-permute-done.18.refs_5_), channel_id=1, source_target_pairs={{0,24},{1,7},{2,26},{3,1},{4,28},{5,3},{6,30},{7,5},{8,0},{9,15},{... | collective-permute-start | bytes 3145736 | tf_op jit(solution)/shard_map/ppermute | solution.py:122
  120.5 21.6 %collective-permute-start.19 = (bf16[2,16,16384]{2,1,0:T(8,128)(2,1)}, bf16[2,16,16384]{2,1,0:T(8,128)(2,1)S(1)}, u32[]{:S(2)}, u32[]{:S(2)}) collective-permute-start(bf16[2,16,16384]{2,1,0:T(8,128)(2,1)} %collective-permute-done.15.refs_2_), channel_id=1, source_target_pairs={{0,8},{1,3},{2,10},{3,5},{4,12},{5,7},{6,14},{7,1},{8,16},{9,11},{... | collective-permute-start | bytes 3145736 | tf_op jit(solution)/shard_map/ppermute | solution.py:121
  122.5 19.6 %copy-start.5 = (bf16[8,8,128,128]{3,2,1,0:T(8,128)(2,1)S(1)}, bf16[8,8,128,128]{3,2,1,0:T(8,128)(2,1)}, u32[]{:S(2)}) copy-start(bf16[8,8,128,128]{3,2,1,0:T(8,128)(2,1)} %copy-done.4) | copy-start | bytes 6291460
  131.0 11.2 %copy-start.1 = (bf16[8,8,128,128]{3,2,1,0:T(8,128)(2,1)S(1)}, bf16[8,8,128,128]{3,2,1,0:T(8,128)(2,1)}, u32[]{:S(2)}) copy-start(bf16[8,8,128,128]{3,2,1,0:T(8,128)(2,1)} %copy-done) | copy-start | bytes 6291460
  131.2 28.7 %collective-permute-start.28 = (f16[256,512]{1,0:T(8,128)(2,1)S(1)}, f16[256,512]{1,0:T(8,128)(2,1)S(1)}, u32[]{:S(2)}, u32[]{:S(2)}) collective-permute-start(f16[256,512]{1,0:T(8,128)(2,1)S(1)} %get-tuple-element.38), channel_id=1, source_target_pairs={{0,128},{1,129},{2,130},{3,131},{4,132},{5,133},{6,134},{7,135},{8... | collective-permute-start | bytes 786440 | tf_op jit(solution)/shard_map/ppermute | solution.py:182
  141.8 21.8 %collective-permute-start.27 = (f16[256,512]{1,0:T(8,128)(2,1)S(1)}, f16[256,512]{1,0:T(8,128)(2,1)S(1)}, u32[]{:S(2)}, u32[]{:S(2)}) collective-permute-start(f16[256,512]{1,0:T(8,128)(2,1)S(1)} %get-tuple-element.37), channel_id=1, source_target_pairs={{0,128},{1,129},{2,130},{3,131},{4,132},{5,133},{6,134},{7,135},{8... | collective-permute-start | bytes 786440 | tf_op jit(solution)/shard_map/ppermute | solution.py:183
  160.0 3.6 %collective-permute-start.29 = (bf16[256,512]{1,0:T(8,128)(2,1)S(1)}, bf16[256,512]{1,0:T(8,128)(2,1)S(1)}, u32[]{:S(2)}, u32[]{:S(2)}) collective-permute-start(bf16[256,512]{1,0:T(8,128)(2,1)S(1)} %fusion.2), channel_id=1, source_target_pairs={{0,1},{1,0},{2,3},{3,2},{4,5},{5,4},{6,7},{7,6},{8,9},{9,8},{10,11... | collective-permute-start | bytes 786440 | tf_op jit(solution)/shard_map/ppermute | solution.py:187

commit v5 on v4

--- a/solution.py
+++ b/solution.py
@@ -169,7 +169,7 @@
     half = lax.ppermute(near_goes, both, onward)
     far_amps = spread(far, *gather(far, 0, (1, -1, 2)))
     near_goes, near_stays, own, *own_near = lax.optimization_barrier(
-        (near_goes, near_stays, own, *own_near, *far_amps[:6])
+        (near_goes, near_stays, own, *own_near, *far_amps[:2], far_amps[3], far_amps[5])
     )[:6]
     own_amps = spread(own, *own_near)
     others = [lax.ppermute(x, "tile", swapped()) for x in (near_stays, near_goes)]

time: 167 us -> 166 us (level)
    ppermute x1, waiting for transfers between devices: 11.9 us -> 15.9 us  [on_device(): near_stays = lax.ppermute(stays, both, onward)]
    ppermute x2, waiting for transfers between devices: 4.31 us -> 0.32 us  [spread(): fore_behind = lax.ppermute(fore, 'tile', moved(1, -1))]
  transfers between devices with their start and end apart: 30 -> 30, of which waited for: 11 -> 10; matrix products, arithmetic and copies ran while one was open for 7% -> 7% of each run, Pallas kernels for 24% -> 24%
where the time goes in v5:
time: 166 us; the launch traced here: 164 us
  starting transfers between devices  58.4 us (35%)
  waiting for transfers between devices  52.9 us (32%)
  Pallas kernels  39 us (23%)
  other arithmetic  9.39 us (6%)
  local copies, waits for them, and re-layouts  3.7 us (2%)
    pallas_call x3, Pallas kernels, partial_ladder(): pl.pallas_call(functools.partial(body, len(amps), low, tail, ordered), ou...  39 us
    ppermute x1, waiting for transfers between devices, on_device(): near_stays = lax.ppermute(stays, both, onward)  15.9 us
    ppermute x2, waiting for transfers between devices, spread(): fore_before = lax.ppermute(fore, 'tile', moved(1, 1))  13.6 us
    ppermute x2, waiting for transfers between devices, spread(): aft_before = lax.ppermute(aft, 'tile', moved(1, 1))  10.4 us
    ppermute x1, starting transfers between devices, on_device(): back_1 = lax.ppermute(back[1], both, turned(groups, tiles))  9.68 us
    ppermute x1, starting transfers between devices, on_device(): near_goes = lax.ppermute(goes, both, onward)  8.38 us
    ppermute x6, starting transfers between devices, gather(): return [lax.ppermute(shard, 'tile', moved(phase, step)) for step in steps]  7.03 us
    ppermute x1, starting transfers between devices, on_device(): far = lax.ppermute(own, both, turned(groups, tiles))  5.17 us
  transfers between devices with their start and end apart: 30, of which 10 were waited for; matrix products, arithmetic and copies ran while one was open for 7% of the time, Pallas kernels for 24%

profile of v5, /device:TPU:1, one launch (start us, length us, event | category | flops | bytes accessed | tf_op | source)
XLA Modules:
  0.0 163.8 jit_solution(16366057925188164895)
XLA Ops:
  0.0 3.2 %collective-permute-start = (bf16[4,16,128,128]{3,2,1,0:T(8,128)(2,1)}, bf16[4,16,128,128]{3,2,1,0:T(8,128)(2,1)S(1)}, u32[]{:S(2)}, u32[]{:S(2)}) collective-permute-start(bf16[4,16,128,128]{3,2,1,0:T(8,128)(2,1)} %param.7), channel_id=1, source_target_pairs={{0,1},{1,0},{2,3},{3,2},{4,5},{5,4},{6,7},{7,6},{8,9},{9,8},{10,11... | collective-permute-start | bytes 6291464 | tf_op jit(solution)/shard_map/ppermute | solution.py:154
  3.2 5.2 %collective-permute-start.1 = (bf16[16,16384]{1,0:T(8,128)(2,1)}, bf16[16,16384]{1,0:T(8,128)(2,1)}, u32[]{:S(2)}, u32[]{:S(2)}) collective-permute-start(bf16[16,16384]{1,0:T(8,128)(2,1)} %bitcast.43), channel_id=1, source_target_pairs={{0,128},{1,129},{2,130},{3,131},{4,132},{5,133},{6,134},{7,135},{8... | collective-permute-start | bytes 1572872 | tf_op jit(solution)/shard_map/ppermute | solution.py:147
  8.4 1.3 collective-permute-start.3
  9.7 1.4 collective-permute-start.4
  11.2 1.6 %collective-permute-start.5 = (bf16[16,16384]{1,0:T(8,128)(2,1)}, bf16[16,16384]{1,0:T(8,128)(2,1)}, u32[]{:S(2)}, u32[]{:S(2)}) collective-permute-start(bf16[16,16384]{1,0:T(8,128)(2,1)} %bitcast.46), channel_id=1, source_target_pairs={{0,4},{1,17},{2,6},{3,19},{4,0},{5,21},{6,2},{7,23},{8,12},{9,25},... | collective-permute-start | bytes 1572872 | tf_op jit(solution)/shard_map/ppermute | solution.py:112
  12.8 0.8 iota_compare_fusion.1
  13.5 1.0 fusion.7
  14.6 0.7 pad_add_fusion
  15.3 1.8 %constant_dynamic-update-slice_fusion.1 = bf16[8,16,128,128]{3,2,1,0:T(8,128)(2,1)S(1)} fusion(bf16[4,16,128,128]{3,2,1,0:T(8,128)(2,1)} %param.7), kind=kLoop, calls=%fused_computation.45 | loop fusion | bytes 4194304
  17.1 1.0 collective-permute-start.2
  18.2 0.3 constant_dynamic-update-slice_fusion
  18.4 1.6 broadcast_select_fusion
  20.1 3.2 %collective-permute-done.1 = bf16[16,16384]{1,0:T(8,128)(2,1)} collective-permute-done((bf16[16,16384]{1,0:T(8,128)(2,1)}, bf16[16,16384]{1,0:T(8,128)(2,1)}, u32[]{:S(2)}, u32[]{:S(2)}) %collective-permute-start.1) | collective-permute-done | bytes 524320 | tf_op jit(solution)/shard_map/ppermute | solution.py:147
  23.2 1.9 %collective-permute-done.5 = bf16[16,16384]{1,0:T(8,128)(2,1)} collective-permute-done((bf16[16,16384]{1,0:T(8,128)(2,1)}, bf16[16,16384]{1,0:T(8,128)(2,1)}, u32[]{:S(2)}, u32[]{:S(2)}) %collective-permute-start.5) | collective-permute-done | bytes 524320 | tf_op jit(solution)/shard_map/ppermute | solution.py:112
  25.1 1.5 collective-permute-start.9
  26.6 1.1 collective-permute-start.10
  27.8 8.4 %collective-permute-start.6 = (bf16[8,8,128,128]{3,2,1,0:T(8,128)(2,1)S(1)}, bf16[8,8,128,128]{3,2,1,0:T(8,128)(2,1)}, u32[]{:S(2)}, u32[]{:S(2)}) collective-permute-start(bf16[8,8,128,128]{3,2,1,0:T(8,128)(2,1)S(1)} %get-tuple-element.20.refs_9_), channel_id=1, source_target_pairs={{0,32},{1,225},{2,34},{3,227},{4,36},{5,229},{6,38},{7,231},{8,40}... | collective-permute-start | bytes 6291464 | tf_op jit(solution)/shard_map/ppermute | solution.py:167
  36.2 4.4 %collective-permute-start.7 = (bf16[8,8,128,128]{3,2,1,0:T(8,128)(2,1)}, bf16[8,8,128,128]{3,2,1,0:T(8,128)(2,1)}, u32[]{:S(2)}, u32[]{:S(2)}) collective-permute-start(bf16[8,8,128,128]{3,2,1,0:T(8,128)(2,1)} %get-tuple-element.21.refs_8_), channel_id=1, source_target_pairs={{0,32},{1,225},{2,34},{3,227},{4,36},{5,229},{6,38},{7,231},{8,40}... | collective-permute-start | bytes 6291464 | tf_op jit(solution)/shard_map/ppermute | solution.py:168
  40.6 0.0 copy-start.16
  40.6 0.1 pad_maximum_fusion.1.refs_1_
  40.7 1.3 collective-permute-start.11
  42.0 1.5 collective-permute-start.12
  43.4 2.1 %pad_maximum_fusion.refs_0_ = bf16[2,16,16384]{2,1,0:T(8,128)(2,1)} fusion(bf16[1,16,16384]{2,1,0:T(8,128)(2,1)S(1)} %bitcast.49, bf16[1,16,16384]{2,1,0:T(8,128)(2,1)} %bitcast.3), kind=kLoop, calls=%fused_computation.2 | loop fusion | flops 524288 | bytes 2097152 | tf_op jit(solution)/shard_map/stack | solution.py:116
  45.6 0.0 copy-start.12
  45.6 0.0 copy-start.14
  45.6 10.4 %collective-permute-done.11.refs_3_ = bf16[2,16,16384]{2,1,0:T(8,128)(2,1)} collective-permute-done((bf16[2,16,16384]{2,1,0:T(8,128)(2,1)S(1)}, bf16[2,16,16384]{2,1,0:T(8,128)(2,1)}, u32[]{:S(2)}, u32[]{:S(2)}) %collective-permute-start.11) | collective-permute-done | bytes 1048608 | tf_op jit(solution)/shard_map/ppermute | solution.py:119
  56.0 1.3 collective-permute-start.23
  57.3 1.4 collective-permute-start.25
  58.7 8.6 %collective-permute-done.22.refs_2_ = bf16[2,16,16384]{2,1,0:T(8,128)(2,1)} collective-permute-done((bf16[2,16,16384]{2,1,0:T(8,128)(2,1)}, bf16[2,16,16384]{2,1,0:T(8,128)(2,1)}, u32[]{:S(2)}, u32[]{:S(2)}) %collective-permute-start.22) | collective-permute-done | bytes 1048608 | tf_op jit(solution)/shard_map/ppermute | solution.py:117
  67.3 15.9 %collective-permute-done.7.refs_10_ = bf16[8,8,128,128]{3,2,1,0:T(8,128)(2,1)} collective-permute-done((bf16[8,8,128,128]{3,2,1,0:T(8,128)(2,1)}, bf16[8,8,128,128]{3,2,1,0:T(8,128)(2,1)}, u32[]{:S(2)}, u32[]{:S(2)}) %collective-permute-start.7) | collective-permute-done | bytes 2097184 | tf_op jit(solution)/shard_map/ppermute | solution.py:168
  83.2 1.5 collective-permute-start.19
  84.7 2.3 %pad_maximum_fusion.3.refs_1_ = bf16[2,16,16384]{2,1,0:T(8,128)(2,1)} fusion(bf16[1,16,16384]{2,1,0:T(8,128)(2,1)} %bitcast.10, bf16[1,16,16384]{2,1,0:T(8,128)(2,1)} %bitcast.9), kind=kLoop, calls=%fused_computation.5 | loop fusion | flops 524288 | bytes 2097152 | tf_op jit(solution)/shard_map/stack | solution.py:116
  87.0 4.3 %collective-permute-start.21 = (bf16[8,8,128,128]{3,2,1,0:T(8,128)(2,1)}, bf16[8,8,128,128]{3,2,1,0:T(8,128)(2,1)}, u32[]{:S(2)}, u32[]{:S(2)}) collective-permute-start(bf16[8,8,128,128]{3,2,1,0:T(8,128)(2,1)} %collective-permute-done.6.refs_11_), channel_id=1, source_target_pairs={{0,32},{1,225},{2,34},{3,227},{4,36},{5,229},{6,38},{7,231},{8,40}... | collective-permute-start | bytes 6291464 | tf_op jit(solution)/shard_map/ppermute | solution.py:169
  91.3 0.1 pad_maximum_fusion.2.refs_0_
  91.4 1.6 collective-permute-start.14
  93.0 1.2 collective-permute-start.16
  94.2 0.3 collective-permute-start.13
  94.5 2.4 %collective-permute-start.15 = (bf16[2,16,16384]{2,1,0:T(8,128)(2,1)S(1)}, bf16[2,16,16384]{2,1,0:T(8,128)(2,1)}, u32[]{:S(2)}, u32[]{:S(2)}) collective-permute-start(bf16[2,16,16384]{2,1,0:T(8,128)(2,1)S(1)} %pad_maximum_fusion.2.refs_0_), channel_id=1, source_target_pairs={{0,24},{1,7},{2,26},{3,1},{4,28},{5,3},{6,30},{7,5},{8,0},{9,15},{... | collective-permute-start | bytes 3145736 | tf_op jit(solution)/shard_map/ppermute | solution.py:120
  96.9 0.1 broadcast_add_fusion
  97.0 0.1 add.75.place
  97.1 0.1 fusion.10
  97.2 0.1 slice_select_fusion
  97.3 0.1 concatenate.23
  97.4 0.1 copy.14
  97.6 0.2 convert_element_type.28.live
  97.7 0.1 reshape_squeeze.3.blocks_in
  97.8 14.9 %shard_map.64.refs_10_ = f32[2,256,512]{2,1,0:T(8,128)S(1)} custom-call(s32[16]{0:T(128)S(1)} %add.75.place, s32[512]{0:T(512)S(1)} %reshape_squeeze.3.blocks_in, f32[1024]{0:T(1024)S(1)} %convert_element_type.28.live, bf16[2,16,16384]{2,1,0:T(8,128)(2,1)} %pad_maximum_fusion.refs_0_, bf16[2,16,16384]{2,1,0:T(8,128)(2,1)} %copy-done.2, ...), custom_call_target="tpu_custom_call" | custom-call | flops 3221225472 | bytes 20971520 | tf_op jit(solution)/shard_map/pallas_call | solution.py:89
  112.8 5.1 %collective-permute-done.13.refs_2_ = bf16[2,16,16384]{2,1,0:T(8,128)(2,1)} collective-permute-done((bf16[2,16,16384]{2,1,0:T(8,128)(2,1)S(1)}, bf16[2,16,16384]{2,1,0:T(8,128)(2,1)}, u32[]{:S(2)}, u32[]{:S(2)}) %collective-permute-start.13) | collective-permute-done | bytes 1048608 | tf_op jit(solution)/shard_map/ppermute | solution.py:117
  117.9 0.3 collective-permute-done.15.refs_4_
  118.2 2.4 %collective-permute-start.18 = (bf16[2,16,16384]{2,1,0:T(8,128)(2,1)}, bf16[2,16,16384]{2,1,0:T(8,128)(2,1)S(1)}, u32[]{:S(2)}, u32[]{:S(2)}) collective-permute-start(bf16[2,16,16384]{2,1,0:T(8,128)(2,1)} %collective-permute-done.16.refs_5_), channel_id=1, source_target_pairs={{0,24},{1,7},{2,26},{3,1},{4,28},{5,3},{6,30},{7,5},{8,0},{9,15},{... | collective-permute-start | bytes 3145736 | tf_op jit(solution)/shard_map/ppermute | solution.py:122
  120.6 2.0 %collective-permute-done.26.refs_15_.refs_9_ = bf16[8,8,128,128]{3,2,1,0:T(8,128)(2,1)S(1)} collective-permute-done((bf16[8,8,128,128]{3,2,1,0:T(8,128)(2,1)}, bf16[8,8,128,128]{3,2,1,0:T(8,128)(2,1)S(1)}, u32[]{:S(2)}, u32[]{:S(2)}) %collective-permute-start.26) | collective-permute-done | bytes 2097184 | tf_op jit(solution)/shard_map/ppermute | solution.py:179
  122.6 8.4 %shard_map.66 = f32[2,256,512]{2,1,0:T(8,128)S(1)} custom-call(s32[16]{0:T(128)S(1)} %add.75.place, s32[512]{0:T(512)S(1)} %reshape_squeeze.3.blocks_in, f32[1024]{0:T(1024)S(1)} %convert_element_type.28.live, bf16[2,16,16384]{2,1,0:T(8,128)(2,1)} %pad_maximum_fusion.refs_0_, bf16[2,16,16384]{2,1,0:T(8,128)(2,1)S(1)} %copy-done.3, ...), custom_call_target="tpu_custom_call" | custom-call | flops 1073741824 | bytes 12582912 | tf_op jit(solution)/shard_map/pallas_call | solution.py:89
  131.1 0.1 convert_element_type.29
  131.2 0.1 slice_bitcast_fusion.3
  131.3 9.7 %collective-permute-start.28 = (f16[256,512]{1,0:T(8,128)(2,1)S(1)}, f16[256,512]{1,0:T(8,128)(2,1)S(1)}, u32[]{:S(2)}, u32[]{:S(2)}) collective-permute-start(f16[256,512]{1,0:T(8,128)(2,1)S(1)} %get-tuple-element.38), channel_id=1, source_target_pairs={{0,128},{1,129},{2,130},{3,131},{4,132},{5,133},{6,134},{7,135},{8... | collective-permute-start | bytes 786440 | tf_op jit(solution)/shard_map/ppermute | solution.py:182
  140.9 0.3 collective-permute-start.27
  141.3 15.7 %shard_map.65 = f32[2,256,512]{2,1,0:T(8,128)S(1)} custom-call(s32[16]{0:T(128)S(1)} %add.75.place, s32[512]{0:T(512)S(1)} %reshape_squeeze.3.blocks_in, f32[1024]{0:T(1024)S(1)} %convert_element_type.28.live, bf16[2,16,16384]{2,1,0:T(8,128)(2,1)S(1)} %pad_maximum_fusion.2.refs_0_, bf16[2,16,16384]{2,1,0:T(8,128)(2,1)} %pad_maximum_fusion.3.refs_1_, ...), custom_call_target="tpu_custom_call" | custom-call | flops 4294967296 | bytes 25165824 | tf_op jit(solution)/shard_map/pallas_call | solution.py:89
  157.0 2.1 %collective-permute-done.28 = f16[256,512]{1,0:T(8,128)(2,1)S(1)} collective-permute-done((f16[256,512]{1,0:T(8,128)(2,1)S(1)}, f16[256,512]{1,0:T(8,128)(2,1)S(1)}, u32[]{:S(2)}, u32[]{:S(2)}) %collective-permute-start.28) | collective-permute-done | bytes 262176 | tf_op jit(solution)/shard_map/ppermute | solution.py:182
  159.0 0.1 fusion.2
  159.1 0.1 collective-permute-start.29
  159.2 3.5 %collective-permute-done.27 = f16[256,512]{1,0:T(8,128)(2,1)S(1)} collective-permute-done((f16[256,512]{1,0:T(8,128)(2,1)S(1)}, f16[256,512]{1,0:T(8,128)(2,1)S(1)}, u32[]{:S(2)}, u32[]{:S(2)}) %collective-permute-start.27) | collective-permute-done | bytes 262176 | tf_op jit(solution)/shard_map/ppermute | solution.py:183
  162.7 0.1 broadcast_select_fusion.3
  162.9 0.1 maximum_bitcast_fusion
  162.9 0.9 copy.15
  (61 shorter events, 0.2 us)
Async XLA Ops:
  0.0 17.1 %collective-permute-start = (bf16[4,16,128,128]{3,2,1,0:T(8,128)(2,1)}, bf16[4,16,128,128]{3,2,1,0:T(8,128)(2,1)S(1)}, u32[]{:S(2)}, u32[]{:S(2)}) collective-permute-start(bf16[4,16,128,128]{3,2,1,0:T(8,128)(2,1)} %param.7), channel_id=1, source_target_pairs={{0,1},{1,0},{2,3},{3,2},{4,5},{5,4},{6,7},{7,6},{8,9},{9,8},{10,11... | collective-permute-start | bytes 6291464 | tf_op jit(solution)/shard_map/ppermute | solution.py:154
  3.2 20.0 %collective-permute-start.1 = (bf16[16,16384]{1,0:T(8,128)(2,1)}, bf16[16,16384]{1,0:T(8,128)(2,1)}, u32[]{:S(2)}, u32[]{:S(2)}) collective-permute-start(bf16[16,16384]{1,0:T(8,128)(2,1)} %bitcast.43), channel_id=1, source_target_pairs={{0,128},{1,129},{2,130},{3,131},{4,132},{5,133},{6,134},{7,135},{8... | collective-permute-start | bytes 1572872 | tf_op jit(solution)/shard_map/ppermute | solution.py:147
  8.4 14.8 %collective-permute-start.3 = (bf16[16,16384]{1,0:T(8,128)(2,1)}, bf16[16,16384]{1,0:T(8,128)(2,1)S(1)}, u32[]{:S(2)}, u32[]{:S(2)}) collective-permute-start(bf16[16,16384]{1,0:T(8,128)(2,1)} %bitcast.44), channel_id=1, source_target_pairs={{0,2},{1,9},{2,4},{3,11},{4,6},{5,13},{6,0},{7,15},{8,10},{9,17},{... | collective-permute-start | bytes 1572872 | tf_op jit(solution)/shard_map/ppermute | solution.py:112
  9.7 13.5 %collective-permute-start.4 = (bf16[16,16384]{1,0:T(8,128)(2,1)}, bf16[16,16384]{1,0:T(8,128)(2,1)}, u32[]{:S(2)}, u32[]{:S(2)}) collective-permute-start(bf16[16,16384]{1,0:T(8,128)(2,1)} %bitcast.45), channel_id=1, source_target_pairs={{0,6},{1,25},{2,0},{3,27},{4,2},{5,29},{6,4},{7,31},{8,14},{9,1},{... | collective-permute-start | bytes 1572872 | tf_op jit(solution)/shard_map/ppermute | solution.py:112
  11.2 14.0 %collective-permute-start.5 = (bf16[16,16384]{1,0:T(8,128)(2,1)}, bf16[16,16384]{1,0:T(8,128)(2,1)}, u32[]{:S(2)}, u32[]{:S(2)}) collective-permute-start(bf16[16,16384]{1,0:T(8,128)(2,1)} %bitcast.46), channel_id=1, source_target_pairs={{0,4},{1,17},{2,6},{3,19},{4,0},{5,21},{6,2},{7,23},{8,12},{9,25},... | collective-permute-start | bytes 1572872 | tf_op jit(solution)/shard_map/ppermute | solution.py:112
  17.1 2.9 %collective-permute-start.2 = (s32[3,4,128]{2,1,0:T(4,128)S(1)}, s32[3,4,128]{2,1,0:T(4,128)S(1)}, u32[]{:S(2)}, u32[]{:S(2)}) collective-permute-start(s32[3,4,128]{2,1,0:T(4,128)S(1)} %pad_add_fusion), channel_id=1, source_target_pairs={{0,1},{1,0},{2,3},{3,2},{4,5},{5,4},{6,7},{7,6},{8,9},{9,8},{10,11... | collective-permute-start | bytes 18440 | tf_op jit(solution)/shard_map/ppermute | solution.py:139
  20.1 25.5 %copy-start = (bf16[8,8,128,128]{3,2,1,0:T(8,128)(2,1)}, bf16[8,8,128,128]{3,2,1,0:T(8,128)(2,1)S(1)}, u32[]{:S(2)}) copy-start(bf16[8,8,128,128]{3,2,1,0:T(8,128)(2,1)S(1)} %get-tuple-element.20.refs_9_) | copy-start | bytes 6291460
  23.2 17.3 %copy-start.13 = (bf16[16,16384]{1,0:T(8,128)(2,1)}, bf16[16,16384]{1,0:T(8,128)(2,1)S(1)}, u32[]{:S(2)}) copy-start(bf16[16,16384]{1,0:T(8,128)(2,1)S(1)} %collective-permute-done.3) | copy-start | bytes 1572868
  25.1 15.4 %collective-permute-start.9 = (bf16[16,16384]{1,0:T(8,128)(2,1)}, bf16[16,16384]{1,0:T(8,128)(2,1)S(1)}, u32[]{:S(2)}, u32[]{:S(2)}) collective-permute-start(bf16[16,16384]{1,0:T(8,128)(2,1)} %collective-permute-done.1), channel_id=1, source_target_pairs={{0,6},{1,25},{2,0},{3,27},{4,2},{5,29},{6,4},{7,31},{8,14},{9,1},{... | collective-permute-start | bytes 1572872 | tf_op jit(solution)/shard_map/ppermute | solution.py:112
  26.6 13.9 %collective-permute-start.10 = (bf16[16,16384]{1,0:T(8,128)(2,1)}, bf16[16,16384]{1,0:T(8,128)(2,1)S(1)}, u32[]{:S(2)}, u32[]{:S(2)}) collective-permute-start(bf16[16,16384]{1,0:T(8,128)(2,1)} %collective-permute-done.1), channel_id=1, source_target_pairs={{0,4},{1,17},{2,6},{3,19},{4,0},{5,21},{6,2},{7,23},{8,12},{9,25},... | collective-permute-start | bytes 1572872 | tf_op jit(solution)/shard_map/ppermute | solution.py:112
  27.8 15.7 %collective-permute-start.8 = (bf16[16,16384]{1,0:T(8,128)(2,1)}, bf16[16,16384]{1,0:T(8,128)(2,1)S(1)}, u32[]{:S(2)}, u32[]{:S(2)}) collective-permute-start(bf16[16,16384]{1,0:T(8,128)(2,1)} %collective-permute-done.1), channel_id=1, source_target_pairs={{0,2},{1,9},{2,4},{3,11},{4,6},{5,13},{6,0},{7,15},{8,10},{9,17},{... | collective-permute-start | bytes 1572872 | tf_op jit(solution)/shard_map/ppermute | solution.py:112
  27.8 39.5 %collective-permute-start.6 = (bf16[8,8,128,128]{3,2,1,0:T(8,128)(2,1)S(1)}, bf16[8,8,128,128]{3,2,1,0:T(8,128)(2,1)}, u32[]{:S(2)}, u32[]{:S(2)}) collective-permute-start(bf16[8,8,128,128]{3,2,1,0:T(8,128)(2,1)S(1)} %get-tuple-element.20.refs_9_), channel_id=1, source_target_pairs={{0,32},{1,225},{2,34},{3,227},{4,36},{5,229},{6,38},{7,231},{8,40}... | collective-permute-start | bytes 6291464 | tf_op jit(solution)/shard_map/ppermute | solution.py:167
  36.2 47.0 %collective-permute-start.7 = (bf16[8,8,128,128]{3,2,1,0:T(8,128)(2,1)}, bf16[8,8,128,128]{3,2,1,0:T(8,128)(2,1)}, u32[]{:S(2)}, u32[]{:S(2)}) collective-permute-start(bf16[8,8,128,128]{3,2,1,0:T(8,128)(2,1)} %get-tuple-element.21.refs_8_), channel_id=1, source_target_pairs={{0,32},{1,225},{2,34},{3,227},{4,36},{5,229},{6,38},{7,231},{8,40}... | collective-permute-start | bytes 6291464 | tf_op jit(solution)/shard_map/ppermute | solution.py:168
  40.6 5.0 %copy-start.16 = (s32[4]{0:T(128)S(1)}, s32[4]{0:T(128)}, u32[]{:S(2)}) copy-start(s32[4]{0:T(128)} %constant.97.clone) | copy-start | bytes 52
  40.7 46.3 %copy-start.2 = (bf16[2,16,16384]{2,1,0:T(8,128)(2,1)}, bf16[2,16,16384]{2,1,0:T(8,128)(2,1)S(1)}, u32[]{:S(2)}) copy-start(bf16[2,16,16384]{2,1,0:T(8,128)(2,1)S(1)} %pad_maximum_fusion.1.refs_1_) | copy-start | bytes 3145732
  40.7 15.3 %collective-permute-start.11 = (bf16[2,16,16384]{2,1,0:T(8,128)(2,1)S(1)}, bf16[2,16,16384]{2,1,0:T(8,128)(2,1)}, u32[]{:S(2)}, u32[]{:S(2)}) collective-permute-start(bf16[2,16,16384]{2,1,0:T(8,128)(2,1)S(1)} %pad_maximum_fusion.1.refs_1_), channel_id=1, source_target_pairs={{0,8},{1,3},{2,10},{3,5},{4,12},{5,7},{6,14},{7,1},{8,16},{9,11},{... | collective-permute-start | bytes 3145736 | tf_op jit(solution)/shard_map/ppermute | solution.py:119
  42.0 15.3 %collective-permute-start.12 = (bf16[2,16,16384]{2,1,0:T(8,128)(2,1)S(1)}, bf16[2,16,16384]{2,1,0:T(8,128)(2,1)}, u32[]{:S(2)}, u32[]{:S(2)}) collective-permute-start(bf16[2,16,16384]{2,1,0:T(8,128)(2,1)S(1)} %pad_maximum_fusion.1.refs_1_), channel_id=1, source_target_pairs={{0,24},{1,7},{2,26},{3,1},{4,28},{5,3},{6,30},{7,5},{8,0},{9,15},{... | collective-permute-start | bytes 3145736 | tf_op jit(solution)/shard_map/ppermute | solution.py:118
  45.6 21.7 %collective-permute-start.22 = (bf16[2,16,16384]{2,1,0:T(8,128)(2,1)}, bf16[2,16,16384]{2,1,0:T(8,128)(2,1)}, u32[]{:S(2)}, u32[]{:S(2)}) collective-permute-start(bf16[2,16,16384]{2,1,0:T(8,128)(2,1)} %pad_maximum_fusion.refs_0_), channel_id=1, source_target_pairs={{0,8},{1,3},{2,10},{3,5},{4,12},{5,7},{6,14},{7,1},{8,16},{9,11},{... | collective-permute-start | bytes 3145736 | tf_op jit(solution)/shard_map/ppermute | solution.py:117
  45.6 45.7 %copy-start.12 = (bf16[2,8,16384]{2,1,0:T(8,128)(2,1)S(1)}, bf16[2,8,16384]{2,1,0:T(8,128)(2,1)}, u32[]{:S(2)}) copy-start(bf16[2,8,16384]{2,1,0:T(8,128)(2,1)} %param.6) | copy-start | bytes 1572868
  45.6 45.7 %copy-start.14 = (bf16[16,16384]{1,0:T(8,128)(2,1)S(1)}, bf16[16,16384]{1,0:T(8,128)(2,1)}, u32[]{:S(2)}) copy-start(bf16[16,16384]{1,0:T(8,128)(2,1)} %copy-done.13) | copy-start | bytes 1572868
  56.0 31.0 %collective-permute-start.23 = (bf16[2,16,16384]{2,1,0:T(8,128)(2,1)}, bf16[2,16,16384]{2,1,0:T(8,128)(2,1)S(1)}, u32[]{:S(2)}, u32[]{:S(2)}) collective-permute-start(bf16[2,16,16384]{2,1,0:T(8,128)(2,1)} %pad_maximum_fusion.refs_0_), channel_id=1, source_target_pairs={{0,24},{1,7},{2,26},{3,1},{4,28},{5,3},{6,30},{7,5},{8,0},{9,15},{... | collective-permute-start | bytes 3145736 | tf_op jit(solution)/shard_map/ppermute | solution.py:120
  57.3 34.1 %collective-permute-start.25 = (bf16[2,16,16384]{2,1,0:T(8,128)(2,1)}, bf16[2,16,16384]{2,1,0:T(8,128)(2,1)S(1)}, u32[]{:S(2)}, u32[]{:S(2)}) collective-permute-start(bf16[2,16,16384]{2,1,0:T(8,128)(2,1)} %collective-permute-done.12.refs_5_), channel_id=1, source_target_pairs={{0,24},{1,7},{2,26},{3,1},{4,28},{5,3},{6,30},{7,5},{8,0},{9,15},{... | collective-permute-start | bytes 3145736 | tf_op jit(solution)/shard_map/ppermute | solution.py:122
  67.3 25.8 %collective-permute-start.24 = (bf16[2,16,16384]{2,1,0:T(8,128)(2,1)}, bf16[2,16,16384]{2,1,0:T(8,128)(2,1)S(1)}, u32[]{:S(2)}, u32[]{:S(2)}) collective-permute-start(bf16[2,16,16384]{2,1,0:T(8,128)(2,1)} %collective-permute-done.22.refs_2_), channel_id=1, source_target_pairs={{0,8},{1,3},{2,10},{3,5},{4,12},{5,7},{6,14},{7,1},{8,16},{9,11},{... | collective-permute-start | bytes 3145736 | tf_op jit(solution)/shard_map/ppermute | solution.py:121
  83.2 11.0 %collective-permute-start.19 = (bf16[8,8,128,128]{3,2,1,0:T(8,128)(2,1)}, bf16[8,8,128,128]{3,2,1,0:T(8,128)(2,1)S(1)}, u32[]{:S(2)}, u32[]{:S(2)}) collective-permute-start(bf16[8,8,128,128]{3,2,1,0:T(8,128)(2,1)} %collective-permute-done.7.refs_10_), channel_id=1, source_target_pairs={{0,1},{1,0},{2,3},{3,2},{4,5},{5,4},{6,7},{7,6},{8,9},{9,8},{10,11... | collective-permute-start | bytes 6291464 | tf_op jit(solution)/shard_map/ppermute | solution.py:175
  84.7 9.8 %collective-permute-start.20 = (bf16[8,8,128,128]{3,2,1,0:T(8,128)(2,1)}, bf16[8,8,128,128]{3,2,1,0:T(8,128)(2,1)}, u32[]{:S(2)}, u32[]{:S(2)}) collective-permute-start(bf16[8,8,128,128]{3,2,1,0:T(8,128)(2,1)} %collective-permute-done.6.refs_11_), channel_id=1, source_target_pairs={{0,1},{1,0},{2,3},{3,2},{4,5},{5,4},{6,7},{7,6},{8,9},{9,8},{10,11... | collective-permute-start | bytes 6291464 | tf_op jit(solution)/shard_map/ppermute | solution.py:175
  84.7 12.4 %copy-start.15 = (s32[4,128]{1,0:T(4,128)S(1)}, s32[4,128]{1,0:T(4,128)}, u32[]{:S(2)}) copy-start(s32[4,128]{1,0:T(4,128)} %param.8) | copy-start | bytes 6148
  87.0 7.5 %copy-start.6 = (bf16[2,16,16384]{2,1,0:T(8,128)(2,1)}, bf16[2,16,16384]{2,1,0:T(8,128)(2,1)S(1)}, u32[]{:S(2)}) copy-start(bf16[2,16,16384]{2,1,0:T(8,128)(2,1)S(1)} %collective-permute-done.23.refs_4_) | copy-start | bytes 3145732
  87.0 31.2 %collective-permute-start.21 = (bf16[8,8,128,128]{3,2,1,0:T(8,128)(2,1)}, bf16[8,8,128,128]{3,2,1,0:T(8,128)(2,1)}, u32[]{:S(2)}, u32[]{:S(2)}) collective-permute-start(bf16[8,8,128,128]{3,2,1,0:T(8,128)(2,1)} %collective-permute-done.6.refs_11_), channel_id=1, source_target_pairs={{0,32},{1,225},{2,34},{3,227},{4,36},{5,229},{6,38},{7,231},{8,40}... | collective-permute-start | bytes 6291464 | tf_op jit(solution)/shard_map/ppermute | solution.py:169
  91.4 3.1 %copy-start.8 = (bf16[2,16,16384]{2,1,0:T(8,128)(2,1)}, bf16[2,16,16384]{2,1,0:T(8,128)(2,1)S(1)}, u32[]{:S(2)}) copy-start(bf16[2,16,16384]{2,1,0:T(8,128)(2,1)S(1)} %collective-permute-done.25.refs_7_) | copy-start | bytes 3145732
  91.4 21.4 %collective-permute-start.14 = (bf16[2,16,16384]{2,1,0:T(8,128)(2,1)}, bf16[2,16,16384]{2,1,0:T(8,128)(2,1)}, u32[]{:S(2)}, u32[]{:S(2)}) collective-permute-start(bf16[2,16,16384]{2,1,0:T(8,128)(2,1)} %pad_maximum_fusion.3.refs_1_), channel_id=1, source_target_pairs={{0,8},{1,3},{2,10},{3,5},{4,12},{5,7},{6,14},{7,1},{8,16},{9,11},{... | collective-permute-start | bytes 3145736 | tf_op jit(solution)/shard_map/ppermute | solution.py:119
  93.0 3.9 %copy-start.10 = (bf16[2,16,16384]{2,1,0:T(8,128)(2,1)}, bf16[2,16,16384]{2,1,0:T(8,128)(2,1)S(1)}, u32[]{:S(2)}) copy-start(bf16[2,16,16384]{2,1,0:T(8,128)(2,1)S(1)} %collective-permute-done.24.refs_6_) | copy-start | bytes 3145732
  93.0 19.8 %collective-permute-start.16 = (bf16[2,16,16384]{2,1,0:T(8,128)(2,1)}, bf16[2,16,16384]{2,1,0:T(8,128)(2,1)}, u32[]{:S(2)}, u32[]{:S(2)}) collective-permute-start(bf16[2,16,16384]{2,1,0:T(8,128)(2,1)} %pad_maximum_fusion.3.refs_1_), channel_id=1, source_target_pairs={{0,24},{1,7},{2,26},{3,1},{4,28},{5,3},{6,30},{7,5},{8,0},{9,15},{... | collective-permute-start | bytes 3145736 | tf_op jit(solution)/shard_map/ppermute | solution.py:118
  94.2 3.6 %copy-start.4 = (bf16[8,8,128,128]{3,2,1,0:T(8,128)(2,1)}, bf16[8,8,128,128]{3,2,1,0:T(8,128)(2,1)S(1)}, u32[]{:S(2)}) copy-start(bf16[8,8,128,128]{3,2,1,0:T(8,128)(2,1)S(1)} %collective-permute-done.19.refs_12_) | copy-start | bytes 6291460
  94.2 23.7 %collective-permute-start.13 = (bf16[2,16,16384]{2,1,0:T(8,128)(2,1)S(1)}, bf16[2,16,16384]{2,1,0:T(8,128)(2,1)}, u32[]{:S(2)}, u32[]{:S(2)}) collective-permute-start(bf16[2,16,16384]{2,1,0:T(8,128)(2,1)S(1)} %pad_maximum_fusion.2.refs_0_), channel_id=1, source_target_pairs={{0,8},{1,3},{2,10},{3,5},{4,12},{5,7},{6,14},{7,1},{8,16},{9,11},{... | collective-permute-start | bytes 3145736 | tf_op jit(solution)/shard_map/ppermute | solution.py:117
  94.5 23.7 %collective-permute-start.15 = (bf16[2,16,16384]{2,1,0:T(8,128)(2,1)S(1)}, bf16[2,16,16384]{2,1,0:T(8,128)(2,1)}, u32[]{:S(2)}, u32[]{:S(2)}) collective-permute-start(bf16[2,16,16384]{2,1,0:T(8,128)(2,1)S(1)} %pad_maximum_fusion.2.refs_0_), channel_id=1, source_target_pairs={{0,24},{1,7},{2,26},{3,1},{4,28},{5,3},{6,30},{7,5},{8,0},{9,15},{... | collective-permute-start | bytes 3145736 | tf_op jit(solution)/shard_map/ppermute | solution.py:120
  97.8 24.8 %copy-start.3 = (bf16[2,16,16384]{2,1,0:T(8,128)(2,1)S(1)}, bf16[2,16,16384]{2,1,0:T(8,128)(2,1)}, u32[]{:S(2)}) copy-start(bf16[2,16,16384]{2,1,0:T(8,128)(2,1)} %copy-done.2) | copy-start | bytes 3145732
  97.8 24.8 %copy-start.7 = (bf16[2,16,16384]{2,1,0:T(8,128)(2,1)S(1)}, bf16[2,16,16384]{2,1,0:T(8,128)(2,1)}, u32[]{:S(2)}) copy-start(bf16[2,16,16384]{2,1,0:T(8,128)(2,1)} %copy-done.6) | copy-start | bytes 3145732
  97.8 24.8 %copy-start.9 = (bf16[2,16,16384]{2,1,0:T(8,128)(2,1)S(1)}, bf16[2,16,16384]{2,1,0:T(8,128)(2,1)}, u32[]{:S(2)}) copy-start(bf16[2,16,16384]{2,1,0:T(8,128)(2,1)} %copy-done.8) | copy-start | bytes 3145732
  97.8 24.8 %copy-start.11 = (bf16[2,16,16384]{2,1,0:T(8,128)(2,1)S(1)}, bf16[2,16,16384]{2,1,0:T(8,128)(2,1)}, u32[]{:S(2)}) copy-start(bf16[2,16,16384]{2,1,0:T(8,128)(2,1)} %copy-done.10) | copy-start | bytes 3145732
  118.2 4.4 %collective-permute-start.26 = (bf16[8,8,128,128]{3,2,1,0:T(8,128)(2,1)}, bf16[8,8,128,128]{3,2,1,0:T(8,128)(2,1)S(1)}, u32[]{:S(2)}, u32[]{:S(2)}) collective-permute-start(bf16[8,8,128,128]{3,2,1,0:T(8,128)(2,1)} %collective-permute-done.21.refs_14_.refs_8_), channel_id=1, source_target_pairs={{0,1},{1,0},{2,3},{3,2},{4,5},{5,4},{6,7},{7,6},{8,9},{9,8},{10,11... | collective-permute-start | bytes 6291464 | tf_op jit(solution)/shard_map/ppermute | solution.py:179
  118.2 23.0 %collective-permute-start.18 = (bf16[2,16,16384]{2,1,0:T(8,128)(2,1)}, bf16[2,16,16384]{2,1,0:T(8,128)(2,1)S(1)}, u32[]{:S(2)}, u32[]{:S(2)}) collective-permute-start(bf16[2,16,16384]{2,1,0:T(8,128)(2,1)} %collective-permute-done.16.refs_5_), channel_id=1, source_target_pairs={{0,24},{1,7},{2,26},{3,1},{4,28},{5,3},{6,30},{7,5},{8,0},{9,15},{... | collective-permute-start | bytes 3145736 | tf_op jit(solution)/shard_map/ppermute | solution.py:122
  120.6 20.7 %collective-permute-start.17 = (bf16[2,16,16384]{2,1,0:T(8,128)(2,1)}, bf16[2,16,16384]{2,1,0:T(8,128)(2,1)S(1)}, u32[]{:S(2)}, u32[]{:S(2)}) collective-permute-start(bf16[2,16,16384]{2,1,0:T(8,128)(2,1)} %collective-permute-done.13.refs_2_), channel_id=1, source_target_pairs={{0,8},{1,3},{2,10},{3,5},{4,12},{5,7},{6,14},{7,1},{8,16},{9,11},{... | collective-permute-start | bytes 3145736 | tf_op jit(solution)/shard_map/ppermute | solution.py:121
  122.6 18.7 %copy-start.5 = (bf16[8,8,128,128]{3,2,1,0:T(8,128)(2,1)S(1)}, bf16[8,8,128,128]{3,2,1,0:T(8,128)(2,1)}, u32[]{:S(2)}) copy-start(bf16[8,8,128,128]{3,2,1,0:T(8,128)(2,1)} %copy-done.4) | copy-start | bytes 6291460
  131.0 10.2 %copy-start.1 = (bf16[8,8,128,128]{3,2,1,0:T(8,128)(2,1)S(1)}, bf16[8,8,128,128]{3,2,1,0:T(8,128)(2,1)}, u32[]{:S(2)}) copy-start(bf16[8,8,128,128]{3,2,1,0:T(8,128)(2,1)} %copy-done) | copy-start | bytes 6291460
  131.3 27.8 %collective-permute-start.28 = (f16[256,512]{1,0:T(8,128)(2,1)S(1)}, f16[256,512]{1,0:T(8,128)(2,1)S(1)}, u32[]{:S(2)}, u32[]{:S(2)}) collective-permute-start(f16[256,512]{1,0:T(8,128)(2,1)S(1)} %get-tuple-element.38), channel_id=1, source_target_pairs={{0,128},{1,129},{2,130},{3,131},{4,132},{5,133},{6,134},{7,135},{8... | collective-permute-start | bytes 786440 | tf_op jit(solution)/shard_map/ppermute | solution.py:182
  140.9 21.8 %collective-permute-start.27 = (f16[256,512]{1,0:T(8,128)(2,1)S(1)}, f16[256,512]{1,0:T(8,128)(2,1)S(1)}, u32[]{:S(2)}, u32[]{:S(2)}) collective-permute-start(f16[256,512]{1,0:T(8,128)(2,1)S(1)} %get-tuple-element.37), channel_id=1, source_target_pairs={{0,128},{1,129},{2,130},{3,131},{4,132},{5,133},{6,134},{7,135},{8... | collective-permute-start | bytes 786440 | tf_op jit(solution)/shard_map/ppermute | solution.py:183
  159.1 3.6 %collective-permute-start.29 = (bf16[256,512]{1,0:T(8,128)(2,1)S(1)}, bf16[256,512]{1,0:T(8,128)(2,1)S(1)}, u32[]{:S(2)}, u32[]{:S(2)}) collective-permute-start(bf16[256,512]{1,0:T(8,128)(2,1)S(1)} %fusion.2), channel_id=1, source_target_pairs={{0,1},{1,0},{2,3},{3,2},{4,5},{5,4},{6,7},{7,6},{8,9},{9,8},{10,11... | collective-permute-start | bytes 786440 | tf_op jit(solution)/shard_map/ppermute | solution.py:187
